TPU v7x, 256 devices: a whole 4x4x8 slice. The times are simulated.
256 devices in a mesh: seq: 256 (over y, z, x, core).
Axes of the slice: x: 4, y: 4, z: 8, core: 2. Of those that a mesh axis runs over, the one named last changes fastest.
Arguments:
- queries: bfloat16 [65536, 768], P('seq'), may hold values from -4 to 4
- key_states: bfloat16 [65536, 768], P('seq'), may hold values from -4 to 4
- value_states: bfloat16 [65536, 768], P('seq'), may hold values from -6 to 6
- cotangent: bfloat16 [65536, 768], P('seq'), may hold values from -6 to 6
- offsets: int32 [3, 16], replicated, may hold values from 0 to 255, as said below
Outputs:
- attended: bfloat16 [65536, 768], P('seq')
- grad_query: bfloat16 [65536, 768], P('seq')
- grad_keys: bfloat16 [65536, 768], P('seq')
- grad_values: bfloat16 [65536, 768], P('seq')
Inputs may be any that keep to these rules, and one draw needn't show every extreme that they name: Row b of offsets (b = 0, 1, 2) holds values below the dilation of branch b + 2 (8, 64, 256); every row holds a zero and its dilation minus one.
All inputs are finite; a program needn't handle non-finite values.
Results may differ from a plain program's by a relative error of at most 0.0033.
The roundings to bfloat16 on the way count: a program that leaves them out, or rounds other values in their place, can miss the bound.
Values may be sent and summed in bfloat16 or wider, within the bound.
No kernel may reach another device: no remote copies, remote signals or barrier semaphores. Data moves between devices by JAX's collectives and lax.ppermute only.
A program may use at most 128 MiB of HBM per device.

v0:
```python
import jax
import jax.numpy as jnp
from jax import lax
from jax.sharding import PartitionSpec as P

DILATION_TWO = 8
DILATION_THREE = 64
DILATION_FOUR = 256


def swapped(block, axis, stride):
    count = lax.axis_size(axis)
    route = []
    for low in range(count):
        high = low | 1 << stride
        if high != low and high < count:
            route += [(low, high), (high, low)]
    return lax.ppermute(block, axis, route)


def pick_rows(tensor, offset_row, dilation):
    if dilation == 1:
        return tensor
    selected = tensor.shape[0] // dilation
    shaped = tensor.reshape(selected, dilation, tensor.shape[1], tensor.shape[2])
    chosen = jnp.arange(dilation, dtype=jnp.int32)[:, None] == offset_row[None, :]
    return jnp.sum(jnp.where(chosen[None, :, :, None], shaped, jnp.zeros((), tensor.dtype)), axis=1)


def place_rows(tensor, offset_row, dilation):
    if dilation == 1:
        return tensor
    chosen = jnp.arange(dilation, dtype=jnp.int32)[:, None] == offset_row[None, :]
    spread = jnp.where(chosen[None, :, :, None], tensor[:, None], jnp.zeros((), tensor.dtype))
    return spread.reshape(tensor.shape[0] * dilation, tensor.shape[1], tensor.shape[2])


def to_pairs(tensor):
    dims_in = tensor.shape
    return jnp.swapaxes(tensor.reshape((dims_in[0], dims_in[1] // 2, 2) + dims_in[2:]), 0, 1)


def from_pairs(tensor):
    dims_in = tensor.shape
    return jnp.swapaxes(tensor, 0, 1).reshape((dims_in[1], dims_in[0] * 2) + dims_in[3:])


def forward_block(query_rows, key_rows, value_rows):
    factor = query_rows.shape[-1] ** (-0.5)
    scores = (
        jnp.einsum("qhc,khc->hqk", query_rows, key_rows, preferred_element_type=jnp.float32)
        * factor
    )
    weights = jnp.exp(scores)
    sums_row = jnp.sum(weights, axis=-1)
    rounded = (weights / sums_row[:, :, None]).astype(jnp.bfloat16)
    output = jnp.einsum("hqk,khc->qhc", rounded, value_rows, preferred_element_type=jnp.float32)
    return (output, sums_row.T)


def backward_block(query_rows, key_rows, value_rows, grad_rows, totals, row_dots):
    factor = query_rows.shape[-1] ** (-0.5)
    scores = (
        jnp.einsum("qhc,khc->hqk", query_rows, key_rows, preferred_element_type=jnp.float32)
        * factor
    )
    shares = jnp.exp(scores) / totals.T[:, :, None]
    rounded = shares.astype(jnp.bfloat16)
    grad_probs = jnp.einsum(
        "qhc,khc->hqk", grad_rows, value_rows, preferred_element_type=jnp.float32
    )
    grad_scores = (shares * (grad_probs - row_dots.T[:, :, None])).astype(jnp.bfloat16)
    query_part = (
        jnp.einsum("hqk,khc->qhc", grad_scores, key_rows, preferred_element_type=jnp.float32)
        * factor
    )
    key_part = (
        jnp.einsum("hqk,qhc->khc", grad_scores, query_rows, preferred_element_type=jnp.float32)
        * factor
    )
    value_part = jnp.einsum("hqk,qhc->khc", rounded, grad_rows, preferred_element_type=jnp.float32)
    return (query_part, key_part, value_part)


def forward_pairs(query_rows, key_rows, value_rows):
    output, sums_row = lax.map(
        lambda blocks: forward_block(*blocks),
        (to_pairs(query_rows), to_pairs(key_rows), to_pairs(value_rows)),
    )
    return (from_pairs(output), from_pairs(sums_row))


def backward_pairs(query_rows, key_rows, value_rows, grad_rows, totals, row_dots):
    parts_out = lax.map(
        lambda blocks: backward_block(*blocks),
        (
            to_pairs(query_rows),
            to_pairs(key_rows),
            to_pairs(value_rows),
            to_pairs(grad_rows),
            to_pairs(totals),
            to_pairs(row_dots),
        ),
    )
    return tuple((from_pairs(part) for part in parts_out))


def swap_keys(members, which_bit):
    return (swapped(members[0], "seq", which_bit),)


def swap_grads(tensor, which_bit):
    return swapped(tensor, "seq", which_bit)


def double_up(members, bit_list, swapper):
    position = lax.axis_index("seq")
    for which_bit in bit_list:
        partner = swapper(members, which_bit)
        on_upper = position >> which_bit & 1 == 1
        members = tuple(
            (
                jnp.where(
                    on_upper, jnp.concatenate([theirs, mine], 1), jnp.concatenate([mine, theirs], 1)
                )
                for mine, theirs in zip(members, partner)
            )
        )
    return members


def halve_down(buffer, bit_list, swapper):
    position = lax.axis_index("seq")
    for which_bit in reversed(bit_list):
        half_rows = buffer.shape[1] // 2
        lower_half = buffer[:, :half_rows]
        upper_half = buffer[:, half_rows:]
        on_upper = position >> which_bit & 1 == 1
        sending = jnp.where(on_upper, lower_half, upper_half)
        keeping = jnp.where(on_upper, upper_half, lower_half)
        buffer = keeping + swapper(sending, which_bit)
    return buffer


def gather_forward(near_query, near_keys, near_values, bit_count):
    selected, head_count, head_size = near_keys.shape
    model_width = head_count * head_size
    stacked = jnp.stack(
        [near_keys.reshape(selected, model_width), near_values.reshape(selected, model_width)]
    )
    if bit_count > 0:
        gathered = double_up((stacked,), list(range(bit_count)), swap_keys)[0]
    else:
        gathered = lax.all_gather(stacked, "seq", axis=1, tiled=True)
    gathered_rows = gathered.shape[1]
    far_keys = gathered[0].reshape(gathered_rows, head_count, head_size)
    far_values = gathered[1].reshape(gathered_rows, head_count, head_size)
    output, sums_row = forward_pairs(near_query, far_keys, far_values)
    return (output * sums_row[:, :, None], sums_row, (far_keys, far_values))


def partial_grads(near_query, far_keys, far_values, near_grad, near_totals, near_dots, bit_count):
    query_part, far_key_grad, far_value_grad = backward_pairs(
        near_query, far_keys, far_values, near_grad, near_totals, near_dots
    )
    gathered_rows, head_count, head_size = far_keys.shape
    model_width = head_count * head_size
    partial_value = jnp.stack(
        [
            far_key_grad.reshape(gathered_rows, model_width),
            far_value_grad.reshape(gathered_rows, model_width),
        ]
    )
    if bit_count > 0:
        summed = halve_down(partial_value, list(range(bit_count)), swap_grads)
    else:
        summed = lax.psum_scatter(partial_value, "seq", scatter_dimension=1, tiled=True)
    selected = summed.shape[1]
    return (
        query_part,
        summed[0].reshape(selected, head_count, head_size),
        summed[1].reshape(selected, head_count, head_size),
    )


def group_grads(near_query, far_keys, far_values, near_grad, near_totals, near_dots, bit_count):
    result = partial_grads(
        near_query, far_keys, far_values, near_grad, near_totals, near_dots, bit_count
    )
    return result


def gather_backward(saved, near_query, near_grad, near_totals, near_dots, bit_count):
    far_keys, far_values = saved
    if bit_count == 0:
        result = partial_grads(
            near_query, far_keys, far_values, near_grad, near_totals, near_dots, bit_count
        )
    else:
        result = group_grads(
            near_query, far_keys, far_values, near_grad, near_totals, near_dots, bit_count
        )
    return result


def per_device(queries, key_states, value_states, cotangent, offsets):
    local_rows, model_width = queries.shape
    head_count = offsets.shape[1]
    head_size = model_width // head_count
    full_bits = lax.axis_size("seq").bit_length() - 1

    def split_heads(tensor):
        return tensor.reshape(local_rows, head_count, head_size)

    query_heads = split_heads(queries)
    key_heads = split_heads(key_states)
    value_heads = split_heads(value_states)
    grad_heads = split_heads(cotangent)
    broad_bit_count = full_bits - 1
    branch_list = [
        (1, offsets[0], 1),
        (DILATION_TWO, offsets[0], 4),
        (DILATION_THREE, offsets[1], broad_bit_count),
        (DILATION_FOUR, offsets[2], 0),
    ]
    numerator = jnp.zeros((local_rows, head_count, head_size), jnp.float32)
    totals = jnp.zeros((local_rows, head_count), jnp.float32)
    stored = []
    for dilation, offset_row, bit_count in branch_list:
        group_bits = bit_count if bit_count > 0 else full_bits
        near_query = pick_rows(query_heads, offset_row, dilation)
        near_keys = pick_rows(key_heads, offset_row, dilation)
        near_values = pick_rows(value_heads, offset_row, dilation)
        if dilation == 1:
            weighted, sums_row, saved = gather_forward(
                near_query, near_keys, near_values, bit_count
            )
        else:
            weighted, sums_row, saved = gather_forward(
                near_query, near_keys, near_values, bit_count
            )
        numerator = numerator + place_rows(weighted, offset_row, dilation)
        totals = totals + place_rows(sums_row[:, :, None], offset_row, dilation)[:, :, 0]
        stored.append(
            (dilation, offset_row, bit_count, group_bits, near_query, near_keys, near_values, saved)
        )
    merged = numerator / totals[:, :, None]
    attended = merged.astype(jnp.bfloat16).reshape(local_rows, model_width)
    row_dots = jnp.sum(grad_heads.astype(jnp.float32) * merged, axis=-1)
    grad_query = jnp.zeros((local_rows, head_count, head_size), jnp.float32)
    grad_keys = jnp.zeros((local_rows, head_count, head_size), jnp.float32)
    grad_values = jnp.zeros((local_rows, head_count, head_size), jnp.float32)
    for (
        dilation,
        offset_row,
        bit_count,
        group_bits,
        near_query,
        near_keys,
        near_values,
        saved,
    ) in stored:
        near_grad = pick_rows(grad_heads, offset_row, dilation)
        near_totals = pick_rows(totals[:, :, None], offset_row, dilation)[:, :, 0]
        near_dots = pick_rows(row_dots[:, :, None], offset_row, dilation)[:, :, 0]
        if dilation == 1:
            query_part, key_part, value_part = partial_grads(
                near_query, saved[0], saved[1], near_grad, near_totals, near_dots, bit_count
            )
        else:
            query_part, key_part, value_part = gather_backward(
                saved, near_query, near_grad, near_totals, near_dots, bit_count
            )
        grad_query = grad_query + place_rows(query_part, offset_row, dilation)
        grad_keys = grad_keys + place_rows(key_part, offset_row, dilation)
        grad_values = grad_values + place_rows(value_part, offset_row, dilation)
    return (
        attended,
        grad_query.astype(jnp.bfloat16).reshape(local_rows, model_width),
        grad_keys.astype(jnp.bfloat16).reshape(local_rows, model_width),
        grad_values.astype(jnp.bfloat16).reshape(local_rows, model_width),
    )


def solution(mesh):
    return jax.shard_map(
        per_device,
        mesh=mesh,
        in_specs=(P("seq", None), P("seq", None), P("seq", None), P("seq", None), P()),
        out_specs=(P("seq", None), P("seq", None), P("seq", None), P("seq", None)),
        check_vma=False,
    )
```

profile of v0, /device:TPU:1, one launch (start us, length us, event | category | flops | bytes accessed | tf_op | source)
XLA Modules:
  0.0 829.3 jit_solution(4940436757072628498)
XLA Ops:
  7.2 2.3 reshape_reshape.43
  10.4 2.2 reshape_reshape.37
  12.6 2.2 reshape_reshape.38
  14.8 2.2 reshape_reshape.36
  17.1 4.1 select_reduce_fusion
  22.5 3.5 collective-permute-start.1
  31.7 6.0 select_reduce_fusion.4
  40.2 75.8 %all_gather.3 = bf16[2,256,768]{2,0,1:T(2,128)(2,1)S(1)} all-gather(bf16[2,1,768]{2,0,1:T(2,128)(2,1)S(1)} %copy.537), channel_id=1, replica_groups=mesh['seq'=256] {'seq'}, dimensions={1}, use_global_device_ids=true | all-gather | bytes 789504 | tf_op jit(solution)/shard_map/all_gather | solution.py:154
  116.0 2.0 fusion.177
  118.0 2.2 copy.640
  120.2 2.0 copy.541
  124.3 17.9 %while.107 = (s32[]{:T(128)}, f32[8,1,2,48]{3,2,1,0:T(2,128)S(1)}, f32[8,1,2]{2,1,0:T(1,128)S(1)}, bf16[8,256,2,48]{3,2,1,0:T(2,128)(2,1)}, bf16[8,1,2,48]{3,2,1...) while((s32[]{:T(128)}, f32[8,1,2,48]{3,2,1,0:T(2,128)S(1)}, f32[8,1,2]{2,1,0:T(1,128)S(1)}, ...), condition=%wide.region_20.21_spmd, body=%wide.region_18.20_spmd.sunk | while | flops 100864 | bytes 307253 | solution.py:86
  146.4 2.8 collective-permute-start.7
  149.3 2.1 collective-permute-done.7
  156.5 5.4 collective-permute-done.8
  165.6 16.6 %collective-permute-done.9 = bf16[2,64,768]{1,2,0:T(8,128)(2,1)S(1)} collective-permute-done((bf16[2,64,768]{1,2,0:T(8,128)(2,1)S(1)}, bf16[2,64,768]{1,2,0:T(8,128)(2,1)S(1)}, u32[]{:S(2)}, u32[]{:S(2)}) %collective-permute-start.9) | collective-permute-done | bytes 196640 | tf_op jit(solution)/shard_map/ppermute | solution.py:18
  182.6 3.9 collective-permute-start.10
  195.1 10.3 %collective-permute-done.10 = bf16[2,128,768]{1,2,0:T(8,128)(2,1)} collective-permute-done((bf16[2,128,768]{1,2,0:T(8,128)(2,1)S(1)}, bf16[2,128,768]{1,2,0:T(8,128)(2,1)}, u32[]{:S(2)}, u32[]{:S(2)}) %collective-permute-start.10) | collective-permute-done | bytes 393248 | tf_op jit(solution)/shard_map/ppermute | solution.py:18
  205.4 2.3 maximum_select_fusion.4
  212.6 13.7 %while.104 = (s32[]{:T(128)}, f32[8,256,2,48]{1,3,2,0:T(8,128)S(1)}, f32[8,256,2]{1,2,0:T(2,128)S(1)}, bf16[8,512,2,48]{1,3,2,0:T(8,128)(2,1)}, bf16[8,256,2,48]...) while((s32[]{:T(128)}, f32[8,256,2,48]{1,3,2,0:T(8,128)S(1)}, ...), condition=%wide.region_2.3_spmd, body=%wide.region_0.2_spmd.sunk | while | flops 51379712 | bytes 2451545 | solution.py:86
  228.3 2.3 maximum_select_fusion.1
  231.6 10.8 %while.105 = (s32[]{:T(128)}, f32[8,32,2,48]{3,1,2,0:T(8,128)S(1)}, f32[8,32,2]{1,2,0:T(2,128)S(1)}, bf16[8,512,2,48]{1,3,2,0:T(8,128)(2,1)}, bf16[8,32,2,48]{3,...) while((s32[]{:T(128)}, f32[8,32,2,48]{3,1,2,0:T(8,128)S(1)}, ...), condition=%wide.region_8.9_spmd, body=%wide.region_6.8_spmd.sunk | while | flops 6422466 | bytes 513369 | solution.py:86
  250.6 2.3 maximum_select_fusion.2
  253.5 8.9 %while.106 = (s32[]{:T(128)}, f32[8,4,2,48]{3,1,2,0:T(4,128)S(1)}, f32[8,4,2]{1,2,0:T(2,128)S(1)}, bf16[8,512,2,48]{1,3,2,0:T(8,128)(2,1)S(1)}, bf16[8,4,2,48]{3...) while((s32[]{:T(128)}, f32[8,4,2,48]{3,1,2,0:T(4,128)S(1)}, ...), condition=%wide.region_14.15_spmd, body=%wide.region_12.14_spmd.sunk | while | flops 802810 | bytes 240761 | solution.py:86
  275.3 50.4 %while.109 = (s32[]{:T(128)}, f32[8,32,2,48]{3,1,2,0:T(8,128)}, f32[8,512,2,48]{1,3,2,0:T(8,128)S(1)}, f32[8,512,2,48]{1,3,2,0:T(8,128)}, bf16[8,512,2,48]{1,3,2...) while((s32[]{:T(128)}, f32[8,32,2,48]{3,1,2,0:T(8,128)}, ...), condition=%wide.region_28.29_spmd, body=%wide.region_27.28_spmd.sunk | while | flops 15977474 | bytes 1383801 | solution.py:94
  325.7 2.8 broadcast_select_fusion.1
  331.6 50.2 %while.110 = (s32[]{:T(128)}, f32[8,4,2,48]{3,1,2,0:T(4,128)S(1)}, f32[8,512,2,48]{1,3,2,0:T(8,128)}, f32[8,512,2,48]{1,3,2,0:T(8,128)}, bf16[8,512,2,48]{1,3,2,...) while((s32[]{:T(128)}, f32[8,4,2,48]{3,1,2,0:T(4,128)S(1)}, ...), condition=%wide.region_33.34_spmd, body=%wide.region_32.33_spmd.sunk | while | flops 2040194 | bytes 779577 | solution.py:94
  382.4 3.3 broadcast_select_fusion
  391.0 78.7 %while.111 = (s32[]{:T(128)}, f32[8,1,2,48]{3,2,1,0:T(2,128)}, f32[8,256,2,48]{1,3,2,0:T(8,128)}, f32[8,256,2,48]{1,3,2,0:T(8,128)}, bf16[8,256,2,48]{3,2,1,0:T(...) while((s32[]{:T(128)}, f32[8,1,2,48]{3,2,1,0:T(2,128)}, ...), condition=%wide.region_38.39_spmd, body=%wide.region_37.38_spmd.sunk | while | flops 298178 | bytes 1155169 | solution.py:94
  470.4 2.6 pad_maximum_fusion.3
  473.0 3.7 copy.598
  476.8 2.3 select_add_fusion.1
  484.4 3.0 collective-permute-start.18
  490.0 62.4 %while.108 = (s32[]{:T(128)}, f32[8,256,2,48]{1,3,2,0:T(8,128)}, f32[8,512,2,48]{1,3,2,0:T(8,128)S(1)}, f32[8,512,2,48]{1,3,2,0:T(8,128)}, bf16[8,512,2,48]{1,3,...) while((s32[]{:T(128)}, f32[8,256,2,48]{1,3,2,0:T(8,128)}, ...), condition=%wide.region_23.24_spmd, body=%wide.region_22.23_spmd.sunk | while | flops 127475712 | bytes 5719161 | solution.py:94
  554.2 2.8 broadcast_select_fusion.2
  557.0 2.2 collective-permute-start.12
  568.5 175.6 %all-reduce.3.cloned.1.call-done = f32[2,256,768]{2,0,1:T(2,128)} async-done(((f32[2,256,768]{2,0,1:T(2,128)}), f32[2,256,768]{2,0,1:T(2,128)}) %all-reduce.3.cloned.1.call-update) | async-done | bytes 1572880
  747.3 3.7 collective-permute-start.19
  754.4 13.9 %collective-permute-done.19 = f32[2,64,768]{2,1,0:T(8,128)} collective-permute-done((f32[2,64,768]{2,1,0:T(8,128)S(1)}, f32[2,64,768]{2,1,0:T(8,128)}, u32[]{:S(2)}, u32[]{:S(2)}) %collective-permute-start.19) | collective-permute-done | bytes 393248 | tf_op jit(solution)/shard_map/ppermute | solution.py:18
  774.4 2.3 collective-permute-done.20
  778.6 2.8 collective-permute-start.21
  781.4 3.8 select_add_fusion.2
  788.3 2.1 collective-permute-done.22
  792.1 3.7 collective-permute-start.23
  798.0 2.3 copy.600
  802.5 2.3 copy.585
  810.8 3.1 broadcast_in_dim.594
  813.9 3.6 fusion.157
  (752 shorter events, 418.2 us)
Async XLA Ops:
  7.2 5.4 copy-start.22
  7.2 736.9 %all-reduce.3.cloned.1.call-start = ((), (), s32[]{:S(2)}) async-start(), calls=%async_computation | async-start | bytes 3145728
  9.5 5.3 copy-start.13
  10.4 29.2 %copy-start.55 = (s32[16]{0:T(128)}, s32[16]{0:T(128)S(1)}, u32[]{:S(2)}) copy-start(s32[16]{0:T(128)S(1)} %get-tuple-element.839) | copy-start | bytes 196
  10.4 176.9 %copy-start.61 = (pred[8,16]{1,0:T(8,128)(4,1)}, pred[8,16]{1,0:T(8,128)(4,1)S(1)}, u32[]{:S(2)}) copy-start(pred[8,16]{1,0:T(8,128)(4,1)S(1)} %iota_compare_fusion.3) | copy-start | bytes 388
  17.1 8.9 %copy-start.21 = (bf16[256,768]{1,0:T(8,128)(2,1)S(1)}, bf16[256,768]{1,0:T(8,128)(2,1)}, u32[]{:S(2)}) copy-start(bf16[256,768]{1,0:T(8,128)(2,1)} %param.24) | copy-start | bytes 1179652
  22.5 132.0 %collective-permute-start.1 = (bf16[2,32,768]{1,2,0:T(8,128)(2,1)}, bf16[2,32,768]{1,2,0:T(8,128)(2,1)}, u32[]{:S(2)}, u32[]{:S(2)}) collective-permute-start(bf16[2,32,768]{1,2,0:T(8,128)(2,1)} %copy.518), channel_id=1, source_target_pairs={{0,1},{1,0},{2,3},{3,2},{4,5},{5,4},{6,7},{7,6},{8,9},{9,8},{10,11... | collective-permute-start | bytes 294920 | tf_op jit(solution)/shard_map/ppermute | solution.py:18
  26.1 241.1 %copy-start.6 = (bf16[256,768]{0,1:T(8,128)(2,1)}, bf16[256,768]{0,1:T(8,128)(2,1)S(1)}, u32[]{:S(2)}) copy-start(bf16[256,768]{0,1:T(8,128)(2,1)S(1)} %copy.552) | copy-start | bytes 1179652
  38.0 105.6 %collective-permute-start.5 = (bf16[2,4,768]{2,1,0:T(4,128)(2,1)S(1)}, bf16[2,4,768]{2,1,0:T(4,128)(2,1)S(1)}, u32[]{:S(2)}, u32[]{:S(2)}) collective-permute-start(bf16[2,4,768]{2,1,0:T(4,128)(2,1)S(1)} %pad_maximum_fusion.8), channel_id=1, source_target_pairs={{0,1},{1,0},{2,3},{3,2},{4,5},{5,4},{6,7},{7,6},{8,9},{9,8},{10,11... | collective-permute-start | bytes 36872 | tf_op jit(solution)/shard_map/ppermute | solution.py:18
  39.1 169.9 %collective-permute-start = (bf16[2,256,768]{2,1,0:T(8,128)(2,1)}, bf16[2,256,768]{2,1,0:T(8,128)(2,1)}, u32[]{:S(2)}, u32[]{:S(2)}) collective-permute-start(bf16[2,256,768]{2,1,0:T(8,128)(2,1)} %pad_maximum_fusion.4), channel_id=1, source_target_pairs={{0,1},{1,0},{2,3},{3,2},{4,5},{5,4},{6,7},{7,6},{8,9},{9,8},{10,11... | collective-permute-start | bytes 2359304 | tf_op jit(solution)/shard_map/ppermute | solution.py:18
  39.6 78.4 %copy-start.41 = (pred[256,16]{0,1:T(8,128)(4,1)}, pred[256,16]{0,1:T(8,128)(4,1)S(1)}, u32[]{:S(2)}) copy-start(pred[256,16]{0,1:T(8,128)(4,1)S(1)} %iota_compare_fusion.1) | copy-start | bytes 12292
  142.2 14.1 %copy-start.7 = (bf16[8,256,2,48]{3,2,1,0:T(2,128)(2,1)}, bf16[8,256,2,48]{3,2,1,0:T(2,128)(2,1)S(1)}, u32[]{:S(2)}) copy-start(bf16[8,256,2,48]{3,2,1,0:T(2,128)(2,1)S(1)} %get-tuple-element.1492) | copy-start | bytes 1179652
  143.5 12.8 %copy-start.58 = (f32[16]{0:T(128)}, f32[16]{0:T(128)S(1)}, u32[]{:S(2)}) copy-start(f32[16]{0:T(128)S(1)} %mul.164) | copy-start | bytes 196
  143.6 2.8 collective-permute-start.6
  146.4 5.1 collective-permute-start.7
  153.6 8.2 collective-permute-start.8
  156.4 31.7 %copy-start.25 = (bf16[4,16,48]{0,2,1:T(8,128)(2,1)S(1)}, bf16[4,16,48]{0,2,1:T(8,128)(2,1)}, u32[]{:S(2)}) copy-start(bf16[4,16,48]{0,2,1:T(8,128)(2,1)} %get-tuple-element.660) | copy-start | bytes 18436
  156.4 7.9 collective-permute-start.2
  162.3 19.9 %collective-permute-start.9 = (bf16[2,64,768]{1,2,0:T(8,128)(2,1)S(1)}, bf16[2,64,768]{1,2,0:T(8,128)(2,1)S(1)}, u32[]{:S(2)}, u32[]{:S(2)}) collective-permute-start(bf16[2,64,768]{1,2,0:T(8,128)(2,1)S(1)} %maximum_select_fusion.7), channel_id=1, source_target_pairs={{0,16},{16,0},{1,17},{17,1},{2,18},{18,2},{3,19},{19,3},{4,20},{20... | collective-permute-start | bytes 589832 | tf_op jit(solution)/shard_map/ppermute | solution.py:18
  164.2 29.7 %copy-start.29 = (bf16[32,16,48]{2,1,0:T(8,128)(2,1)S(1)}, bf16[32,16,48]{2,1,0:T(8,128)(2,1)}, u32[]{:S(2)}) copy-start(bf16[32,16,48]{2,1,0:T(8,128)(2,1)} %get-tuple-element.664) | copy-start | bytes 147460
  164.2 29.7 %copy-start.30 = (bf16[32,16,48]{2,1,0:T(8,128)(2,1)S(1)}, bf16[32,16,48]{2,1,0:T(8,128)(2,1)}, u32[]{:S(2)}) copy-start(bf16[32,16,48]{2,1,0:T(8,128)(2,1)} %get-tuple-element.666) | copy-start | bytes 147460
  164.8 29.2 %collective-permute-start.3 = (bf16[2,128,768]{1,2,0:T(8,128)(2,1)S(1)}, bf16[2,128,768]{1,2,0:T(8,128)(2,1)S(1)}, u32[]{:S(2)}, u32[]{:S(2)}) collective-permute-start(bf16[2,128,768]{1,2,0:T(8,128)(2,1)S(1)} %maximum_select_fusion.6), channel_id=1, source_target_pairs={{0,4},{4,0},{1,5},{5,1},{2,6},{6,2},{3,7},{7,3},{8,12},{12,8},{9,1... | collective-permute-start | bytes 1179656 | tf_op jit(solution)/shard_map/ppermute | solution.py:18
  182.6 22.8 %collective-permute-start.10 = (bf16[2,128,768]{1,2,0:T(8,128)(2,1)S(1)}, bf16[2,128,768]{1,2,0:T(8,128)(2,1)}, u32[]{:S(2)}, u32[]{:S(2)}) collective-permute-start(bf16[2,128,768]{1,2,0:T(8,128)(2,1)S(1)} %maximum_select_fusion.8), channel_id=1, source_target_pairs={{0,32},{32,0},{1,33},{33,1},{2,34},{34,2},{3,35},{35,3},{4,36},{36... | collective-permute-start | bytes 1179656 | tf_op jit(solution)/shard_map/ppermute | solution.py:18
  187.3 20.4 %copy-start.36 = (pred[64,16]{1,0:T(8,128)(4,1)}, pred[64,16]{1,0:T(8,128)(4,1)S(1)}, u32[]{:S(2)}) copy-start(pred[64,16]{1,0:T(8,128)(4,1)S(1)} %copy.524) | copy-start | bytes 3076
  195.1 33.2 %collective-permute-start.4 = (bf16[2,256,768]{1,2,0:T(8,128)(2,1)}, bf16[2,256,768]{1,2,0:T(8,128)(2,1)}, u32[]{:S(2)}, u32[]{:S(2)}) collective-permute-start(bf16[2,256,768]{1,2,0:T(8,128)(2,1)} %maximum_select_fusion.3), channel_id=1, source_target_pairs={{0,8},{8,0},{1,9},{9,1},{2,10},{10,2},{3,11},{11,3},{4,12},{12,4},... | collective-permute-start | bytes 2359304 | tf_op jit(solution)/shard_map/ppermute | solution.py:18
  207.7 42.9 %collective-permute-start.11 = (bf16[2,256,768]{1,2,0:T(8,128)(2,1)}, bf16[2,256,768]{1,2,0:T(8,128)(2,1)}, u32[]{:S(2)}, u32[]{:S(2)}) collective-permute-start(bf16[2,256,768]{1,2,0:T(8,128)(2,1)} %maximum_select_fusion.4), channel_id=1, source_target_pairs={{0,64},{64,0},{1,65},{65,1},{2,66},{66,2},{3,67},{67,3},{4,68},{68... | collective-permute-start | bytes 2359304 | tf_op jit(solution)/shard_map/ppermute | solution.py:18
  226.3 40.9 %copy-start.9 = (f32[8,256,2,48]{1,3,2,0:T(8,128)}, f32[8,256,2,48]{1,3,2,0:T(8,128)S(1)}, u32[]{:S(2)}) copy-start(f32[8,256,2,48]{1,3,2,0:T(8,128)S(1)} %get-tuple-element.352) | copy-start | bytes 2359300
  252.9 10.3 %copy-start.37 = (pred[64,16]{1,0:T(8,128)(4,1)S(1)}, pred[64,16]{1,0:T(8,128)(4,1)}, u32[]{:S(2)}) copy-start(pred[64,16]{1,0:T(8,128)(4,1)} %copy-done.36) | copy-start | bytes 3076
  328.5 148.3 %collective-permute-start.13 = (f32[2,256,768]{1,2,0:T(8,128)}, f32[2,256,768]{1,2,0:T(8,128)}, u32[]{:S(2)}, u32[]{:S(2)}) collective-permute-start(f32[2,256,768]{1,2,0:T(8,128)} %broadcast_select_fusion.1), channel_id=1, source_target_pairs={{0,8},{8,0},{1,9},{9,1},{2,10},{10,2},{3,11},{11,3},{4,12},{12,4},... | collective-permute-start | bytes 4718600 | tf_op jit(solution)/shard_map/ppermute | solution.py:18
  382.4 4.7 copy-start.33
  382.4 4.7 copy-start.49
  382.4 4.7 copy-start.62
  382.4 4.7 copy-start.64
  385.8 95.7 %collective-permute-start.17 = (f32[2,256,768]{1,2,0:T(8,128)}, f32[2,256,768]{1,2,0:T(8,128)}, u32[]{:S(2)}, u32[]{:S(2)}) collective-permute-start(f32[2,256,768]{1,2,0:T(8,128)} %broadcast_select_fusion), channel_id=1, source_target_pairs={{0,64},{64,0},{1,65},{65,1},{2,66},{66,2},{3,67},{67,3},{4,68},{68... | collective-permute-start | bytes 4718600 | tf_op jit(solution)/shard_map/ppermute | solution.py:18
  480.1 270.9 %collective-permute-start.14 = (f32[2,128,768]{1,2,0:T(8,128)}, f32[2,128,768]{1,2,0:T(8,128)}, u32[]{:S(2)}, u32[]{:S(2)}) collective-permute-start(f32[2,128,768]{1,2,0:T(8,128)} %slice_select_fusion.8), channel_id=1, source_target_pairs={{0,4},{4,0},{1,5},{5,1},{2,6},{6,2},{3,7},{7,3},{8,12},{12,8},{9,1... | collective-permute-start | bytes 2359304 | tf_op jit(solution)/shard_map/ppermute | solution.py:18
  483.4 5.1 copy-start.4
  484.4 261.0 %collective-permute-start.18 = (f32[2,128,768]{1,2,0:T(8,128)}, f32[2,128,768]{1,2,0:T(8,128)}, u32[]{:S(2)}, u32[]{:S(2)}) collective-permute-start(f32[2,128,768]{1,2,0:T(8,128)} %slice_select_fusion.5), channel_id=1, source_target_pairs={{0,32},{32,0},{1,33},{33,1},{2,34},{34,2},{3,35},{35,3},{4,36},{36... | collective-permute-start | bytes 2359304 | tf_op jit(solution)/shard_map/ppermute | solution.py:18
  554.2 5.0 copy-start.24
  557.0 224.5 %collective-permute-start.12 = (f32[2,256,768]{1,2,0:T(8,128)}, f32[2,256,768]{1,2,0:T(8,128)}, u32[]{:S(2)}, u32[]{:S(2)}) collective-permute-start(f32[2,256,768]{1,2,0:T(8,128)} %broadcast_select_fusion.2), channel_id=1, source_target_pairs={{0,1},{1,0},{2,3},{3,2},{4,5},{5,4},{6,7},{7,6},{8,9},{9,8},{10,11... | collective-permute-start | bytes 4718600 | tf_op jit(solution)/shard_map/ppermute | solution.py:18
  565.8 179.7 %copy-start.5 = (f32[2,256,768]{1,2,0:T(8,128)S(1)}, f32[2,256,768]{1,2,0:T(8,128)}, u32[]{:S(2)}) copy-start(f32[2,256,768]{1,2,0:T(8,128)} %copy-done.4) | copy-start | bytes 4718596
  747.3 21.1 %collective-permute-start.19 = (f32[2,64,768]{2,1,0:T(8,128)S(1)}, f32[2,64,768]{2,1,0:T(8,128)}, u32[]{:S(2)}, u32[]{:S(2)}) collective-permute-start(f32[2,64,768]{2,1,0:T(8,128)S(1)} %copy.586), channel_id=1, source_target_pairs={{0,16},{16,0},{1,17},{17,1},{2,18},{18,2},{3,19},{19,3},{4,20},{20... | collective-permute-start | bytes 1179656 | tf_op jit(solution)/shard_map/ppermute | solution.py:18
  753.2 18.3 %collective-permute-start.15 = (f32[2,64,768]{2,1,0:T(8,128)S(1)}, f32[2,64,768]{2,1,0:T(8,128)}, u32[]{:S(2)}, u32[]{:S(2)}) collective-permute-start(f32[2,64,768]{2,1,0:T(8,128)S(1)} %copy.580), channel_id=1, source_target_pairs={{0,2},{2,0},{1,3},{3,1},{4,6},{6,4},{5,7},{7,5},{8,10},{10,8},{9,1... | collective-permute-start | bytes 1179656 | tf_op jit(solution)/shard_map/ppermute | solution.py:18
  771.1 5.6 collective-permute-start.20
  773.5 11.7 %collective-permute-start.16 = (f32[2,32,768]{2,1,0:T(8,128)S(1)}, f32[2,32,768]{2,1,0:T(8,128)S(1)}, u32[]{:S(2)}, u32[]{:S(2)}) collective-permute-start(f32[2,32,768]{2,1,0:T(8,128)S(1)} %copy.582), channel_id=1, source_target_pairs={{0,1},{1,0},{2,3},{3,2},{4,5},{5,4},{6,7},{7,6},{8,9},{9,8},{10,11... | collective-permute-start | bytes 589832 | tf_op jit(solution)/shard_map/ppermute | solution.py:18
  778.6 7.8 collective-permute-start.21
  787.5 3.0 collective-permute-start.22
  792.1 12.6 %collective-permute-start.23 = (f32[2,4,768]{2,1,0:T(4,128)}, f32[2,4,768]{2,1,0:T(4,128)}, u32[]{:S(2)}, u32[]{:S(2)}) collective-permute-start(f32[2,4,768]{2,1,0:T(4,128)} %copy.594), channel_id=1, source_target_pairs={{0,1},{1,0},{2,3},{3,2},{4,5},{5,4},{6,7},{7,6},{8,9},{9,8},{10,11... | collective-permute-start | bytes 73736 | tf_op jit(solution)/shard_map/ppermute | solution.py:18
  808.9 5.0 copy-start.17
  (51 other events, 128.0 us)
Sparse Core Ops, SparseCore 0:
  476.9 267.1 all-reduce.2
where the time goes:
time: 842 us; the launch traced here: 829 us
  waiting for transfers between devices  230 us (27%)
  matrix products  187 us (22%)
  local copies, waits for them, and re-layouts  164 us (19%)
  other arithmetic  120 us (14%)
  blocking collectives  75.8 us (9%)
  starting transfers between devices  36.2 us (4%)
  between operations  15.5 us (2%)
    unnamed x2, waiting for transfers between devices  176 us
    all_gather x1, blocking collectives, gather_forward(): gathered = lax.all_gather(stacked, 'seq', axis=1, tiled=True)  75.8 us
    ppermute x24, waiting for transfers between devices, swapped(): return lax.ppermute(block, axis, route)  54.2 us
    broadcast_in_dim x37, local copies, waits for them, and re-layouts, place_rows(): jnp.where(chosen[None, :, :, None], tensor[:, None], jnp.zeros((), tensor...  36.6 us
    ppermute x24, starting transfers between devices, swapped(): return lax.ppermute(block, axis, route)  36.2 us
    dot_general x24, matrix products, backward_block(): jnp.einsum('hqk,khc->qhc', grad_scores, key_rows, preferred_element_type=...  36.2 us
    dot_general x24, matrix products, backward_block(): jnp.einsum('hqk,qhc->khc', rounded, grad_rows, preferred_element_type=jnp...  33.4 us
    dot_general x24, matrix products, backward_block(): jnp.einsum('hqk,qhc->khc', grad_scores, query_rows, preferred_element_typ...  28.1 us
  transfers between devices with their start and end apart: 25, of which 10 were waited for; matrix products, arithmetic and copies ran while one was open for 43% of the time, Pallas kernels for 0%

commit v1 on v0

v1 whole, which is shorter than its diff:
```python
import math

import jax
import jax.numpy as jnp
from jax import lax
from jax.experimental import pallas as pl
from jax.experimental.pallas import tpu as pltpu
from jax.sharding import Mesh, PartitionSpec as P

HEADS = 16
WIDTH = 48
ROWS = 256
GROUP = 16
GROUP_ROWS = GROUP * ROWS
STRIDES = (8, 64, 256)
PICK_TWO = GROUP_ROWS // 8
PICK_THREE = GROUP_ROWS // 64
PICK_FOUR = GROUP_ROWS // 256
PICK_FAR = PICK_THREE + PICK_FOUR
FACTOR = WIDTH**-0.5
EXPONENT = FACTOR * math.log2(math.e)
BF16 = jnp.bfloat16
F32 = jnp.float32
LIMIT = 56 * 1024 * 1024

INSIDE = ("z_low", "x", "core")
ACROSS = ("y", "z_high")


def dot(a, b):
    return lax.dot_general(a, b, (((1,), (0,)), ((), ())), preferred_element_type=F32)


def dot_t(a, b):
    return lax.dot_general(a, b, (((1,), (1,)), ((), ())), preferred_element_type=F32)


def call(kernel, out_shape, scratch=(), smem=0, args=()):
    vmem = pl.BlockSpec(memory_space=pltpu.VMEM)
    specs = [pl.BlockSpec(memory_space=pltpu.SMEM)] * smem + [vmem] * (len(args) - smem)
    return pl.pallas_call(
        kernel,
        out_shape=out_shape,
        in_specs=specs,
        out_specs=jax.tree.map(lambda _: vmem, out_shape),
        scratch_shapes=list(scratch),
        compiler_params=pltpu.CompilerParams(vmem_limit_bytes=LIMIT),
    )(*args)


def pack_kernel(k_ref, v_ref, q_ref, g_ref, out_ref):
    for place, ref in enumerate((k_ref, v_ref, q_ref, g_ref)):
        turned = ref[...].T
        out_ref[:, place * WIDTH : (place + 1) * WIDTH, :] = turned.reshape(HEADS, WIDTH, ROWS)


def unpack_kernel(in_ref, a_ref, q_ref, k_ref, v_ref):
    for place, ref in enumerate((a_ref, q_ref, k_ref, v_ref)):
        block = in_ref[:, place * WIDTH : (place + 1) * WIDTH, :].reshape(HEADS * WIDTH, ROWS)
        ref[...] = block.T


def select_kernel(off_ref, r_ref, kv2_ref, qg2_ref, kv_far_ref, qg_far_ref):
    o2, o3, o4 = off_ref[0], off_ref[1], off_ref[2]
    count = ROWS // 8
    row = lax.broadcasted_iota(jnp.int32, (count + PICK_FAR, ROWS), 0)
    col = lax.broadcasted_iota(jnp.int32, (count + PICK_FAR, ROWS), 1)
    three = row - count
    four = three - PICK_THREE
    near = row < count
    is_three = jnp.logical_and(three >= 0, four < 0)
    target = jnp.where(near, 8 * row + o2, jnp.where(is_three, 64 * (three & 3) + o3, o4))
    source = jnp.where(is_three, three >> 2, four)
    hit = col == target
    far_kv = jnp.zeros((PICK_FAR, 2 * WIDTH), F32)
    far_qg = jnp.zeros((PICK_FAR, 2 * WIDTH), F32)
    for s in range(GROUP):
        chosen = jnp.logical_and(hit, jnp.logical_or(near, source == s))
        chosen = jnp.where(chosen, 1.0, 0.0).astype(BF16)
        kv = dot_t(chosen, r_ref[s, : 2 * WIDTH, :])
        qg = dot_t(chosen, r_ref[s, 2 * WIDTH :, :])
        kv2_ref[s * count : (s + 1) * count, :] = kv[:count].astype(BF16)
        qg2_ref[s * count : (s + 1) * count, :] = qg[:count].astype(BF16)
        far_kv = far_kv + kv[count:]
        far_qg = far_qg + qg[count:]
    qg_far_ref[...] = far_qg.astype(BF16)
    low = far_kv.astype(BF16)
    for s in range(GROUP):
        kv_far_ref[s] = low


def upper(q_t):
    return jnp.concatenate([q_t, jnp.zeros_like(q_t)], axis=0)


def lower(g_t):
    return jnp.concatenate([jnp.zeros_like(g_t), g_t], axis=0)


def forward_unit(kv, v_t, q_t):
    weights = jnp.exp2(dot(kv, upper(q_t)) * EXPONENT)
    sums = jnp.sum(weights, axis=0, keepdims=True)
    low = (weights * (1.0 / (sums * 0.25))).astype(BF16)
    output = dot(v_t, low) * 0.25
    return output * sums, sums


def to_rows(numerator, sums):
    queries = numerator.shape[1]
    block = jnp.concatenate(
        [numerator, jnp.broadcast_to(sums, (80, queries))], axis=0
    )
    return block.T


def backward_unit(kv, q_t, g_t, inverse, dots):
    shares = jnp.exp2(dot(kv, upper(q_t)) * EXPONENT) * inverse
    probs = dot(kv, lower(g_t))
    grad = (shares * (probs - dots)).astype(BF16)
    return shares.astype(BF16), grad


def turn(x):
    return x.T


def stack_far(all_ref, half):
    base = half * 8
    three = jnp.concatenate([all_ref[base + j, :PICK_THREE, :] for j in range(8)], axis=0)
    four = jnp.concatenate([all_ref[j, PICK_THREE:, :] for j in range(16)], axis=0)
    return three, four


def forward_kernel(
    off_ref, r_ref, kv2_ref, qg2_ref, kv_all_ref, qg_far_ref,
    att_ref, td_ref, td2_ref, far_ref, acc_ref, tdr_ref,
):
    o2, o3, o4, half = off_ref[0], off_ref[1], off_ref[2], off_ref[3]

    def segment(seg, carry):
        kv_t = jnp.concatenate([r_ref[2 * seg, : 2 * WIDTH, :], r_ref[2 * seg + 1, : 2 * WIDTH, :]], axis=1)
        kv = turn(kv_t)
        for part in range(2):
            s = 2 * seg + part
            numerator, sums = forward_unit(kv, kv_t[WIDTH:], r_ref[s, 2 * WIDTH : 3 * WIDTH, :])
            acc_ref[pl.ds(pl.multiple_of(s * ROWS, ROWS), ROWS), :] = to_rows(numerator, sums)
        return carry

    lax.fori_loop(0, 8, segment, 0)

    kv2 = kv2_ref[...]
    kv2_t = turn(kv2)
    qg2_t = turn(qg2_ref[...])
    for part in range(2):
        span = slice(part * 256, part * 256 + 256)
        numerator, sums = forward_unit(kv2, kv2_t[WIDTH:], qg2_t[:WIDTH, span])
        rows = pl.ds(part * 2048 + o2, 256, stride=8)
        acc_ref[rows, :] = acc_ref[rows, :] + to_rows(numerator, sums)

    kv3, kv4 = stack_far(kv_all_ref, half)
    qg_far = qg_far_ref[...]
    qg_far_t = turn(jnp.concatenate([qg_far, jnp.zeros((128 - PICK_FAR, 2 * WIDTH), BF16)], axis=0))
    q_far_t = qg_far_t[:WIDTH]
    numerator, sums = forward_unit(kv3, turn(kv3)[WIDTH:], q_far_t)
    rows = pl.ds(o3, PICK_THREE, stride=64)
    acc_ref[rows, :] = acc_ref[rows, :] + to_rows(numerator, sums)[:PICK_THREE]
    numerator, sums = forward_unit(kv4, turn(kv4)[WIDTH:], q_far_t)
    rows = pl.ds(o4, PICK_FOUR, stride=256)
    acc_ref[rows, :] = acc_ref[rows, :] + to_rows(numerator, sums)[PICK_THREE:PICK_FAR]

    def finish(s, carry):
        rows = pl.ds(pl.multiple_of(s * ROWS, ROWS), ROWS)
        block = acc_ref[rows, :].T
        total = block[WIDTH : WIDTH + 1]
        merged = block[:WIDTH] / total
        att_ref[s] = merged.astype(BF16)
        dots = jnp.sum(r_ref[s, 3 * WIDTH :, :].astype(F32) * merged, axis=0, keepdims=True)
        inverse = 1.0 / (total * 0.25)
        both = jnp.concatenate(
            [inverse, dots, jnp.zeros((126, ROWS), F32)], axis=0
        )
        td_ref[s] = both[:8]
        tdr_ref[rows, :] = both.T
        return carry

    lax.fori_loop(0, GROUP, finish, 0)

    td2_ref[...] = tdr_ref[pl.ds(o2, PICK_TWO, stride=8), :].T[:8]
    three = tdr_ref[pl.ds(o3, PICK_THREE, stride=64), :]
    four = tdr_ref[pl.ds(o4, PICK_FOUR, stride=256), :]
    td_far = jnp.concatenate([three, four], axis=0)
    block = jnp.concatenate([qg_far.astype(F32), td_far[:, : 128 - 2 * WIDTH]], axis=1)
    for s in range(GROUP):
        far_ref[s] = block


def backward_kernel(
    off_ref, r_ref, kv2_ref, qg2_ref, kv_all_ref, qg_all_ref, kv_far_ref, own_far_ref, att_ref, td_ref, td2_ref,
    out_ref, accq_ref, acckv_ref,
):
    o2, o3, o4, half = off_ref[0], off_ref[1], off_ref[2], off_ref[3]
    scale = FACTOR * 0.25

    def pick(grad_part, value_part):
        lane = lax.broadcasted_iota(jnp.int32, grad_part.shape, 1)
        return jnp.where(lane < WIDTH, grad_part * scale, value_part * 0.25)

    def widen(x):
        return jnp.concatenate([x, jnp.zeros((x.shape[0], 128 - x.shape[1]), F32)], axis=1)

    def query_rows(part_t):
        return jnp.concatenate([part_t * scale, jnp.zeros((128 - WIDTH, part_t.shape[1]), F32)], axis=0).T

    def segment(seg, carry):
        kv_t = jnp.concatenate([r_ref[2 * seg, : 2 * WIDTH, :], r_ref[2 * seg + 1, : 2 * WIDTH, :]], axis=1)
        kv = turn(kv_t)
        total_grad = jnp.zeros((512, 2 * WIDTH), F32)
        total_value = jnp.zeros((512, 2 * WIDTH), F32)
        for part in range(2):
            s = 2 * seg + part
            qg_t = r_ref[s, 2 * WIDTH :, :]
            shares, grad = backward_unit(
                kv, qg_t[:WIDTH], qg_t[WIDTH:], td_ref[s, 0:1, :], td_ref[s, 1:2, :]
            )
            accq_ref[pl.ds(pl.multiple_of(s * ROWS, ROWS), ROWS), :] = query_rows(dot(kv_t[:WIDTH], grad))
            qg = turn(qg_t)
            total_grad = total_grad + dot(grad, qg)
            total_value = total_value + dot(shares, qg)
        acckv_ref[pl.ds(pl.multiple_of(seg * 512, 512), 512), :] = widen(pick(total_grad, total_value))
        return carry

    lax.fori_loop(0, 8, segment, 0)

    kv2 = kv2_ref[...]
    kv2_t = turn(kv2)
    qg2 = qg2_ref[...]
    qg2_t = turn(qg2)
    total_grad = jnp.zeros((512, 2 * WIDTH), F32)
    total_value = jnp.zeros((512, 2 * WIDTH), F32)
    for part in range(2):
        span = slice(part * 256, part * 256 + 256)
        shares, grad = backward_unit(
            kv2, qg2_t[:WIDTH, span], qg2_t[WIDTH:, span], td2_ref[0:1, span], td2_ref[1:2, span]
        )
        rows = pl.ds(part * 2048 + o2, 256, stride=8)
        accq_ref[rows, :] = accq_ref[rows, :] + query_rows(dot(kv2_t[:WIDTH], grad))
        total_grad = total_grad + dot(grad, qg2[span])
        total_value = total_value + dot(shares, qg2[span])
    rows = pl.ds(o2, PICK_TWO, stride=8)
    acckv_ref[rows, :] = acckv_ref[rows, :] + widen(pick(total_grad, total_value))

    kv3, kv4 = stack_far(kv_all_ref, half)
    far3, far4 = stack_far(qg_all_ref, half)
    own_t = jnp.concatenate([own_far_ref[0], jnp.zeros((128 - PICK_FAR, 128), F32)], axis=0).T
    kv_own = kv_far_ref[0]
    for kv, far, stride, offset, low, count in (
        (kv3, far3, 64, o3, 0, PICK_THREE),
        (kv4, far4, 256, o4, PICK_THREE, PICK_FOUR),
    ):
        rows = pl.ds(offset, count, stride=stride)
        shares, grad = backward_unit(
            kv, own_t[:WIDTH].astype(BF16), own_t[WIDTH : 2 * WIDTH].astype(BF16),
            own_t[2 * WIDTH : 2 * WIDTH + 1], own_t[2 * WIDTH + 1 : 2 * WIDTH + 2],
        )
        part = query_rows(dot(turn(kv)[:WIDTH], grad))
        accq_ref[rows, :] = accq_ref[rows, :] + part[low : low + count]
        far_t = far.T
        qg = far[:, : 2 * WIDTH].astype(BF16)
        shares, grad = backward_unit(
            kv_own, far_t[:WIDTH].astype(BF16), far_t[WIDTH : 2 * WIDTH].astype(BF16),
            far_t[2 * WIDTH : 2 * WIDTH + 1], far_t[2 * WIDTH + 1 : 2 * WIDTH + 2],
        )
        part = widen(pick(dot(grad, qg), dot(shares, qg)))
        acckv_ref[rows, :] = acckv_ref[rows, :] + part[low : low + count]

    def finish(s, carry):
        rows = pl.ds(pl.multiple_of(s * ROWS, ROWS), ROWS)
        out_ref[s, :WIDTH, :] = att_ref[s]
        out_ref[s, WIDTH : 2 * WIDTH, :] = accq_ref[rows, :].T[:WIDTH].astype(BF16)
        out_ref[s, 2 * WIDTH :, :] = acckv_ref[rows, :].T[: 2 * WIDTH].astype(BF16)
        return carry

    lax.fori_loop(0, GROUP, finish, 0)


def per_device(queries, key_states, value_states, cotangent, offsets):
    struct = jax.ShapeDtypeStruct
    head = lax.axis_index(INSIDE)
    across = lax.axis_index(ACROSS)
    own = lax.dynamic_slice(offsets, (0, head), (3, 1))[:, 0]
    scalars = jnp.concatenate([own, (across // 8).astype(jnp.int32)[None]])

    packed = call(
        pack_kernel, struct((HEADS, 4 * WIDTH, ROWS), BF16), args=(key_states, value_states, queries, cotangent)
    )
    r = lax.all_to_all(packed, INSIDE, 0, 0, tiled=True)
    kv2, qg2, kv_far, qg_far = call(
        select_kernel,
        (
            struct((PICK_TWO, 2 * WIDTH), BF16),
            struct((PICK_TWO, 2 * WIDTH), BF16),
            struct((GROUP, PICK_FAR, 2 * WIDTH), BF16),
            struct((PICK_FAR, 2 * WIDTH), BF16),
        ),
        smem=1,
        args=(scalars, r),
    )
    kv_all = lax.all_to_all(kv_far, ACROSS, 0, 0, tiled=True)
    att, td, td2, far = call(
        forward_kernel,
        (
            struct((GROUP, WIDTH, ROWS), BF16),
            struct((GROUP, 8, ROWS), F32),
            struct((8, PICK_TWO), F32),
            struct((GROUP, PICK_FAR, 128), F32),
        ),
        scratch=(pltpu.VMEM((GROUP_ROWS, 128), F32), pltpu.VMEM((GROUP_ROWS, 128), F32)),
        smem=1,
        args=(scalars, r, kv2, qg2, kv_all, qg_far),
    )
    qg_all = lax.all_to_all(far, ACROSS, 0, 0, tiled=True)
    back = call(
        backward_kernel,
        struct((GROUP, 4 * WIDTH, ROWS), BF16),
        scratch=(pltpu.VMEM((GROUP_ROWS, 128), F32), pltpu.VMEM((GROUP_ROWS, 128), F32)),
        smem=1,
        args=(scalars, r, kv2, qg2, kv_all, qg_all, kv_far, far, att, td, td2),
    )
    out = lax.all_to_all(back, INSIDE, 0, 0, tiled=True)
    shape = struct((ROWS, HEADS * WIDTH), BF16)
    return tuple(call(unpack_kernel, (shape,) * 4, args=(out,)))


def solution(mesh):
    axes = ("y", "z_high", "z_low", "x", "core")
    inner = Mesh(mesh.devices.reshape(4, 4, 2, 4, 2), axes)
    rows = P(axes, None)
    return jax.shard_map(
        per_device,
        mesh=inner,
        in_specs=(rows, rows, rows, rows, P()),
        out_specs=(rows, rows, rows, rows),
        check_vma=False,
    )
```

time: 842 us -> 146 us (0.17); the launches traced: 829 us -> 145 us
  waiting for transfers between devices: 230 us -> 21 us
  matrix products: 187 us -> 0 us
  local copies, waits for them, and re-layouts: 164 us -> 1.36 us
  other arithmetic: 120 us -> 0.65 us
  Pallas kernels: 0 us -> 38.3 us
  starting transfers between devices: 36.2 us -> 7.17 us
  between operations: 15.5 us -> 0.65 us
    dot_general x184 -> x0, matrix products: 187 us -> none  [the longest x24 36.2 us: backward_block(): jnp.einsum('hqk,khc->qhc', grad_scores, key_rows, preferred_element_type=...]
    unnamed x2 -> x0, waiting for transfers between devices: 176 us -> none
    all_to_all x0 -> x3, blocking collectives: none -> 76.4 us  [the longest x1 28.9 us: per_device(): out = lax.all_to_all(back, INSIDE, 0, 0, tiled=True)]
    all_gather x1 -> x0, blocking collectives: 75.8 us -> none  [gather_forward(): gathered = lax.all_gather(stacked, 'seq', axis=1, tiled=True)]
    ppermute x24 -> x0, waiting for transfers between devices: 54.2 us -> none  [swapped(): return lax.ppermute(block, axis, route)]
    pallas_call x0 -> x5, Pallas kernels: none -> 38.3 us  [call(): pl.pallas_call(kernel, out_shape=out_shape, in_specs=specs, out_specs=jax...]
    broadcast_in_dim x37 -> x0, local copies, waits for them, and re-layouts: 36.6 us -> none  [place_rows(): jnp.where(chosen[None, :, :, None], tensor[:, None], jnp.zeros((), tensor...]
    ppermute x24 -> x0, starting transfers between devices: 36.2 us -> none  [swapped(): return lax.ppermute(block, axis, route)]
  transfers between devices with their start and end apart: 25 -> 1, of which waited for: 10 -> 1; matrix products, arithmetic and copies ran while one was open for 43% -> 1% of each run, Pallas kernels for 0% -> 0%
where the time goes in v1:
time: 146 us; the launch traced here: 145 us
  blocking collectives  76.4 us (52%)
  Pallas kernels  38.3 us (26%)
  waiting for transfers between devices  21 us (14%)
  starting transfers between devices  7.17 us (5%)
    pallas_call x5, Pallas kernels, call(): pl.pallas_call(kernel, out_shape=out_shape, in_specs=specs, out_specs=jax...  38.3 us
    all_to_all x1, blocking collectives, per_device(): out = lax.all_to_all(back, INSIDE, 0, 0, tiled=True)  28.9 us
    all_to_all x1, blocking collectives, per_device(): qg_all = lax.all_to_all(far, ACROSS, 0, 0, tiled=True)  23.8 us
    all_to_all x1, blocking collectives, per_device(): kv_all = lax.all_to_all(kv_far, ACROSS, 0, 0, tiled=True)  23.7 us
    all_to_all x1, waiting for transfers between devices, per_device(): r = lax.all_to_all(packed, INSIDE, 0, 0, tiled=True)  21 us
    all_to_all x1, starting transfers between devices, per_device(): r = lax.all_to_all(packed, INSIDE, 0, 0, tiled=True)  7.17 us
  transfers between devices with their start and end apart: 1, of which 1 were waited for; matrix products, arithmetic and copies ran while one was open for 1% of the time, Pallas kernels for 0%

profile of v1, /device:TPU:1, one launch (start us, length us, event | category | flops | bytes accessed | tf_op | source)
XLA Modules:
  0.0 145.4 jit_solution(10760839007968901745)
XLA Ops:
  0.6 0.0 copy-start
  0.6 3.0 %shard_map.84 = bf16[16,192,256]{2,1,0:T(8,128)(2,1)} custom-call(bf16[256,768]{1,0:T(8,128)(2,1)} %k_ref.1, bf16[256,768]{1,0:T(8,128)(2,1)} %v_ref.1, bf16[256,768]{1,0:T(8,128)(2,1)} %q_ref.1, bf16[256,768]{1,0:T(8,128)(2,1)} %g_ref.1), custom_call_target="tpu_custom_call" | custom-call | tf_op jit(solution)/shard_map/pallas_call | solution.py:41
  3.6 7.2 %all-to-all-start = ((bf16[16,192,256]{2,1,0:T(8,128)(2,1)}), bf16[16,192,256]{2,1,0:T(8,128)(2,1)S(1)}, u32[]{:S(2)}, u32[]{:S(2)}) async-start(bf16[16,192,256]{2,1,0:T(8,128)(2,1)} %shard_map.84), calls=%async_computation | async-start | bytes 3145728 | tf_op jit(solution)/shard_map/all_to_all | solution.py:296
  10.8 0.0 copy-done
  10.8 0.2 dynamic-slice_reduce_fusion
  11.0 0.6 pad_add_fusion.off_ref
  11.6 21.0 %all-to-all-done.r_ref = bf16[16,192,256]{2,1,0:T(8,128)(2,1)S(1)} async-done(((bf16[16,192,256]{2,1,0:T(8,128)(2,1)}), bf16[16,192,256]{2,1,0:T(8,128)(2,1)S(1)}, u32[]{:S(2)}, u32[]{:S(2)}) %all-to-all-start) | async-done | bytes 1572896 | tf_op jit(solution)/shard_map/all_to_all | solution.py:296
  32.6 0.0 copy-start.1
  32.6 1.2 copy-done.1
  33.8 2.8 %shard_map.85 = (bf16[512,96]{1,0:T(8,128)(2,1)}, bf16[512,96]{1,0:T(8,128)(2,1)}, bf16[16,80,96]{2,1,0:T(8,128)(2,1)}, bf16[80,96]{1,0:T(8,128)(2,1)}) custom-call(s32[4]{0:T(128)} %pad_add_fusion.off_ref, bf16[16,192,256]{2,1,0:T(8,128)(2,1)} %copy-done.1), custom_call_target="tpu_custom_call" | custom-call | tf_op jit(solution)/shard_map/pallas_call | solution.py:41
  36.6 23.7 %all_to_all.20.kv_all_ref = bf16[16,80,96]{2,1,0:T(8,128)(2,1)} all-to-all(bf16[16,80,96]{2,1,0:T(8,128)(2,1)} %get-tuple-element.14.kv_far_ref), channel_id=1, replica_groups=mesh['y'=4,'z_high'=4,'z_low'=2,'x'=4,'core'=2] {'y','z_high'}, dimensions={0} | all-to-all | bytes 491520 | tf_op jit(solution)/shard_map/all_to_all | solution.py:308
  60.3 15.0 %shard_map.86 = (bf16[16,48,256]{2,1,0:T(8,128)(2,1)}, f32[16,8,256]{2,1,0:T(8,128)}, f32[8,512]{1,0:T(8,128)}, f32[16,80,128]{2,1,0:T(8,128)}) custom-call(s32[4]{0:T(128)} %pad_add_fusion.off_ref, bf16[16,192,256]{2,1,0:T(8,128)(2,1)} %copy-done.1, bf16[512,96]{1,0:T(8,128)(2,1)} %get-tuple-element.12.kv2_ref, bf16[512,96]{1,0:T(8,128)(2,1)} %get-tuple-element.13.qg2_ref, ...), custom_call_target="tpu_custom_call" | custom-call | tf_op jit(solution)/shard_map/pallas_call | solution.py:41
  75.3 23.8 %all_to_all.21.qg_all_ref = f32[16,80,128]{2,1,0:T(8,128)} all-to-all(f32[16,80,128]{2,1,0:T(8,128)} %get-tuple-element.16.own_far_ref), channel_id=1, replica_groups=mesh['y'=4,'z_high'=4,'z_low'=2,'x'=4,'core'=2] {'y','z_high'}, dimensions={0} | all-to-all | bytes 1310720 | tf_op jit(solution)/shard_map/all_to_all | solution.py:321
  99.1 14.7 %shard_map.87 = bf16[16,192,256]{2,1,0:T(8,128)(2,1)} custom-call(s32[4]{0:T(128)} %pad_add_fusion.off_ref, bf16[16,192,256]{2,1,0:T(8,128)(2,1)} %copy-done.1, bf16[512,96]{1,0:T(8,128)(2,1)} %get-tuple-element.12.kv2_ref, bf16[512,96]{1,0:T(8,128)(2,1)} %get-tuple-element.13.qg2_ref, bf16[16,80,96]{2,1,0:T(8,128)(2,1)} %all_to_all.20.kv_all_ref, ...), custom_call_target="tpu_custom_call" | custom-call | tf_op jit(solution)/shard_map/pallas_call | solution.py:41
  113.8 28.9 %all_to_all.22.in_ref = bf16[16,192,256]{2,1,0:T(8,128)(2,1)} all-to-all(bf16[16,192,256]{2,1,0:T(8,128)(2,1)} %shard_map.87), channel_id=1, replica_groups=mesh['y'=4,'z_high'=4,'z_low'=2,'x'=4,'core'=2] {'z_low','x','core'}, dimensions={0} | all-to-all | bytes 3145728 | tf_op jit(solution)/shard_map/all_to_all | solution.py:329
  142.7 2.7 %shard_map.88 = (bf16[256,768]{1,0:T(8,128)(2,1)}, bf16[256,768]{1,0:T(8,128)(2,1)}, bf16[256,768]{1,0:T(8,128)(2,1)}, bf16[256,768]{1,0:T(8,128)(2,1)}) custom-call(bf16[16,192,256]{2,1,0:T(8,128)(2,1)} %all_to_all.22.in_ref), custom_call_target="tpu_custom_call" | custom-call | tf_op jit(solution)/shard_map/pallas_call | solution.py:41
Async XLA Ops:
  0.6 10.2 %copy-start = (s32[3,16]{1,0:T(4,128)S(1)}, s32[3,16]{1,0:T(4,128)}, u32[]{:S(2)}) copy-start(s32[3,16]{1,0:T(4,128)} %param.9) | copy-start | bytes 580
  3.6 29.0 %all-to-all-start = ((bf16[16,192,256]{2,1,0:T(8,128)(2,1)}), bf16[16,192,256]{2,1,0:T(8,128)(2,1)S(1)}, u32[]{:S(2)}, u32[]{:S(2)}) async-start(bf16[16,192,256]{2,1,0:T(8,128)(2,1)} %shard_map.84), calls=%async_computation | async-start | bytes 3145728 | tf_op jit(solution)/shard_map/all_to_all | solution.py:296
  32.6 1.2 copy-start.1

commit v2 on v1

v2 whole, which is shorter than its diff:
```python
import math

import jax
import jax.numpy as jnp
from jax import lax
from jax.experimental import pallas as pl
from jax.experimental.pallas import tpu as pltpu
from jax.sharding import Mesh, PartitionSpec as P

HEADS = 16
WIDTH = 48
ROWS = 256
GROUP = 16
GROUP_ROWS = GROUP * ROWS
STRIDES = (8, 64, 256)
PICK_TWO = GROUP_ROWS // 8
PICK_THREE = GROUP_ROWS // 64
PICK_FOUR = GROUP_ROWS // 256
PICK_FAR = PICK_THREE + PICK_FOUR
FACTOR = WIDTH**-0.5
EXPONENT = FACTOR * math.log2(math.e)
BF16 = jnp.bfloat16
F32 = jnp.float32
LIMIT = 56 * 1024 * 1024

INSIDE = ("z_low", "x", "core")
ACROSS = ("y", "z_high")


def dot(a, b):
    return lax.dot_general(a, b, (((1,), (0,)), ((), ())), preferred_element_type=F32)


def dot_t(a, b):
    return lax.dot_general(a, b, (((1,), (1,)), ((), ())), preferred_element_type=F32)


def call(kernel, out_shape, scratch=(), smem=0, args=()):
    vmem = pl.BlockSpec(memory_space=pltpu.VMEM)
    specs = [pl.BlockSpec(memory_space=pltpu.SMEM)] * smem + [vmem] * (len(args) - smem)
    return pl.pallas_call(
        kernel,
        out_shape=out_shape,
        in_specs=specs,
        out_specs=jax.tree.map(lambda _: vmem, out_shape),
        scratch_shapes=list(scratch),
        compiler_params=pltpu.CompilerParams(vmem_limit_bytes=LIMIT),
    )(*args)


def pack_kernel(k_ref, v_ref, q_ref, g_ref, out_ref):
    for place, ref in enumerate((k_ref, v_ref, q_ref, g_ref)):
        turned = ref[...].T
        out_ref[:, place * WIDTH : (place + 1) * WIDTH, :] = turned.reshape(HEADS, WIDTH, ROWS)


def unpack_kernel(in_ref, a_ref, q_ref, k_ref, v_ref):
    for place, ref in enumerate((a_ref, q_ref, k_ref, v_ref)):
        block = in_ref[:, place * WIDTH : (place + 1) * WIDTH, :].reshape(HEADS * WIDTH, ROWS)
        ref[...] = block.T


def far_choice(o3, o4, s):
    row = lax.broadcasted_iota(jnp.int32, (PICK_FAR, ROWS), 0)
    col = lax.broadcasted_iota(jnp.int32, (PICK_FAR, ROWS), 1)
    four = row - PICK_THREE
    is_three = four < 0
    target = jnp.where(is_three, 64 * (row & 3) + o3, o4)
    source = jnp.where(is_three, row >> 2, four)
    hit = jnp.logical_and(col == target, source == s)
    return jnp.where(hit, 1.0, 0.0).astype(BF16)


def two_choice(o2):
    row = lax.broadcasted_iota(jnp.int32, (ROWS // 8, ROWS), 0)
    col = lax.broadcasted_iota(jnp.int32, (ROWS // 8, ROWS), 1)
    return jnp.where(col == 8 * row + o2, 1.0, 0.0).astype(BF16)


def upper(q_t):
    return jnp.concatenate([q_t, jnp.zeros_like(q_t)], axis=0)


def lower(g_t):
    return jnp.concatenate([jnp.zeros_like(g_t), g_t], axis=0)


def forward_units(blocks):
    scores = [dot(kv, upper(q_t)) for kv, _, q_t in blocks]
    weights = [jnp.exp2(score * EXPONENT) for score in scores]
    sums = [jnp.sum(weight, axis=0, keepdims=True) for weight in weights]
    low = [(weight * (1.0 / (total * 0.25))).astype(BF16) for weight, total in zip(weights, sums)]
    outputs = [dot(block[1], probs) * 0.25 for block, probs in zip(blocks, low)]
    return [(output * total, total) for output, total in zip(outputs, sums)]


def forward_unit(kv, v_t, q_t):
    return forward_units([(kv, v_t, q_t)])[0]


def to_rows(numerator, sums):
    queries = numerator.shape[1]
    block = jnp.concatenate(
        [numerator, jnp.broadcast_to(sums, (80, queries))], axis=0
    )
    return block.T


def backward_units(blocks):
    scores = [dot(block[0], upper(block[1])) for block in blocks]
    probs = [dot(block[0], lower(block[2])) for block in blocks]
    shares = [jnp.exp2(score * EXPONENT) * block[3] for score, block in zip(scores, blocks)]
    grads = [(share * (prob - block[4])).astype(BF16) for share, prob, block in zip(shares, probs, blocks)]
    return [(share.astype(BF16), grad) for share, grad in zip(shares, grads)]


def backward_unit(kv, q_t, g_t, inverse, dots):
    return backward_units([(kv, q_t, g_t, inverse, dots)])[0]


def pair(ref, seg, low, high):
    return jnp.concatenate([ref[2 * seg, low:high, :], ref[2 * seg + 1, low:high, :]], axis=1)


def turn(x):
    return x.T


FAR_LANES = 256
TD = 4 * WIDTH


def thirds(x):
    high = x.astype(BF16).astype(F32)
    rest = x - high
    middle = rest.astype(BF16).astype(F32)
    return high, middle, rest - middle


def near_forward_kernel(off_ref, r_ref, acc_ref, kv2_ref, qg2_ref, far_ref):
    o2, o3, o4 = off_ref[0], off_ref[1], off_ref[2]
    count = ROWS // 8
    two = two_choice(o2)
    for s in range(GROUP):
        kv2_ref[s * count : (s + 1) * count, :] = dot_t(two, r_ref[s, : 2 * WIDTH, :]).astype(BF16)
        qg2_ref[s * count : (s + 1) * count, :] = dot_t(two, r_ref[s, 2 * WIDTH :, :]).astype(BF16)
    picked = jnp.zeros((PICK_FAR, 4 * WIDTH), F32)
    for s in range(GROUP):
        picked = picked + dot_t(far_choice(o3, o4, s), r_ref[s])

    def segments(step, carry):
        blocks = []
        for j in range(4):
            seg = 4 * step + j
            kv_t = pair(r_ref, seg, 0, 2 * WIDTH)
            blocks.append((turn(kv_t), kv_t[WIDTH:], pair(r_ref, seg, 2 * WIDTH, 3 * WIDTH)))
        for j, (numerator, sums) in enumerate(forward_units(blocks)):
            start = pl.multiple_of((4 * step + j) * 512, 512)
            acc_ref[pl.ds(start, 512), :] = to_rows(numerator, sums)
        return carry

    lax.fori_loop(0, 2, segments, 0)

    kv2 = kv2_ref[...]
    numerator, sums = forward_unit(kv2, turn(kv2)[WIDTH:], turn(qg2_ref[...])[:WIDTH])
    rows = pl.ds(o2, PICK_TWO, stride=8)
    acc_ref[rows, :] = acc_ref[rows, :] + to_rows(numerator, sums)

    base = jnp.concatenate(
        [acc_ref[pl.ds(o3, PICK_THREE, stride=64), :], acc_ref[pl.ds(o4, PICK_FOUR, stride=256), :]], axis=0
    )
    total = base[:, WIDTH : WIDTH + 1]
    merged = base[:, :WIDTH] / total
    dots = jnp.sum(picked[:, 3 * WIDTH :] * merged, axis=1, keepdims=True)
    large, small = total > 2.0**60, total < 2.0**-60
    level = jnp.where(large, 2.0**64, jnp.where(small, 2.0**-64, 1.0))
    unlevel = jnp.where(large, 2.0**-64, jnp.where(small, 2.0**64, 1.0))
    block = jnp.concatenate([picked, jnp.zeros((PICK_FAR, FAR_LANES - TD), F32)], axis=1)
    lane = lax.broadcasted_iota(jnp.int32, block.shape, 1)
    for place, column in enumerate((*thirds(total * unlevel), level, *thirds(dots))):
        block = jnp.where(lane == TD + place, column, block)
    low = block.astype(BF16)
    for s in range(GROUP):
        far_ref[s] = low


def near_sums(far_t):
    td = far_t[TD : TD + 8].astype(F32)
    return (td[0:1] + td[1:2] + td[2:3]) * td[3:4], td[4:5] + td[5:6] + td[6:7]


def pick(grad_part, value_part):
    lane = lax.broadcasted_iota(jnp.int32, grad_part.shape, 1)
    return jnp.where(lane < WIDTH, grad_part * (FACTOR * 0.25), value_part * 0.25)


def widen(x):
    return jnp.concatenate([x, jnp.zeros((x.shape[0], 128 - x.shape[1]), F32)], axis=1)


def query_rows(part_t):
    part_t = part_t * (FACTOR * 0.25)
    return jnp.concatenate([part_t, jnp.zeros((128 - WIDTH, part_t.shape[1]), F32)], axis=0).T


def far_rows(numerator, sums, g_t):
    count = numerator.shape[1]
    lined = jnp.sum(g_t.astype(F32) * numerator, axis=0, keepdims=True)
    block = jnp.concatenate(
        [numerator, jnp.broadcast_to(sums, (8, count)), jnp.broadcast_to(lined, (72, count))], axis=0
    )
    return block.T


def far_units(stacks):
    blocks = []
    turned = []
    for far in stacks:
        far_t = turn(far)
        turned.append(far_t)
        blocks.append((far[:, : 2 * WIDTH], far_t[WIDTH : 2 * WIDTH], far_t[2 * WIDTH : 3 * WIDTH]))
    results = forward_units(blocks)
    return turned, [far_rows(*result, far_t[3 * WIDTH : TD]) for result, far_t in zip(results, turned)]


def totals_of(far_t, rows):
    near_total, near_dots = near_sums(far_t)
    far = rows.T
    total = near_total + far[WIDTH : WIDTH + 1]
    return 1.0 / (total * 0.25), (near_dots * near_total + far[WIDTH + 8 : WIDTH + 9]) / total


def backward_kernel(
    off_ref, r_ref, kv2_ref, qg2_ref, acc_in_ref, all_ref,
    out_ref, acc_ref, td_ref, accq_ref, acckv_ref, three_ref, four_ref,
):
    o2, o3, o4, across = off_ref[0], off_ref[1], off_ref[2], off_ref[3]
    half = across // 8
    meet = (o4 & 63) == o3
    rows2 = pl.ds(o2, PICK_TWO, stride=8)
    rows3 = pl.ds(o3, PICK_THREE, stride=64)
    rows4 = pl.ds(o4, PICK_FOUR, stride=256)
    own_rows3 = pl.ds(pl.multiple_of(across * PICK_THREE, PICK_THREE), PICK_THREE)
    own_rows4 = pl.ds(pl.multiple_of(across * PICK_FOUR, PICK_FOUR), PICK_FOUR)
    half_rows = pl.ds(pl.multiple_of(half * 512, 512), 512)

    acc_ref[...] = acc_in_ref[...]

    def stack_three(which):
        return jnp.concatenate([all_ref[which * 8 + j, :PICK_THREE, :] for j in range(8)], axis=0)

    far3 = stack_three(half)
    far4 = jnp.concatenate([all_ref[j, PICK_THREE:, :] for j in range(GROUP)], axis=0)
    (far3_t, far4_t), (block3, block4) = far_units((far3, far4))
    three_ref[half_rows, :] = block3
    four_ref[...] = block4

    @pl.when(meet)
    def _():
        other = 1 - half
        three_ref[pl.ds(pl.multiple_of(other * 512, 512), 512), :] = far_units((stack_three(other),))[1][0]
        same = pl.ds(o4 >> 6, 256, stride=4)
        both = three_ref[same, :] + four_ref[...]
        three_ref[same, :] = both
        four_ref[...] = both

    acc_ref[rows3, :] = acc_ref[rows3, :] + three_ref[own_rows3, :]
    acc_ref[rows4, :] = acc_ref[rows4, :] + jnp.where(meet, 0.0, four_ref[own_rows4, :])
    inverse3, dots3 = totals_of(far3_t, three_ref[half_rows, :])
    inverse4, dots4 = totals_of(far4_t, four_ref[...])

    def near_totals(block, g_t):
        total = block[WIDTH : WIDTH + 1]
        merged = block[:WIDTH] / total
        dots = jnp.sum(g_t.astype(F32) * merged, axis=0, keepdims=True)
        return merged, 1.0 / (total * 0.25), dots

    def finish(s, carry):
        rows = pl.ds(pl.multiple_of(s * ROWS, ROWS), ROWS)
        merged, inverse, dots = near_totals(acc_ref[rows, :].T, r_ref[s, 3 * WIDTH :, :])
        out_ref[s, :WIDTH, :] = merged.astype(BF16)
        td_ref[s] = jnp.concatenate([inverse, dots, jnp.zeros((6, ROWS), F32)], axis=0)
        return carry

    lax.fori_loop(0, GROUP, finish, 0, unroll=4)

    def segments(step, carry):
        blocks = []
        turned = []
        for j in range(2):
            seg = 2 * step + j
            kv_t = pair(r_ref, seg, 0, 2 * WIDTH)
            qg_t = pair(r_ref, seg, 2 * WIDTH, 4 * WIDTH)
            td = pair(td_ref, seg, 0, 8)
            blocks.append((turn(kv_t), qg_t[:WIDTH], qg_t[WIDTH:], td[0:1], td[1:2]))
            turned.append((kv_t[:WIDTH], turn(qg_t)))
        results = backward_units(blocks)
        query_parts = [dot(keys, grad) for (keys, _), (_, grad) in zip(turned, results)]
        grad_parts = [dot(grad, qg) for (_, qg), (_, grad) in zip(turned, results)]
        value_parts = [dot(share, qg) for (_, qg), (share, _) in zip(turned, results)]
        for j in range(2):
            rows = pl.ds(pl.multiple_of((2 * step + j) * 512, 512), 512)
            accq_ref[rows, :] = query_rows(query_parts[j])
            acckv_ref[rows, :] = widen(pick(grad_parts[j], value_parts[j]))
        return carry

    lax.fori_loop(0, 4, segments, 0)

    qg2 = qg2_ref[...]
    kv2 = kv2_ref[...]
    qg2_t = turn(qg2)
    _, inverse2, dots2 = near_totals(acc_ref[rows2, :].T, qg2_t[WIDTH:])
    own = jnp.concatenate(
        [all_ref[across], jnp.zeros((128 - PICK_FAR, FAR_LANES), BF16)], axis=0
    )
    own_t = turn(own)
    own_block = jnp.concatenate(
        [three_ref[own_rows3, :], four_ref[own_rows4, :], jnp.zeros((128 - PICK_FAR, 128), F32)], axis=0
    )
    own_total, own_lined = near_sums(own_t)
    own_block = own_block.T
    own_lined = own_lined * own_total + own_block[WIDTH + 8 : WIDTH + 9]
    own_total = own_total + own_block[WIDTH : WIDTH + 1]
    own_total = jnp.where(own_total > 0.0, own_total, 1.0)
    own_inverse = 1.0 / (own_total * 0.25)
    own_dots = own_lined / own_total
    own_q, own_g = own_t[2 * WIDTH : 3 * WIDTH], own_t[3 * WIDTH : TD]
    kv_own = own[:, : 2 * WIDTH]
    qg3 = far3[:, 2 * WIDTH : TD]
    qg4 = far4[:, 2 * WIDTH : TD]
    results = backward_units((
        (kv2, qg2_t[:WIDTH], qg2_t[WIDTH:], inverse2, dots2),
        (far3[:, : 2 * WIDTH], own_q, own_g, own_inverse, own_dots),
        (far4[:, : 2 * WIDTH], own_q, own_g, own_inverse, own_dots),
        (kv_own, far3_t[2 * WIDTH : 3 * WIDTH], far3_t[3 * WIDTH : TD], inverse3, dots3),
        (kv_own, far4_t[2 * WIDTH : 3 * WIDTH], far4_t[3 * WIDTH : TD], inverse4, dots4),
    ))
    query2 = query_rows(dot(turn(kv2)[:WIDTH], results[0][1]))
    query3 = query_rows(dot(far3_t[:WIDTH], results[1][1]))
    query4 = query_rows(dot(far4_t[:WIDTH], results[2][1]))
    keys2 = widen(pick(dot(results[0][1], qg2), dot(results[0][0], qg2)))
    keys3 = widen(pick(dot(results[3][1], qg3), dot(results[3][0], qg3)))
    keys4 = widen(pick(dot(results[4][1], qg4), dot(results[4][0], qg4)))
    far_end = PICK_THREE + PICK_FOUR
    for ref, part2, part3, part4 in ((accq_ref, query2, query3, query4), (acckv_ref, keys2, keys3, keys4)):
        ref[rows2, :] = ref[rows2, :] + part2
        ref[rows3, :] = ref[rows3, :] + part3[:PICK_THREE]
        ref[rows4, :] = ref[rows4, :] + part4[PICK_THREE:far_end]

    def leave(s, carry):
        rows = pl.ds(pl.multiple_of(s * ROWS, ROWS), ROWS)
        out_ref[s, WIDTH : 2 * WIDTH, :] = accq_ref[rows, :].astype(BF16).T[:WIDTH]
        out_ref[s, 2 * WIDTH :, :] = acckv_ref[rows, :].astype(BF16).T[: 2 * WIDTH]
        return carry

    lax.fori_loop(0, GROUP, leave, 0, unroll=4)


def per_device(queries, key_states, value_states, cotangent, offsets):
    struct = jax.ShapeDtypeStruct
    head = lax.axis_index(INSIDE)
    across = lax.axis_index(ACROSS)
    own = lax.dynamic_slice(offsets, (0, head), (3, 1))[:, 0]
    scalars = jnp.concatenate([own, across.astype(jnp.int32)[None]])
    scalars, key_states = lax.optimization_barrier((scalars, key_states))

    packed = call(
        pack_kernel, struct((HEADS, 4 * WIDTH, ROWS), BF16), args=(key_states, value_states, queries, cotangent)
    )
    r = lax.all_to_all(packed, INSIDE, 0, 0, tiled=True)
    rows_f32 = struct((GROUP_ROWS, 128), F32)
    scratch = pltpu.VMEM((GROUP_ROWS, 128), F32)
    picked_two = struct((PICK_TWO, 2 * WIDTH), BF16)
    acc, kv2, qg2, far = call(
        near_forward_kernel,
        (rows_f32, picked_two, picked_two, struct((GROUP, PICK_FAR, FAR_LANES), BF16)),
        smem=1,
        args=(scalars, r),
    )
    far_all = lax.all_to_all(far, ACROSS, 0, 0, tiled=True)
    back = call(
        backward_kernel,
        struct((GROUP, 4 * WIDTH, ROWS), BF16),
        scratch=(
            scratch,
            pltpu.VMEM((GROUP, 8, ROWS), F32),
            scratch,
            scratch,
            pltpu.VMEM((1024, 128), F32),
            pltpu.VMEM((256, 128), F32),
        ),
        smem=1,
        args=(scalars, r, kv2, qg2, acc, far_all),
    )
    out = lax.all_to_all(back, INSIDE, 0, 0, tiled=True)
    shape = struct((ROWS, HEADS * WIDTH), BF16)
    return tuple(call(unpack_kernel, (shape,) * 4, args=(out,)))


def solution(mesh):
    axes = ("y", "z_high", "z_low", "x", "core")
    inner = Mesh(mesh.devices.reshape(4, 4, 2, 4, 2), axes)
    rows = P(axes, None)
    return jax.shard_map(
        per_device,
        mesh=inner,
        in_specs=(rows, rows, rows, rows, P()),
        out_specs=(rows, rows, rows, rows),
        check_vma=False,
    )
```

time: 146 us -> 116 us (0.79)
  waiting for transfers between devices: 21 us -> 0 us
  Pallas kernels: 38.3 us -> 26.6 us
  blocking collectives: 76.4 us -> 86.5 us
  starting transfers between devices: 7.17 us -> 0 us
    all_to_all x1 -> x0, waiting for transfers between devices: 21 us -> none  [per_device(): r = lax.all_to_all(packed, INSIDE, 0, 0, tiled=True)]
    pallas_call x5 -> x4, Pallas kernels: 38.3 us -> 26.6 us  [call(): pl.pallas_call(kernel, out_shape=out_shape, in_specs=specs, out_specs=jax...]
    all_to_all x2, blocking collectives: 47.5 us -> 57.7 us  [the longest x1 29.1 us: per_device(): far_all = lax.all_to_all(far, ACROSS, 0, 0, tiled=True)]
    all_to_all x1 -> x0, starting transfers between devices: 7.17 us -> none  [per_device(): r = lax.all_to_all(packed, INSIDE, 0, 0, tiled=True)]
  transfers between devices with their start and end apart: 1 -> 0, of which waited for: 1 -> 0; matrix products, arithmetic and copies ran while one was open for 1% -> 0% of each run, Pallas kernels for 0% -> 0%
where the time goes in v2:
time: 116 us; the launch traced here: 115 us
  blocking collectives  86.5 us (75%)
  Pallas kernels  26.6 us (23%)
    all_to_all x1, blocking collectives, per_device(): far_all = lax.all_to_all(far, ACROSS, 0, 0, tiled=True)  29.1 us
    all_to_all x1, blocking collectives, per_device(): out = lax.all_to_all(back, INSIDE, 0, 0, tiled=True)  28.8 us
    all_to_all x1, blocking collectives, per_device(): r = lax.all_to_all(packed, INSIDE, 0, 0, tiled=True)  28.6 us
    pallas_call x4, Pallas kernels, call(): pl.pallas_call(kernel, out_shape=out_shape, in_specs=specs, out_specs=jax...  26.6 us

profile of v2, /device:TPU:1, one launch (start us, length us, event | category | flops | bytes accessed | tf_op | source)
XLA Modules:
  0.0 115.2 jit_solution(8309259762370804072)
XLA Ops:
  0.6 0.0 copy-start
  0.7 0.7 copy-done
  1.3 0.2 dynamic-slice_reduce_fusion
  1.5 0.6 pad_add_fusion.off_ref
  2.1 3.0 %shard_map.84 = bf16[16,192,256]{2,1,0:T(8,128)(2,1)} custom-call(bf16[256,768]{1,0:T(8,128)(2,1)} %k_ref, bf16[256,768]{1,0:T(8,128)(2,1)} %v_ref.1, bf16[256,768]{1,0:T(8,128)(2,1)} %q_ref.1, bf16[256,768]{1,0:T(8,128)(2,1)} %g_ref.1), custom_call_target="tpu_custom_call" | custom-call | tf_op jit(solution)/shard_map/pallas_call | solution.py:41
  5.1 28.6 %all_to_all.15.r_ref = bf16[16,192,256]{2,1,0:T(8,128)(2,1)} all-to-all(bf16[16,192,256]{2,1,0:T(8,128)(2,1)} %shard_map.84), channel_id=1, replica_groups=mesh['y'=4,'z_high'=4,'z_low'=2,'x'=4,'core'=2] {'z_low','x','core'}, dimensions={0} | all-to-all | bytes 3145728 | tf_op jit(solution)/shard_map/all_to_all | solution.py:370
  33.6 7.3 %shard_map.85 = (f32[4096,128]{1,0:T(8,128)}, bf16[512,96]{1,0:T(8,128)(2,1)}, bf16[512,96]{1,0:T(8,128)(2,1)}, bf16[16,80,256]{2,1,0:T(8,128)(2,1)}) custom-call(s32[4]{0:T(128)} %pad_add_fusion.off_ref, bf16[16,192,256]{2,1,0:T(8,128)(2,1)} %all_to_all.15.r_ref), custom_call_target="tpu_custom_call" | custom-call | tf_op jit(solution)/shard_map/pallas_call | solution.py:41
  41.0 29.1 %all_to_all.16.all_ref = bf16[16,80,256]{2,1,0:T(8,128)(2,1)} all-to-all(bf16[16,80,256]{2,1,0:T(8,128)(2,1)} %get-tuple-element.15), channel_id=1, replica_groups=mesh['y'=4,'z_high'=4,'z_low'=2,'x'=4,'core'=2] {'y','z_high'}, dimensions={0} | all-to-all | bytes 1310720 | tf_op jit(solution)/shard_map/all_to_all | solution.py:380
  70.1 13.6 %shard_map.86 = bf16[16,192,256]{2,1,0:T(8,128)(2,1)} custom-call(s32[4]{0:T(128)} %pad_add_fusion.off_ref, bf16[16,192,256]{2,1,0:T(8,128)(2,1)} %all_to_all.15.r_ref, bf16[512,96]{1,0:T(8,128)(2,1)} %get-tuple-element.12.kv2_ref, bf16[512,96]{1,0:T(8,128)(2,1)} %get-tuple-element.13.qg2_ref, f32[4096,128]{1,0:T(8,128)} %get-tuple-element.14.acc_in_ref, ...), custom_call_target="tpu_custom_call" | custom-call | tf_op jit(solution)/shard_map/pallas_call | solution.py:41
  83.7 28.8 %all_to_all.17.in_ref = bf16[16,192,256]{2,1,0:T(8,128)(2,1)} all-to-all(bf16[16,192,256]{2,1,0:T(8,128)(2,1)} %shard_map.86), channel_id=1, replica_groups=mesh['y'=4,'z_high'=4,'z_low'=2,'x'=4,'core'=2] {'z_low','x','core'}, dimensions={0} | all-to-all | bytes 3145728 | tf_op jit(solution)/shard_map/all_to_all | solution.py:395
  112.5 2.7 %shard_map.87 = (bf16[256,768]{1,0:T(8,128)(2,1)}, bf16[256,768]{1,0:T(8,128)(2,1)}, bf16[256,768]{1,0:T(8,128)(2,1)}, bf16[256,768]{1,0:T(8,128)(2,1)}) custom-call(bf16[16,192,256]{2,1,0:T(8,128)(2,1)} %all_to_all.17.in_ref), custom_call_target="tpu_custom_call" | custom-call | tf_op jit(solution)/shard_map/pallas_call | solution.py:41
Async XLA Ops:
  0.6 0.7 copy-start

commit v3 on v2

v3 whole, which is shorter than its diff:
```python
import math

import jax
import jax.numpy as jnp
from jax import lax
from jax.experimental import pallas as pl
from jax.experimental.pallas import tpu as pltpu
from jax.sharding import Mesh, PartitionSpec as P

HEADS = 16
WIDTH = 48
ROWS = 256
OWN = 8
GROUP_ROWS = 16 * ROWS
PICK_TWO = GROUP_ROWS // 8
PICK_THREE = GROUP_ROWS // 64
PICK_FOUR = GROUP_ROWS // 256
PICK_FAR = PICK_THREE + PICK_FOUR
FACTOR = WIDTH**-0.5
EXPONENT = FACTOR * math.log2(math.e)
BF16 = jnp.bfloat16
F32 = jnp.float32
LIMIT = 56 * 1024 * 1024

CHIPS = ("z_low", "x")
HALF = ("y_low", "z_high")


def dot(a, b):
    return lax.dot_general(a, b, (((1,), (0,)), ((), ())), preferred_element_type=F32)


def dot_t(a, b):
    return lax.dot_general(a, b, (((1,), (1,)), ((), ())), preferred_element_type=F32)


def call(kernel, out_shape, scratch=(), smem=0, args=(), steps=0):
    smem_spec = pl.BlockSpec(memory_space=pltpu.SMEM)

    def spec(array):
        if not steps:
            return pl.BlockSpec(memory_space=pltpu.VMEM)
        rest = array.shape[1:]
        return pl.BlockSpec((array.shape[0] // steps, *rest), lambda i: (i,) + (0,) * len(rest))

    return pl.pallas_call(
        kernel,
        out_shape=out_shape,
        grid=(steps,) if steps else (),
        in_specs=[smem_spec] * smem + [spec(array) for array in args[smem:]],
        out_specs=jax.tree.map(spec, out_shape),
        scratch_shapes=list(scratch),
        compiler_params=pltpu.CompilerParams(vmem_limit_bytes=LIMIT),
    )(*args)


def pack_kernel(k_ref, v_ref, q_ref, g_ref, keep_ref, send_ref):
    parts = []
    for ref in (k_ref, v_ref, q_ref, g_ref):
        turned = ref[...].T
        middle = OWN * WIDTH
        parts.append([turned[:middle].reshape(OWN, WIDTH, ROWS), turned[middle:].reshape(OWN, WIDTH, ROWS)])

    def store(low_ref, high_ref):
        for place, (low, high) in enumerate(parts):
            span = slice(place * WIDTH, (place + 1) * WIDTH)
            low_ref[:, span, :] = low
            high_ref[:, span, :] = high

    @pl.when(lax.axis_index("core") == 0)
    def _():
        store(keep_ref, send_ref)

    @pl.when(lax.axis_index("core") == 1)
    def _():
        store(send_ref, keep_ref)


def unpack_kernel(keep_ref, came_ref, a_ref, q_ref, k_ref, v_ref):
    def store(low_ref, high_ref):
        for place, ref in enumerate((a_ref, q_ref, k_ref, v_ref)):
            span = slice(place * WIDTH, (place + 1) * WIDTH)
            low = low_ref[:, span, :].reshape(OWN * WIDTH, ROWS)
            high = high_ref[:, span, :].reshape(OWN * WIDTH, ROWS)
            ref[...] = jnp.concatenate([low, high], axis=0).T

    @pl.when(lax.axis_index("core") == 0)
    def _():
        store(keep_ref, came_ref)

    @pl.when(lax.axis_index("core") == 1)
    def _():
        store(came_ref, keep_ref)


def upper(q_t):
    return jnp.concatenate([q_t, jnp.zeros_like(q_t)], axis=0)


def lower(g_t):
    return jnp.concatenate([jnp.zeros_like(g_t), g_t], axis=0)


def forward_units(blocks):
    scores = [dot(kv, upper(q_t)) for kv, _, q_t in blocks]
    weights = [jnp.exp2(score * EXPONENT) for score in scores]
    sums = [jnp.sum(weight, axis=0, keepdims=True) for weight in weights]
    low = [(weight * (1.0 / (total * 0.25))).astype(BF16) for weight, total in zip(weights, sums)]
    outputs = [dot(block[1], probs) * 0.25 for block, probs in zip(blocks, low)]
    return [(output * total, total) for output, total in zip(outputs, sums)]


def forward_unit(kv, v_t, q_t):
    return forward_units([(kv, v_t, q_t)])[0]


def backward_units(blocks):
    scores = [dot(block[0], upper(block[1])) for block in blocks]
    probs = [dot(block[0], lower(block[2])) for block in blocks]
    shares = [jnp.exp2(score * EXPONENT) * block[3] for score, block in zip(scores, blocks)]
    grads = [(share * (prob - block[4])).astype(BF16) for share, prob, block in zip(shares, probs, blocks)]
    return [(share.astype(BF16), grad) for share, grad in zip(shares, grads)]


def backward_unit(kv, q_t, g_t, inverse, dots):
    return backward_units([(kv, q_t, g_t, inverse, dots)])[0]


def turn(x):
    return x.T


FAR_LANES = 256
TD = 4 * WIDTH
DEN = 96
LINED = 104
TAKEN = 80
SCALE = FACTOR * 0.25


def thirds(x):
    high = x.astype(BF16).astype(F32)
    rest = x - high
    middle = rest.astype(BF16).astype(F32)
    return high, middle, rest - middle


def sum_rows(numerator, sums, g_t):
    count = numerator.shape[1]
    lined = jnp.sum(g_t.astype(F32) * numerator, axis=0, keepdims=True)
    block = jnp.concatenate(
        [
            numerator,
            jnp.zeros((WIDTH, count), F32),
            jnp.broadcast_to(sums, (8, count)),
            jnp.broadcast_to(lined, (24, count)),
        ],
        axis=0,
    )
    return block.T


def query_rows(part_t):
    count = part_t.shape[1]
    return jnp.concatenate([jnp.zeros((WIDTH, count), F32), part_t * SCALE, jnp.zeros((32, count), F32)], axis=0).T


def with_sums(picked, total, dots):
    large, small = total > 2.0**60, total < 2.0**-60
    level = jnp.where(large, 2.0**64, jnp.where(small, 2.0**-64, 1.0))
    unlevel = jnp.where(large, 2.0**-64, jnp.where(small, 2.0**64, 1.0))
    lane = lax.broadcasted_iota(jnp.int32, picked.shape, 1)
    for place, column in enumerate((*thirds(total * unlevel), level, *thirds(dots))):
        picked = jnp.where(lane == TD + place, column, picked)
    return picked.astype(BF16)


def sums_beside(far):
    def column(place):
        return far[:, TD + place : TD + place + 1]

    return (column(0) + column(1) + column(2)) * column(3), column(4) + column(5) + column(6)


def near_sums(far_t):
    td = far_t[TD : TD + 8].astype(F32)
    return (td[0:1] + td[1:2] + td[2:3]) * td[3:4], td[4:5] + td[5:6] + td[6:7]


def pick(grad_part, value_part):
    lane = lax.broadcasted_iota(jnp.int32, grad_part.shape, 1)
    return jnp.where(lane < WIDTH, grad_part * SCALE, value_part * 0.25)


def widen(x):
    return jnp.concatenate([x, jnp.zeros((x.shape[0], 128 - x.shape[1]), F32)], axis=1)


def both(keep_ref, came_ref, j, low, high):
    return jnp.concatenate([keep_ref[j, low:high, :], came_ref[j, low:high, :]], axis=1)


def near_forward_kernel(off_ref, keep_ref, came_ref, acc_ref, taken_ref, base_ref):
    first = OWN * lax.axis_index("core") + 4 * pl.program_id(0)

    blocks = []
    for j in range(4):
        kv_t = both(keep_ref, came_ref, j, 0, 2 * WIDTH)
        blocks.append((turn(kv_t), kv_t[WIDTH:], both(keep_ref, came_ref, j, 2 * WIDTH, 3 * WIDTH)))
    for j, (numerator, sums) in enumerate(forward_units(blocks)):
        g_t = both(keep_ref, came_ref, j, 3 * WIDTH, TD)
        acc_ref[j * 512 : j * 512 + 512, :] = sum_rows(numerator, sums, g_t)

    row = lax.broadcasted_iota(jnp.int32, (TAKEN, 512), 0)
    col = lax.broadcasted_iota(jnp.int32, (TAKEN, 512), 1)
    is_two, is_three = row < 64, row < 72
    start = jnp.where(is_two, 8 * row, jnp.where(is_three, 64 * (row - 64), 256 * (row - 72)))
    for j in range(4):
        o2, o3, o4 = off_ref[0, first + j], off_ref[1, first + j], off_ref[2, first + j]
        base_ref[j, 64:, :] = jnp.ones((16, 128), F32)
        base_ref[j, :64, :] = acc_ref[pl.ds(j * 512 + o2, 64, stride=8), :]
        base_ref[j, 64:72, :] = acc_ref[pl.ds(j * 512 + o3, 8, stride=64), :]
        base_ref[j, 72:74, :] = acc_ref[pl.ds(j * 512 + o4, 2, stride=256), :]
        target = start + jnp.where(is_two, o2, jnp.where(is_three, o3, o4))
        hit = jnp.where(col == target, 1.0, 0.0).astype(BF16)
        picked = dot_t(hit, both(keep_ref, came_ref, j, 0, TD))
        picked = jnp.concatenate([picked, jnp.zeros((TAKEN, FAR_LANES - TD), F32)], axis=1)
        base = base_ref[j]
        total = base[:, DEN : DEN + 1]
        taken_ref[j] = with_sums(picked, total, base[:, LINED : LINED + 1] / total)


def middle_kernel(off_ref, in_ref, block2_ref, far_ref):
    head = OWN * lax.axis_index("core") + lax.axis_index(CHIPS)
    o2, o3, o4 = off_ref[0, head], off_ref[1, head], off_ref[2, head]
    two = jnp.concatenate([in_ref[s, :64, :] for s in range(OWN)], axis=0)
    two_t = turn(two)
    numerator, sums = forward_unit(two[:, : 2 * WIDTH], two_t[WIDTH : 2 * WIDTH], two_t[2 * WIDTH : 3 * WIDTH])
    block2_ref[...] = sum_rows(numerator, sums, two_t[3 * WIDTH : TD])

    rest = jnp.concatenate([in_ref[s, 64:, :] for s in range(OWN)], axis=0)
    row = lax.broadcasted_iota(jnp.int32, (PICK_FAR, 128), 0)
    col = lax.broadcasted_iota(jnp.int32, (PICK_FAR, 128), 1)
    four = row - PICK_THREE
    source = jnp.where(row < PICK_THREE, 16 * (row >> 3) + (row & 7), 16 * (four >> 1) + 8 + (four & 1))
    far = dot(jnp.where(col == source, 1.0, 0.0).astype(BF16), rest)
    total, dots = sums_beside(far)
    from2 = jnp.concatenate(
        [
            jnp.where((o3 & 7) == o2, block2_ref[pl.ds(o3 >> 3, PICK_THREE, stride=8), :], 0.0),
            jnp.where((o4 & 7) == o2, block2_ref[pl.ds(o4 >> 3, PICK_FOUR, stride=32), :], 0.0),
        ],
        axis=0,
    )
    lined = dots * total + from2[:, LINED : LINED + 1]
    total = total + from2[:, DEN : DEN + 1]
    low = with_sums(far, total, lined / total)
    for s in range(8):
        far_ref[s] = low


def far_forward(far):
    far_t = turn(far)
    result = forward_unit(far[:, : 2 * WIDTH], far_t[WIDTH : 2 * WIDTH], far_t[2 * WIDTH : 3 * WIDTH])
    return far_t, sum_rows(*result, far_t[3 * WIDTH : TD])


def three_kernel(off_ref, all_ref, block3_ref, four_ref):
    head = OWN * lax.axis_index("core") + lax.axis_index(CHIPS)
    o3, o4 = off_ref[1, head], off_ref[2, head]
    meet = (o4 & 63) == o3
    far3 = jnp.concatenate([all_ref[j, :PICK_THREE, :] for j in range(8)], axis=0)
    block3_ref[...] = far_forward(far3)[1]
    four = jnp.concatenate([all_ref[j, PICK_THREE:, :] for j in range(8)], axis=0).astype(F32)
    from3 = jnp.where(meet, block3_ref[pl.ds(o4 >> 6, 128, stride=4), :], 0.0)
    total, dots = sums_beside(four)
    lined = dots * total + from3[:, LINED : LINED + 1]
    total = total + from3[:, DEN : DEN + 1]
    four_ref[...] = with_sums(four, total, lined / total)


def totals_of(far_t, rows):
    near_total, near_dots = near_sums(far_t)
    far = rows.T
    total = near_total + far[DEN : DEN + 1]
    total = jnp.where(total > 0.0, total, 1.0)
    return 1.0 / (total * 0.25), (near_dots * near_total + far[LINED : LINED + 1]) / total


def far_kernel(
    off_ref, in_ref, block2_ref, all_ref, block3_ref, here_ref, there_ref,
    out_ref, two_ref, three_ref, four_ref,
):
    head = OWN * lax.axis_index("core") + lax.axis_index(CHIPS)
    group = lax.axis_index(HALF)
    o2, o3, o4 = off_ref[0, head], off_ref[1, head], off_ref[2, head]
    meet = (o4 & 63) == o3
    own_rows3 = pl.ds(pl.multiple_of(group * PICK_THREE, PICK_THREE), PICK_THREE)
    own_rows4 = pl.ds(pl.multiple_of(group * PICK_FOUR, PICK_FOUR), PICK_FOUR)

    far3 = jnp.concatenate([all_ref[j, :PICK_THREE, :] for j in range(8)], axis=0)
    far3_t = turn(far3)
    far4 = jnp.concatenate([here_ref[...], there_ref[...]], axis=0)
    far4_t, block4 = far_forward(far4)
    four_ref[...] = block4
    three_ref[...] = block3_ref[...]
    same = pl.ds(o4 >> 6, 128, stride=4)
    three_ref[same, :] = three_ref[same, :] + jnp.where(meet, four_ref[:128, :], 0.0)

    own3 = three_ref[own_rows3, :]
    own4 = four_ref[own_rows4, :]
    only4 = jnp.where(meet, 0.0, own4)
    two_ref[...] = block2_ref[...]
    in_two = pl.ds(o3 >> 3, PICK_THREE, stride=8)
    two_ref[in_two, :] = two_ref[in_two, :] + jnp.where((o3 & 7) == o2, own3, 0.0)
    in_two = pl.ds(o4 >> 3, PICK_FOUR, stride=32)
    two_ref[in_two, :] = two_ref[in_two, :] + jnp.where((o4 & 7) == o2, only4, 0.0)

    two = jnp.concatenate([in_ref[s, :64, :] for s in range(OWN)], axis=0)
    two_t = turn(two)
    pad = 128 - PICK_FAR
    own = jnp.concatenate(
        [all_ref[group, :PICK_THREE, :], here_ref[own_rows4, :], jnp.zeros((pad, FAR_LANES), BF16)], axis=0
    )
    own_t = turn(own)
    own_block = jnp.concatenate([own3, own4, jnp.zeros((pad, 128), F32)], axis=0)
    inverse2, dots2 = totals_of(two_t, two_ref[...])
    inverse3, dots3 = totals_of(far3_t, three_ref[...])
    inverse4, dots4 = totals_of(far4_t, four_ref[...])
    own_inverse, own_dots = totals_of(own_t, own_block)

    def queries(turned):
        return turned[2 * WIDTH : 3 * WIDTH], turned[3 * WIDTH : TD]

    kv_own = own[:, : 2 * WIDTH]
    results = backward_units((
        (two[:, : 2 * WIDTH], *queries(two_t), inverse2, dots2),
        (far3[:, : 2 * WIDTH], *queries(own_t), own_inverse, own_dots),
        (far4[:, : 2 * WIDTH], *queries(own_t), own_inverse, own_dots),
        (kv_own, *queries(far3_t), inverse3, dots3),
        (kv_own, *queries(far4_t), inverse4, dots4),
    ))
    query2 = query_rows(dot(two_t[:WIDTH], results[0][1])) + block2_ref[...]
    query3 = query_rows(dot(far3_t[:WIDTH], results[1][1]))[:PICK_THREE] + own3
    query4 = query_rows(dot(far4_t[:WIDTH], results[2][1]))[PICK_THREE:PICK_FAR] + only4

    def keys(result, far):
        qg = far[:, 2 * WIDTH : TD]
        return widen(pick(dot(result[1], qg), dot(result[0], qg)))

    keys2 = keys(results[0], two)
    keys3 = keys(results[3], far3)[:PICK_THREE]
    keys4 = keys(results[4], far4)[PICK_THREE:PICK_FAR]
    for lanes, part2, part3, part4 in (
        (slice(0, 128), keys2, keys3, keys4),
        (slice(128, 256), query2, query3, query4),
    ):
        for c in range(OWN):
            out_ref[c, :64, lanes] = part2[64 * c : 64 * c + 64]
            out_ref[c, 64:72, lanes] = part3[8 * c : 8 * c + 8]
            out_ref[c, 72:74, lanes] = part4[2 * c : 2 * c + 2]
            out_ref[c, 74:, lanes] = jnp.zeros((TAKEN - 74, 128), F32)


def near_backward_kernel(
    off_ref, keep_ref, came_ref, acc_ref, back_ref, stay_ref, leave_ref, rows_ref, keys_ref,
):
    first = OWN * lax.axis_index("core") + 2 * pl.program_id(0)

    def add_taken(ref, j, lanes):
        base = j * 512
        for low, high, offset, stride in (
            (0, 64, off_ref[0, first + j], 8),
            (64, 72, off_ref[1, first + j], 64),
            (72, 74, off_ref[2, first + j], 256),
        ):
            rows = pl.ds(base + offset, high - low, stride=stride)
            ref[rows, :] = ref[rows, :] + back_ref[j, low:high, lanes]

    def put(j, low, high, value):
        stay_ref[j, low:high, :] = value[:, :ROWS]
        leave_ref[j, low:high, :] = value[:, ROWS:]

    blocks = []
    turned = []
    rows_ref[...] = acc_ref[...]
    for j in range(2):
        add_taken(rows_ref, j, slice(128, 256))
    for j in range(2):
        kv_t = both(keep_ref, came_ref, j, 0, 2 * WIDTH)
        qg_t = both(keep_ref, came_ref, j, 2 * WIDTH, TD)
        sums = rows_ref[j * 512 : j * 512 + 512, :].T
        total = sums[DEN : DEN + 1]
        merged = sums[:WIDTH] / total
        dots = jnp.sum(qg_t[WIDTH:].astype(F32) * merged, axis=0, keepdims=True)
        put(j, 0, WIDTH, merged.astype(BF16))
        blocks.append((turn(kv_t), qg_t[:WIDTH], qg_t[WIDTH:], 1.0 / (total * 0.25), dots))
        turned.append((kv_t[:WIDTH], turn(qg_t), sums[WIDTH : 2 * WIDTH]))
    results = backward_units(blocks)
    query_parts = [dot(part[0], grad) * SCALE + part[2] for part, (_, grad) in zip(turned, results)]
    grad_parts = [dot(grad, part[1]) for part, (_, grad) in zip(turned, results)]
    value_parts = [dot(share, part[1]) for part, (share, _) in zip(turned, results)]
    for j in range(2):
        put(j, WIDTH, 2 * WIDTH, query_parts[j].astype(BF16))
        keys_ref[j * 512 : j * 512 + 512, :] = widen(pick(grad_parts[j], value_parts[j]))
        add_taken(keys_ref, j, slice(0, 128))
        put(j, 2 * WIDTH, TD, keys_ref[j * 512 : j * 512 + 512, :].astype(BF16).T[: 2 * WIDTH])


def per_device(queries, key_states, value_states, cotangent, offsets):
    struct = jax.ShapeDtypeStruct
    def swap(x):
        return lax.ppermute(x, "core", [(0, 1), (1, 0)])

    half = struct((OWN, 4 * WIDTH, ROWS), BF16)
    keep, send = call(
        pack_kernel, (half, half), args=(key_states, value_states, queries, cotangent)
    )
    came = swap(send)
    rows_f32 = struct((GROUP_ROWS, 128), F32)
    acc, taken = call(
        near_forward_kernel,
        (rows_f32, struct((OWN, TAKEN, FAR_LANES), BF16)),
        scratch=(pltpu.VMEM((4, TAKEN, 128), F32),),
        steps=2,
        smem=1,
        args=(offsets, keep, came),
    )
    taken = lax.all_to_all(taken, CHIPS, 0, 0, tiled=True)
    block2, far = call(
        middle_kernel,
        (struct((PICK_TWO, 128), F32), struct((8, PICK_FAR, FAR_LANES), BF16)),
        smem=1,
        args=(offsets, taken),
    )
    far = lax.all_to_all(far, HALF, 0, 0, tiled=True)
    block3, here = call(
        three_kernel,
        (struct((512, 128), F32), struct((128, FAR_LANES), BF16)),
        smem=1,
        args=(offsets, far),
    )
    there = lax.ppermute(here, "y_high", [(0, 1), (1, 0)])
    back = call(
        far_kernel,
        struct((OWN, TAKEN, 256), F32),
        scratch=(pltpu.VMEM((512, 128), F32), pltpu.VMEM((512, 128), F32), pltpu.VMEM((256, 128), F32)),
        smem=1,
        args=(offsets, taken, block2, far, block3, here, there),
    )
    back = lax.all_to_all(back, CHIPS, 0, 0, tiled=True)
    stay, leave = call(
        near_backward_kernel,
        (half, half),
        scratch=(pltpu.VMEM((1024, 128), F32), pltpu.VMEM((1024, 128), F32)),
        steps=4,
        smem=1,
        args=(offsets, keep, came, acc, back),
    )
    shape = struct((ROWS, HEADS * WIDTH), BF16)
    return tuple(call(unpack_kernel, (shape,) * 4, args=(stay, swap(leave))))


def solution(mesh):
    axes = ("y_high", "y_low", "z_high", "z_low", "x", "core")
    inner = Mesh(mesh.devices.reshape(2, 2, 4, 2, 4, 2), axes)
    rows = P(axes, None)
    return jax.shard_map(
        per_device,
        mesh=inner,
        in_specs=(rows, rows, rows, rows, P()),
        out_specs=(rows, rows, rows, rows),
        check_vma=False,
    )
```

time: 116 us -> 93.3 us (0.80)
  blocking collectives: 86.5 us -> 44 us
  starting transfers between devices: 0 us -> 9.94 us
  waiting for transfers between devices: 0 us -> 6.49 us
  Pallas kernels: 26.6 us -> 29.3 us
  local copies, waits for them, and re-layouts: 0.85 us -> 2.39 us
    all_to_all x3, blocking collectives: 86.5 us -> 44 us  [the longest x1 19.8 us: per_device(): far = lax.all_to_all(far, HALF, 0, 0, tiled=True)]
    ppermute x0 -> x3, starting transfers between devices: none -> 9.94 us  [the longest x2 7.35 us: swap(): return lax.ppermute(x, 'core', [(0, 1), (1, 0)])]
    ppermute x0 -> x3, waiting for transfers between devices: none -> 6.49 us  [the longest x2 4.25 us: swap(): return lax.ppermute(x, 'core', [(0, 1), (1, 0)])]
    pallas_call x4 -> x7, Pallas kernels: 26.6 us -> 29.3 us  [call(): pl.pallas_call(kernel, out_shape=out_shape, grid=(steps,) if steps else (...]
    unnamed x2 -> x6, local copies, waits for them, and re-layouts: 0.67 us -> 2.39 us
  transfers between devices with their start and end apart: 0 -> 3, of which waited for: 0 -> 3; matrix products, arithmetic and copies ran while one was open for 0% -> 0% of each run, Pallas kernels for 0% -> 0%
where the time goes in v3:
time: 93.3 us; the launch traced here: 92.8 us
  blocking collectives  44 us (47%)
  Pallas kernels  29.3 us (31%)
  starting transfers between devices  9.94 us (11%)
  waiting for transfers between devices  6.49 us (7%)
  local copies, waits for them, and re-layouts  2.39 us (3%)
    pallas_call x7, Pallas kernels, call(): pl.pallas_call(kernel, out_shape=out_shape, grid=(steps,) if steps else (...  29.3 us
    all_to_all x1, blocking collectives, per_device(): far = lax.all_to_all(far, HALF, 0, 0, tiled=True)  19.8 us
    all_to_all x1, blocking collectives, per_device(): back = lax.all_to_all(back, CHIPS, 0, 0, tiled=True)  12.7 us
    all_to_all x1, blocking collectives, per_device(): taken = lax.all_to_all(taken, CHIPS, 0, 0, tiled=True)  11.6 us
    ppermute x2, starting transfers between devices, swap(): return lax.ppermute(x, 'core', [(0, 1), (1, 0)])  7.35 us
    ppermute x2, waiting for transfers between devices, swap(): return lax.ppermute(x, 'core', [(0, 1), (1, 0)])  4.25 us
    ppermute x1, starting transfers between devices, per_device(): there = lax.ppermute(here, 'y_high', [(0, 1), (1, 0)])  2.59 us
    unnamed x6, local copies, waits for them, and re-layouts  2.39 us
  transfers between devices with their start and end apart: 3, of which 3 were waited for; matrix products, arithmetic and copies ran while one was open for 0% of the time, Pallas kernels for 0%

profile of v3, /device:TPU:1, one launch (start us, length us, event | category | flops | bytes accessed | tf_op | source)
XLA Modules:
  0.0 92.8 jit_solution(1777358067824429656)
XLA Ops:
  0.6 3.1 %shard_map.84 = (bf16[8,192,256]{2,1,0:T(8,128)(2,1)}, bf16[8,192,256]{2,1,0:T(8,128)(2,1)}) custom-call(bf16[256,768]{1,0:T(8,128)(2,1)} %k_ref.1, bf16[256,768]{1,0:T(8,128)(2,1)} %v_ref.1, bf16[256,768]{1,0:T(8,128)(2,1)} %q_ref.1, bf16[256,768]{1,0:T(8,128)(2,1)} %g_ref.1), custom_call_target="tpu_custom_call" | custom-call | tf_op jit(solution)/shard_map/pallas_call | solution.py:46
  3.7 3.2 %collective-permute-start = (bf16[8,192,256]{2,1,0:T(8,128)(2,1)}, bf16[8,192,256]{2,1,0:T(8,128)(2,1)S(1)}, u32[]{:S(2)}, u32[]{:S(2)}) collective-permute-start(bf16[8,192,256]{2,1,0:T(8,128)(2,1)} %get-tuple-element.15), channel_id=1, source_target_pairs={{0,1},{1,0},{2,3},{3,2},{4,5},{5,4},{6,7},{7,6},{8,9},{9,8},{10,11... | collective-permute-start | bytes 2359304 | tf_op jit(solution)/shard_map/ppermute | solution.py:413
  6.9 2.1 %collective-permute-done.came_ref = bf16[8,192,256]{2,1,0:T(8,128)(2,1)S(1)} collective-permute-done((bf16[8,192,256]{2,1,0:T(8,128)(2,1)}, bf16[8,192,256]{2,1,0:T(8,128)(2,1)S(1)}, u32[]{:S(2)}, u32[]{:S(2)}) %collective-permute-start) | collective-permute-done | bytes 786464 | tf_op jit(solution)/shard_map/ppermute | solution.py:413
  9.0 0.0 copy-start
  9.0 0.9 copy-done
  9.9 5.1 %shard_map.85 = (f32[4096,128]{1,0:T(8,128)}, bf16[8,80,256]{2,1,0:T(8,128)(2,1)}) custom-call(s32[3,16]{1,0:T(4,128)} %off_ref.9, bf16[8,192,256]{2,1,0:T(8,128)(2,1)} %get-tuple-element.14.keep_ref, bf16[8,192,256]{2,1,0:T(8,128)(2,1)} %copy-done), custom_call_target="tpu_custom_call" | custom-call | tf_op jit(solution)/shard_map/pallas_call | solution.py:46
  15.0 11.6 %all_to_all.15.in_ref = bf16[8,80,256]{2,1,0:T(8,128)(2,1)} all-to-all(bf16[8,80,256]{2,1,0:T(8,128)(2,1)} %get-tuple-element.17), channel_id=1, replica_groups=mesh['y_high'=2,'y_low'=2,'z_high'=4,'z_low'=2,'x'=4,'core'=2] {'z_low',..., dimensions={0} | all-to-all | bytes 655360 | tf_op jit(solution)/shard_map/all_to_all | solution.py:429
  26.7 2.8 %shard_map.86 = (f32[512,128]{1,0:T(8,128)}, bf16[8,80,256]{2,1,0:T(8,128)(2,1)}) custom-call(s32[3,16]{1,0:T(4,128)} %off_ref.9, bf16[8,80,256]{2,1,0:T(8,128)(2,1)} %all_to_all.15.in_ref), custom_call_target="tpu_custom_call" | custom-call | tf_op jit(solution)/shard_map/pallas_call | solution.py:46
  29.4 19.8 %all_to_all.16.all_ref = bf16[8,80,256]{2,1,0:T(8,128)(2,1)} all-to-all(bf16[8,80,256]{2,1,0:T(8,128)(2,1)} %get-tuple-element.19), channel_id=1, replica_groups=mesh['y_high'=2,'y_low'=2,'z_high'=4,'z_low'=2,'x'=4,'core'=2] {'y_low',..., dimensions={0} | all-to-all | bytes 655360 | tf_op jit(solution)/shard_map/all_to_all | solution.py:436
  49.2 2.6 %shard_map.87 = (f32[512,128]{1,0:T(8,128)}, bf16[128,256]{1,0:T(8,128)(2,1)}) custom-call(s32[3,16]{1,0:T(4,128)} %off_ref.9, bf16[8,80,256]{2,1,0:T(8,128)(2,1)} %all_to_all.16.all_ref), custom_call_target="tpu_custom_call" | custom-call | tf_op jit(solution)/shard_map/pallas_call | solution.py:46
  51.8 2.6 %collective-permute-start.1 = (bf16[128,256]{1,0:T(8,128)(2,1)}, bf16[128,256]{1,0:T(8,128)(2,1)S(1)}, u32[]{:S(2)}, u32[]{:S(2)}) collective-permute-start(bf16[128,256]{1,0:T(8,128)(2,1)} %get-tuple-element.21.here_ref), channel_id=1, source_target_pairs={{0,128},{128,0},{1,129},{129,1},{2,130},{130,2},{3,131},{131,3},{4... | collective-permute-start | bytes 196616 | tf_op jit(solution)/shard_map/ppermute | solution.py:443
  54.4 2.2 %collective-permute-done.1.there_ref = bf16[128,256]{1,0:T(8,128)(2,1)S(1)} collective-permute-done((bf16[128,256]{1,0:T(8,128)(2,1)}, bf16[128,256]{1,0:T(8,128)(2,1)S(1)}, u32[]{:S(2)}, u32[]{:S(2)}) %collective-permute-start.1) | collective-permute-done | bytes 65568 | tf_op jit(solution)/shard_map/ppermute | solution.py:443
  56.6 0.0 copy-start.2
  56.6 0.6 copy-done.2
  57.2 3.7 %shard_map.88 = f32[8,80,256]{2,1,0:T(8,128)} custom-call(s32[3,16]{1,0:T(4,128)} %off_ref.9, bf16[8,80,256]{2,1,0:T(8,128)(2,1)} %all_to_all.15.in_ref, f32[512,128]{1,0:T(8,128)} %get-tuple-element.18.block2_ref, bf16[8,80,256]{2,1,0:T(8,128)(2,1)} %all_to_all.16.all_ref, f32[512,128]{1,0:T(8,128)} %get-tuple-element.20.block3_ref, ...), custom_call_target="tpu_custom_call" | custom-call | tf_op jit(solution)/shard_map/pallas_call | solution.py:46
  61.0 12.7 %all_to_all.17.back_ref = f32[8,80,256]{2,1,0:T(8,128)} all-to-all(f32[8,80,256]{2,1,0:T(8,128)} %shard_map.88), channel_id=1, replica_groups=mesh['y_high'=2,'y_low'=2,'z_high'=4,'z_low'=2,'x'=4,'core'=2] {'z_low',..., dimensions={0} | all-to-all | bytes 1310720 | tf_op jit(solution)/shard_map/all_to_all | solution.py:451
  73.6 9.1 %shard_map.89 = (bf16[8,192,256]{2,1,0:T(8,128)(2,1)}, bf16[8,192,256]{2,1,0:T(8,128)(2,1)}) custom-call(s32[3,16]{1,0:T(4,128)} %off_ref.9, bf16[8,192,256]{2,1,0:T(8,128)(2,1)} %get-tuple-element.14.keep_ref, bf16[8,192,256]{2,1,0:T(8,128)(2,1)} %copy-done, f32[4096,128]{1,0:T(8,128)} %get-tuple-element.16.acc_ref, f32[8,80,256]{2,1,0:T(8,128)} %all_to_all.17.back_ref), custom_call_target="tpu_custom_call" | custom-call | tf_op jit(solution)/shard_map/pallas_call | solution.py:46
  82.7 4.1 %collective-permute-start.2 = (bf16[8,192,256]{2,1,0:T(8,128)(2,1)}, bf16[8,192,256]{2,1,0:T(8,128)(2,1)S(1)}, u32[]{:S(2)}, u32[]{:S(2)}) collective-permute-start(bf16[8,192,256]{2,1,0:T(8,128)(2,1)} %get-tuple-element.23), channel_id=1, source_target_pairs={{0,1},{1,0},{2,3},{3,2},{4,5},{5,4},{6,7},{7,6},{8,9},{9,8},{10,11... | collective-permute-start | bytes 2359304 | tf_op jit(solution)/shard_map/ppermute | solution.py:413
  86.9 2.1 %collective-permute-done.2.came_ref = bf16[8,192,256]{2,1,0:T(8,128)(2,1)S(1)} collective-permute-done((bf16[8,192,256]{2,1,0:T(8,128)(2,1)}, bf16[8,192,256]{2,1,0:T(8,128)(2,1)S(1)}, u32[]{:S(2)}, u32[]{:S(2)}) %collective-permute-start.2) | collective-permute-done | bytes 786464 | tf_op jit(solution)/shard_map/ppermute | solution.py:413
  89.0 0.0 copy-start.1
  89.0 0.9 copy-done.1
  89.9 3.0 %shard_map.90 = (bf16[256,768]{1,0:T(8,128)(2,1)}, bf16[256,768]{1,0:T(8,128)(2,1)}, bf16[256,768]{1,0:T(8,128)(2,1)}, bf16[256,768]{1,0:T(8,128)(2,1)}) custom-call(bf16[8,192,256]{2,1,0:T(8,128)(2,1)} %get-tuple-element.22.keep_ref, bf16[8,192,256]{2,1,0:T(8,128)(2,1)} %copy-done.1), custom_call_target="tpu_custom_call" | custom-call | tf_op jit(solution)/shard_map/pallas_call | solution.py:46
Async XLA Ops:
  3.7 5.4 %collective-permute-start = (bf16[8,192,256]{2,1,0:T(8,128)(2,1)}, bf16[8,192,256]{2,1,0:T(8,128)(2,1)S(1)}, u32[]{:S(2)}, u32[]{:S(2)}) collective-permute-start(bf16[8,192,256]{2,1,0:T(8,128)(2,1)} %get-tuple-element.15), channel_id=1, source_target_pairs={{0,1},{1,0},{2,3},{3,2},{4,5},{5,4},{6,7},{7,6},{8,9},{9,8},{10,11... | collective-permute-start | bytes 2359304 | tf_op jit(solution)/shard_map/ppermute | solution.py:413
  9.0 0.9 copy-start
  51.8 4.8 %collective-permute-start.1 = (bf16[128,256]{1,0:T(8,128)(2,1)}, bf16[128,256]{1,0:T(8,128)(2,1)S(1)}, u32[]{:S(2)}, u32[]{:S(2)}) collective-permute-start(bf16[128,256]{1,0:T(8,128)(2,1)} %get-tuple-element.21.here_ref), channel_id=1, source_target_pairs={{0,128},{128,0},{1,129},{129,1},{2,130},{130,2},{3,131},{131,3},{4... | collective-permute-start | bytes 196616 | tf_op jit(solution)/shard_map/ppermute | solution.py:443
  56.6 0.6 copy-start.2
  82.7 6.2 %collective-permute-start.2 = (bf16[8,192,256]{2,1,0:T(8,128)(2,1)}, bf16[8,192,256]{2,1,0:T(8,128)(2,1)S(1)}, u32[]{:S(2)}, u32[]{:S(2)}) collective-permute-start(bf16[8,192,256]{2,1,0:T(8,128)(2,1)} %get-tuple-element.23), channel_id=1, source_target_pairs={{0,1},{1,0},{2,3},{3,2},{4,5},{5,4},{6,7},{7,6},{8,9},{9,8},{10,11... | collective-permute-start | bytes 2359304 | tf_op jit(solution)/shard_map/ppermute | solution.py:413
  89.0 0.9 copy-start.1

commit v4 on v3

--- a/solution.py
+++ b/solution.py
@@ -10,6 +10,7 @@
 HEADS = 16
 WIDTH = 48
 ROWS = 256
+HALF_WIDTH = 384
 OWN = 8
 GROUP_ROWS = 16 * ROWS
 PICK_TWO = GROUP_ROWS // 8
@@ -20,7 +21,7 @@
 EXPONENT = FACTOR * math.log2(math.e)
 BF16 = jnp.bfloat16
 F32 = jnp.float32
-LIMIT = 56 * 1024 * 1024
+LIMIT = 32 * 1024 * 1024
 
 CHIPS = ("z_low", "x")
 HALF = ("y_low", "z_high")
@@ -54,43 +55,61 @@
     )(*args)
 
 
-def pack_kernel(k_ref, v_ref, q_ref, g_ref, keep_ref, send_ref):
-    parts = []
-    for ref in (k_ref, v_ref, q_ref, g_ref):
-        turned = ref[...].T
-        middle = OWN * WIDTH
-        parts.append([turned[:middle].reshape(OWN, WIDTH, ROWS), turned[middle:].reshape(OWN, WIDTH, ROWS)])
-
-    def store(low_ref, high_ref):
-        for place, (low, high) in enumerate(parts):
-            span = slice(place * WIDTH, (place + 1) * WIDTH)
-            low_ref[:, span, :] = low
-            high_ref[:, span, :] = high
-
-    @pl.when(lax.axis_index("core") == 0)
-    def _():
-        store(keep_ref, send_ref)
-
-    @pl.when(lax.axis_index("core") == 1)
-    def _():
-        store(send_ref, keep_ref)
-
-
-def unpack_kernel(keep_ref, came_ref, a_ref, q_ref, k_ref, v_ref):
-    def store(low_ref, high_ref):
-        for place, ref in enumerate((a_ref, q_ref, k_ref, v_ref)):
-            span = slice(place * WIDTH, (place + 1) * WIDTH)
-            low = low_ref[:, span, :].reshape(OWN * WIDTH, ROWS)
-            high = high_ref[:, span, :].reshape(OWN * WIDTH, ROWS)
-            ref[...] = jnp.concatenate([low, high], axis=0).T
-
-    @pl.when(lax.axis_index("core") == 0)
-    def _():
-        store(keep_ref, came_ref)
-
-    @pl.when(lax.axis_index("core") == 1)
-    def _():
-        store(came_ref, keep_ref)
+def half_columns(core):
+    return pl.ds(pl.multiple_of(core * HALF_WIDTH, HALF_WIDTH), HALF_WIDTH)
+
+
+def pack_half(arrays, own, half):
+    def kernel(k_ref, v_ref, q_ref, g_ref, out_ref, raw_ref, sem_ref):
+        core = lax.axis_index("core")
+        columns = half_columns(core if own else 1 - core)
+        copies = [
+            pltpu.make_async_copy(ref.at[:, columns], raw_ref.at[place], sem_ref.at[place])
+            for place, ref in enumerate((k_ref, v_ref, q_ref, g_ref))
+        ]
+        for copy in copies:
+            copy.start()
+        for place, copy in enumerate(copies):
+            copy.wait()
+            out_ref[:, place * WIDTH : (place + 1) * WIDTH, :] = raw_ref[place].T.reshape(OWN, WIDTH, ROWS)
+
+    return pl.pallas_call(
+        kernel,
+        out_shape=half,
+        in_specs=[pl.BlockSpec(memory_space=pl.ANY)] * 4,
+        out_specs=pl.BlockSpec(memory_space=pltpu.VMEM),
+        scratch_shapes=[pltpu.VMEM((4, ROWS, HALF_WIDTH), BF16), pltpu.SemaphoreType.DMA((4,))],
+        compiler_params=pltpu.CompilerParams(vmem_limit_bytes=LIMIT),
+    )(*arrays)
+
+
+def unpack_half(half, own, outs):
+    shape = pltpu.HBM((ROWS, HEADS * WIDTH), BF16)
+
+    def kernel(in_ref, *refs):
+        out_refs, raw_ref, sem_ref = refs[-6:-2], refs[-2], refs[-1]
+        core = lax.axis_index("core")
+        columns = half_columns(core if own else 1 - core)
+        copies = []
+        for place, ref in enumerate(out_refs):
+            block = in_ref[:, place * WIDTH : (place + 1) * WIDTH, :].reshape(HALF_WIDTH, ROWS)
+            raw_ref[place] = block.T
+            copy = pltpu.make_async_copy(raw_ref.at[place], ref.at[:, columns], sem_ref.at[place])
+            copy.start()
+            copies.append(copy)
+        for copy in copies:
+            copy.wait()
+
+    anywhere = pl.BlockSpec(memory_space=pl.ANY)
+    return pl.pallas_call(
+        kernel,
+        out_shape=(shape,) * 4,
+        in_specs=[pl.BlockSpec(memory_space=pltpu.VMEM)] + [anywhere] * len(outs),
+        out_specs=(anywhere,) * 4,
+        input_output_aliases={place + 1: place for place in range(len(outs))},
+        scratch_shapes=[pltpu.VMEM((4, ROWS, HALF_WIDTH), BF16), pltpu.SemaphoreType.DMA((4,))],
+        compiler_params=pltpu.CompilerParams(vmem_limit_bytes=LIMIT),
+    )(half, *outs)
 
 
 def upper(q_t):
@@ -111,7 +130,9 @@
 
 
 def forward_unit(kv, v_t, q_t):
-    return forward_units([(kv, v_t, q_t)])[0]
+    middle = q_t.shape[1] // 2
+    parts = forward_units([(kv, v_t, q_t[:, :middle]), (kv, v_t, q_t[:, middle:])])
+    return tuple(jnp.concatenate(pieces, axis=1) for pieces in zip(*parts))
 
 
 def backward_units(blocks):
@@ -145,10 +166,10 @@
     return high, middle, rest - middle
 
 
-def sum_rows(numerator, sums, g_t):
+def sum_columns(numerator, sums, g_t):
     count = numerator.shape[1]
     lined = jnp.sum(g_t.astype(F32) * numerator, axis=0, keepdims=True)
-    block = jnp.concatenate(
+    return jnp.concatenate(
         [
             numerator,
             jnp.zeros((WIDTH, count), F32),
@@ -157,7 +178,10 @@
         ],
         axis=0,
     )
-    return block.T
+
+
+def sum_rows(numerator, sums, g_t):
+    return sum_columns(numerator, sums, g_t).T
 
 
 def query_rows(part_t):
@@ -175,6 +199,23 @@
     return picked.astype(BF16)
 
 
+def fold(rows):
+    tail = rows[:, 128:]
+    pairs = jnp.concatenate([tail[:32, :64], tail[32:64, :64]], axis=1)
+    sums = [tail[16 * i : 16 * i + 16, 64:72] for i in range(4)]
+    last = jnp.concatenate([tail[64:, :72], *sums, jnp.zeros((16, 24), rows.dtype)], axis=1)
+    return jnp.concatenate([rows[:, :128], pairs, last], axis=0)
+
+
+def unfold(block):
+    pairs, last = block[80:112], block[112:]
+    tail = jnp.concatenate([pairs[:, :64], pairs[:, 64:]], axis=0)
+    sums = jnp.concatenate([last[:, 72 + 8 * i : 80 + 8 * i] for i in range(4)], axis=0)
+    three = jnp.concatenate([block[:64], tail, sums, jnp.zeros((64, 56), block.dtype)], axis=1)
+    four = jnp.concatenate([block[64:80], last[:, :72], jnp.zeros((16, 56), block.dtype)], axis=1)
+    return three, four
+
+
 def sums_beside(far):
     def column(place):
         return far[:, TD + place : TD + place + 1]
@@ -200,7 +241,7 @@
     return jnp.concatenate([keep_ref[j, low:high, :], came_ref[j, low:high, :]], axis=1)
 
 
-def near_forward_kernel(off_ref, keep_ref, came_ref, acc_ref, taken_ref, base_ref):
+def near_forward_kernel(off_ref, keep_ref, came_ref, near_ref, taken_ref, base_ref, acc_ref):
     first = OWN * lax.axis_index("core") + 4 * pl.program_id(0)
 
     blocks = []
@@ -208,8 +249,10 @@
         kv_t = both(keep_ref, came_ref, j, 0, 2 * WIDTH)
         blocks.append((turn(kv_t), kv_t[WIDTH:], both(keep_ref, came_ref, j, 2 * WIDTH, 3 * WIDTH)))
     for j, (numerator, sums) in enumerate(forward_units(blocks)):
-        g_t = both(keep_ref, came_ref, j, 3 * WIDTH, TD)
-        acc_ref[j * 512 : j * 512 + 512, :] = sum_rows(numerator, sums, g_t)
+        block = sum_columns(numerator, sums, both(keep_ref, came_ref, j, 3 * WIDTH, TD))
+        near_ref[j, :WIDTH, :] = numerator
+        near_ref[j, WIDTH:, :] = block[DEN : DEN + 16]
+        acc_ref[j * 512 : j * 512 + 512, :] = block.T
 
     row = lax.broadcasted_iota(jnp.int32, (TAKEN, 512), 0)
     col = lax.broadcasted_iota(jnp.int32, (TAKEN, 512), 1)
@@ -254,7 +297,7 @@
     )
     lined = dots * total + from2[:, LINED : LINED + 1]
     total = total + from2[:, DEN : DEN + 1]
-    low = with_sums(far, total, lined / total)
+    low = fold(with_sums(far, total, lined / total))
     for s in range(8):
         far_ref[s] = low
 
@@ -265,13 +308,15 @@
     return far_t, sum_rows(*result, far_t[3 * WIDTH : TD])
 
 
-def three_kernel(off_ref, all_ref, block3_ref, four_ref):
+def three_kernel(off_ref, all_ref, block3_ref, three_ref, four_ref):
     head = OWN * lax.axis_index("core") + lax.axis_index(CHIPS)
     o3, o4 = off_ref[1, head], off_ref[2, head]
     meet = (o4 & 63) == o3
-    far3 = jnp.concatenate([all_ref[j, :PICK_THREE, :] for j in range(8)], axis=0)
+    parts = [unfold(all_ref[j]) for j in range(8)]
+    far3 = jnp.concatenate([part[0] for part in parts], axis=0)
+    three_ref[...] = far3
     block3_ref[...] = far_forward(far3)[1]
-    four = jnp.concatenate([all_ref[j, PICK_THREE:, :] for j in range(8)], axis=0).astype(F32)
+    four = jnp.concatenate([part[1] for part in parts], axis=0).astype(F32)
     from3 = jnp.where(meet, block3_ref[pl.ds(o4 >> 6, 128, stride=4), :], 0.0)
     total, dots = sums_beside(four)
     lined = dots * total + from3[:, LINED : LINED + 1]
@@ -288,7 +333,7 @@
 
 
 def far_kernel(
-    off_ref, in_ref, block2_ref, all_ref, block3_ref, here_ref, there_ref,
+    off_ref, in_ref, block2_ref, far3_ref, block3_ref, here_ref, there_ref,
     out_ref, two_ref, three_ref, four_ref,
 ):
     head = OWN * lax.axis_index("core") + lax.axis_index(CHIPS)
@@ -298,7 +343,7 @@
     own_rows3 = pl.ds(pl.multiple_of(group * PICK_THREE, PICK_THREE), PICK_THREE)
     own_rows4 = pl.ds(pl.multiple_of(group * PICK_FOUR, PICK_FOUR), PICK_FOUR)
 
-    far3 = jnp.concatenate([all_ref[j, :PICK_THREE, :] for j in range(8)], axis=0)
+    far3 = far3_ref[...]
     far3_t = turn(far3)
     far4 = jnp.concatenate([here_ref[...], there_ref[...]], axis=0)
     far4_t, block4 = far_forward(far4)
@@ -320,7 +365,7 @@
     two_t = turn(two)
     pad = 128 - PICK_FAR
     own = jnp.concatenate(
-        [all_ref[group, :PICK_THREE, :], here_ref[own_rows4, :], jnp.zeros((pad, FAR_LANES), BF16)], axis=0
+        [far3_ref[own_rows3, :], here_ref[own_rows4, :], jnp.zeros((pad, FAR_LANES), BF16)], axis=0
     )
     own_t = turn(own)
     own_block = jnp.concatenate([own3, own4, jnp.zeros((pad, 128), F32)], axis=0)
@@ -362,81 +407,142 @@
             out_ref[c, 74:, lanes] = jnp.zeros((TAKEN - 74, 128), F32)
 
 
-def near_backward_kernel(
-    off_ref, keep_ref, came_ref, acc_ref, back_ref, stay_ref, leave_ref, rows_ref, keys_ref,
+def lone_backward_kernel(off_ref, keep_ref, came_ref, acc_ref, near_ref, keys_ref):
+    first = OWN * lax.axis_index("core") + 2 * pl.program_id(0)
+    blocks = []
+    turned = []
+    for j in range(2):
+        kv_t = both(keep_ref, came_ref, j, 0, 2 * WIDTH)
+        qg_t = both(keep_ref, came_ref, j, 2 * WIDTH, TD)
+        sums = acc_ref[j]
+        total = sums[WIDTH : WIDTH + 1]
+        near_ref[j, :WIDTH, :] = (sums[:WIDTH] / total).astype(BF16)
+        inverse = jnp.where(chosen_columns(off_ref, first + j), 0.0, 1.0 / (total * 0.25))
+        blocks.append((turn(kv_t), qg_t[:WIDTH], qg_t[WIDTH:], inverse, sums[WIDTH + 8 : WIDTH + 9] / total))
+        turned.append((kv_t[:WIDTH], turn(qg_t)))
+    results = backward_units(blocks)
+    query_parts = [dot(part[0], grad) * SCALE for part, (_, grad) in zip(turned, results)]
+    grad_parts = [dot(grad, part[1]) for part, (_, grad) in zip(turned, results)]
+    value_parts = [dot(share, part[1]) for part, (share, _) in zip(turned, results)]
+    for j in range(2):
+        near_ref[j, WIDTH:, :] = query_parts[j].astype(BF16)
+        keys_ref[j * 512 : j * 512 + 512, :] = widen(pick(grad_parts[j], value_parts[j]))
+
+
+def chosen_columns(off_ref, head):
+    col = lax.broadcasted_iota(jnp.int32, (1, 512), 1)
+    two = (col & 7) == off_ref[0, head]
+    three = (col & 63) == off_ref[1, head]
+    four = (col & 255) == off_ref[2, head]
+    return jnp.logical_or(two, jnp.logical_or(three, four))
+
+
+def last_backward_kernel(
+    off_ref, keep_ref, came_ref, taken_ref, base_ref, back_ref, near_ref, lone_ref,
+    stay_ref, leave_ref, rows_ref, keys_ref,
 ):
-    first = OWN * lax.axis_index("core") + 2 * pl.program_id(0)
-
-    def add_taken(ref, j, lanes):
-        base = j * 512
-        for low, high, offset, stride in (
-            (0, 64, off_ref[0, first + j], 8),
-            (64, 72, off_ref[1, first + j], 64),
-            (72, 74, off_ref[2, first + j], 256),
-        ):
-            rows = pl.ds(base + offset, high - low, stride=stride)
-            ref[rows, :] = ref[rows, :] + back_ref[j, low:high, lanes]
+    first = OWN * lax.axis_index("core") + 4 * pl.program_id(0)
+    rows_b = slice(128, 256)
 
     def put(j, low, high, value):
         stay_ref[j, low:high, :] = value[:, :ROWS]
         leave_ref[j, low:high, :] = value[:, ROWS:]
 
+    def valid(place, three_in_two, four_in_more):
+        is_three = jnp.logical_and(place >= 64, place < 72)
+        is_four = jnp.logical_and(place >= 72, place < 74)
+        lost = jnp.where(is_three, three_in_two, jnp.where(is_four, four_in_more, jnp.where(place < 64, 0, 1)))
+        return lost == 0
+
     blocks = []
-    turned = []
-    rows_ref[...] = acc_ref[...]
-    for j in range(2):
-        add_taken(rows_ref, j, slice(128, 256))
-    for j in range(2):
+    rest = []
+    for j in range(4):
+        o2, o3, o4 = off_ref[0, first + j], off_ref[1, first + j], off_ref[2, first + j]
+        three_in_two = (o3 & 7) == o2
+        four_in_two = (o4 & 7) == o2
+        meet = (o4 & 63) == o3
+        only_three = jnp.logical_and(meet, jnp.logical_not(four_in_two))
+        flags = (three_in_two.astype(jnp.int32), jnp.logical_or(meet, four_in_two).astype(jnp.int32))
+        rows_ref[j, TAKEN:, :] = jnp.ones((128 - TAKEN, 128), F32)
+        rows_ref[j, :TAKEN, :] = base_ref[j] + back_ref[j, :, rows_b]
+        for rows, low, high, take in (
+            (pl.ds(o3 >> 3, 8, stride=8), 64, 72, three_in_two),
+            (pl.ds(o4 >> 3, 2, stride=32), 72, 74, four_in_two),
+            (pl.ds(64 + (o4 >> 6), 2, stride=4), 72, 74, only_three),
+        ):
+            rows_ref[j, rows, :] = rows_ref[j, rows, :] + jnp.where(take, back_ref[j, low:high, rows_b], 0.0)
+        sums = rows_ref[j].T
+        total = sums[DEN : DEN + 1]
+        lane = lax.broadcasted_iota(jnp.int32, (1, 128), 1)
+        inverse = jnp.where(valid(lane, *flags), 1.0 / (total * 0.25), 0.0)
+        taken = jnp.concatenate([taken_ref[j], jnp.zeros((128 - TAKEN, FAR_LANES), BF16)], axis=0)
+        taken_t = turn(taken)
         kv_t = both(keep_ref, came_ref, j, 0, 2 * WIDTH)
-        qg_t = both(keep_ref, came_ref, j, 2 * WIDTH, TD)
-        sums = rows_ref[j * 512 : j * 512 + 512, :].T
-        total = sums[DEN : DEN + 1]
-        merged = sums[:WIDTH] / total
-        dots = jnp.sum(qg_t[WIDTH:].astype(F32) * merged, axis=0, keepdims=True)
-        put(j, 0, WIDTH, merged.astype(BF16))
-        blocks.append((turn(kv_t), qg_t[:WIDTH], qg_t[WIDTH:], 1.0 / (total * 0.25), dots))
-        turned.append((kv_t[:WIDTH], turn(qg_t), sums[WIDTH : 2 * WIDTH]))
+        blocks.append((
+            turn(kv_t), taken_t[2 * WIDTH : 3 * WIDTH], taken_t[3 * WIDTH : TD], inverse,
+            sums[LINED : LINED + 1] / total,
+        ))
+        row = lax.broadcasted_iota(jnp.int32, (128, 512), 0)
+        col = lax.broadcasted_iota(jnp.int32, (128, 512), 1)
+        target = jnp.where(row < 64, 8 * row + o2, jnp.where(row < 72, 64 * (row - 64) + o3, 256 * (row - 72) + o4))
+        hit = jnp.logical_and(col == target, valid(row, *flags))
+        rest.append((
+            kv_t[:WIDTH], taken[:, 2 * WIDTH : TD], sums[:WIDTH] / total, sums[WIDTH : 2 * WIDTH],
+            jnp.where(hit, 1.0, 0.0).astype(BF16),
+        ))
     results = backward_units(blocks)
-    query_parts = [dot(part[0], grad) * SCALE + part[2] for part, (_, grad) in zip(turned, results)]
-    grad_parts = [dot(grad, part[1]) for part, (_, grad) in zip(turned, results)]
-    value_parts = [dot(share, part[1]) for part, (share, _) in zip(turned, results)]
-    for j in range(2):
-        put(j, WIDTH, 2 * WIDTH, query_parts[j].astype(BF16))
-        keys_ref[j * 512 : j * 512 + 512, :] = widen(pick(grad_parts[j], value_parts[j]))
-        add_taken(keys_ref, j, slice(0, 128))
-        put(j, 2 * WIDTH, TD, keys_ref[j * 512 : j * 512 + 512, :].astype(BF16).T[: 2 * WIDTH])
+    query_parts = [dot(part[0], grad) * SCALE + part[3] for part, (_, grad) in zip(rest, results)]
+    grad_parts = [dot(grad, part[1]) for part, (_, grad) in zip(rest, results)]
+    value_parts = [dot(share, part[1]) for part, (share, _) in zip(rest, results)]
+    for j in range(4):
+        low = jnp.concatenate([rest[j][2], query_parts[j]], axis=0).astype(BF16)
+        spread = dot(low, rest[j][4])
+        chosen = chosen_columns(off_ref, first + j)
+        put(j, 0, 2 * WIDTH, jnp.where(chosen, spread, near_ref[j].astype(F32)).astype(BF16))
+        base = j * 512
+        keys_ref[base : base + 512, :] = lone_ref[base : base + 512, :] + widen(pick(grad_parts[j], value_parts[j]))
+        for low, high, which, stride in ((0, 64, 0, 8), (64, 72, 1, 64), (72, 74, 2, 256)):
+            rows = pl.ds(base + off_ref[which, first + j], high - low, stride=stride)
+            keys_ref[rows, :] = keys_ref[rows, :] + back_ref[j, low:high, :128]
+        put(j, 2 * WIDTH, TD, keys_ref[base : base + 512, :].astype(BF16).T[: 2 * WIDTH])
 
 
 def per_device(queries, key_states, value_states, cotangent, offsets):
     struct = jax.ShapeDtypeStruct
+
+    def in_hbm(x):
+        return pltpu.with_memory_space_constraint(x, pltpu.HBM)
+
+    queries, key_states, value_states, cotangent, offsets = map(
+        in_hbm, (queries, key_states, value_states, cotangent, offsets)
+    )
     def swap(x):
         return lax.ppermute(x, "core", [(0, 1), (1, 0)])
 
     half = struct((OWN, 4 * WIDTH, ROWS), BF16)
-    keep, send = call(
-        pack_kernel, (half, half), args=(key_states, value_states, queries, cotangent)
-    )
-    came = swap(send)
-    rows_f32 = struct((GROUP_ROWS, 128), F32)
-    acc, taken = call(
+    arrays = (key_states, value_states, queries, cotangent)
+    came = swap(pack_half(arrays, False, half))
+    keep = pack_half(arrays, True, half)
+    rows_f32 = pltpu.HBM((GROUP_ROWS, 128), F32)
+    acc, picked, base = call(
         near_forward_kernel,
-        (rows_f32, struct((OWN, TAKEN, FAR_LANES), BF16)),
-        scratch=(pltpu.VMEM((4, TAKEN, 128), F32),),
+        (pltpu.HBM((OWN, 64, 512), F32), struct((OWN, TAKEN, FAR_LANES), BF16), pltpu.HBM((OWN, TAKEN, 128), F32)),
+        scratch=(pltpu.VMEM((4 * 512, 128), F32),),
         steps=2,
         smem=1,
         args=(offsets, keep, came),
     )
-    taken = lax.all_to_all(taken, CHIPS, 0, 0, tiled=True)
+    taken = lax.all_to_all(picked, CHIPS, 0, 0, tiled=True)
     block2, far = call(
         middle_kernel,
-        (struct((PICK_TWO, 128), F32), struct((8, PICK_FAR, FAR_LANES), BF16)),
+        (struct((PICK_TWO, 128), F32), struct((8, 128, 128), BF16)),
         smem=1,
         args=(offsets, taken),
     )
     far = lax.all_to_all(far, HALF, 0, 0, tiled=True)
-    block3, here = call(
+    block3, far3, here = call(
         three_kernel,
-        (struct((512, 128), F32), struct((128, FAR_LANES), BF16)),
+        (struct((512, 128), F32), struct((512, FAR_LANES), BF16), struct((128, FAR_LANES), BF16)),
         smem=1,
         args=(offsets, far),
     )
@@ -446,19 +552,27 @@
         struct((OWN, TAKEN, 256), F32),
         scratch=(pltpu.VMEM((512, 128), F32), pltpu.VMEM((512, 128), F32), pltpu.VMEM((256, 128), F32)),
         smem=1,
-        args=(offsets, taken, block2, far, block3, here, there),
+        args=(offsets, taken, block2, far3, block3, here, there),
     )
     back = lax.all_to_all(back, CHIPS, 0, 0, tiled=True)
-    stay, leave = call(
-        near_backward_kernel,
-        (half, half),
-        scratch=(pltpu.VMEM((1024, 128), F32), pltpu.VMEM((1024, 128), F32)),
+    near, lone = call(
+        lone_backward_kernel,
+        (struct((OWN, 2 * WIDTH, 512), BF16), rows_f32),
         steps=4,
         smem=1,
-        args=(offsets, keep, came, acc, back),
-    )
-    shape = struct((ROWS, HEADS * WIDTH), BF16)
-    return tuple(call(unpack_kernel, (shape,) * 4, args=(stay, swap(leave))))
+        args=(offsets, keep, came, in_hbm(acc)),
+    )
+    stay, leave = call(
+        last_backward_kernel,
+        (half, half),
+        scratch=(pltpu.VMEM((4, 128, 128), F32), pltpu.VMEM((2048, 128), F32)),
+        steps=2,
+        smem=1,
+        args=(offsets, keep, came, picked, in_hbm(base), back, near, in_hbm(lone)),
+    )
+    came = swap(leave)
+    outs = unpack_half(stay, True, ())
+    return tuple(unpack_half(came, False, tuple(map(in_hbm, outs))))
 
 
 def solution(mesh):

time: 93.3 us -> 75.9 us (0.81)
  blocking collectives: 44 us -> 27.6 us
  starting transfers between devices: 9.94 us -> 15.5 us
  waiting for transfers between devices: 6.49 us -> 3.43 us
  local copies, waits for them, and re-layouts: 2.39 us -> 0 us
  Pallas kernels: 29.3 us -> 28.3 us
    all_to_all x2 -> x1, blocking collectives: 24.3 us -> 10.8 us  [per_device(): taken = lax.all_to_all(picked, CHIPS, 0, 0, tiled=True)]
    pallas_call x7 -> x6, Pallas kernels: 29.3 us -> 23.5 us  [call(): pl.pallas_call(kernel, out_shape=out_shape, grid=(steps,) if steps else (...]
    pallas_call x0 -> x4, Pallas kernels: none -> 4.79 us  [the longest x2 2.78 us: pack_half(): pl.pallas_call(kernel, out_shape=half, in_specs=[pl.BlockSpec(memory_spac...]
    all_to_all x0 -> x1, starting transfers between devices: none -> 4.44 us  [per_device(): back = lax.all_to_all(back, CHIPS, 0, 0, tiled=True)]
    all_to_all x1, blocking collectives: 19.8 us -> 16.8 us  [per_device(): far = lax.all_to_all(far, HALF, 0, 0, tiled=True)]
    ppermute x2, waiting for transfers between devices: 4.25 us -> 1.42 us  [swap(): return lax.ppermute(x, 'core', [(0, 1), (1, 0)])]
    unnamed x6 -> x0, local copies, waits for them, and re-layouts: 2.39 us -> none
    ppermute x2, starting transfers between devices: 7.35 us -> 8.35 us  [swap(): return lax.ppermute(x, 'core', [(0, 1), (1, 0)])]
  transfers between devices with their start and end apart: 3 -> 4, of which waited for: 3 -> 3; matrix products, arithmetic and copies ran while one was open for 0% -> 0% of each run, Pallas kernels for 0% -> 14%
where the time goes in v4:
time: 75.9 us; the launch traced here: 75.5 us
  Pallas kernels  28.3 us (37%)
  blocking collectives  27.6 us (36%)
  starting transfers between devices  15.5 us (20%)
  waiting for transfers between devices  3.43 us (5%)
    pallas_call x6, Pallas kernels, call(): pl.pallas_call(kernel, out_shape=out_shape, grid=(steps,) if steps else (...  23.5 us
    all_to_all x1, blocking collectives, per_device(): far = lax.all_to_all(far, HALF, 0, 0, tiled=True)  16.8 us
    all_to_all x1, blocking collectives, per_device(): taken = lax.all_to_all(picked, CHIPS, 0, 0, tiled=True)  10.8 us
    ppermute x2, starting transfers between devices, swap(): return lax.ppermute(x, 'core', [(0, 1), (1, 0)])  8.35 us
    all_to_all x1, starting transfers between devices, per_device(): back = lax.all_to_all(back, CHIPS, 0, 0, tiled=True)  4.44 us
    pallas_call x2, Pallas kernels, pack_half(): pl.pallas_call(kernel, out_shape=half, in_specs=[pl.BlockSpec(memory_spac...  2.78 us
    ppermute x1, starting transfers between devices, per_device(): there = lax.ppermute(here, 'y_high', [(0, 1), (1, 0)])  2.69 us
    pallas_call x2, Pallas kernels, unpack_half(): pl.pallas_call(kernel, out_shape=(shape,) * 4, in_specs=[pl.BlockSpec(mem...  2.02 us
  transfers between devices with their start and end apart: 4, of which 3 were waited for; matrix products, arithmetic and copies ran while one was open for 0% of the time, Pallas kernels for 14%

profile of v4, /device:TPU:1, one launch (start us, length us, event | category | flops | bytes accessed | tf_op | source)
XLA Modules:
  0.0 75.5 jit_solution(9423595539406465272)
XLA Ops:
  0.6 1.4 %shard_map.85 = bf16[8,192,256]{2,1,0:T(8,128)(2,1)S(1)} custom-call(bf16[256,768]{1,0:T(8,128)(2,1)} %k_ref.3, bf16[256,768]{1,0:T(8,128)(2,1)} %v_ref.3, bf16[256,768]{1,0:T(8,128)(2,1)} %q_ref.3, bf16[256,768]{1,0:T(8,128)(2,1)} %g_ref.3), custom_call_target="tpu_custom_call" | custom-call | tf_op jit(solution)/shard_map/pallas_call | solution.py:76
  2.0 3.3 %collective-permute-start = (bf16[8,192,256]{2,1,0:T(8,128)(2,1)S(1)}, bf16[8,192,256]{2,1,0:T(8,128)(2,1)S(1)}, u32[]{:S(2)}, u32[]{:S(2)}) collective-permute-start(bf16[8,192,256]{2,1,0:T(8,128)(2,1)S(1)} %shard_map.85), channel_id=1, source_target_pairs={{0,1},{1,0},{2,3},{3,2},{4,5},{5,4},{6,7},{7,6},{8,9},{9,8},{10,11... | collective-permute-start | bytes 2359304 | tf_op jit(solution)/shard_map/ppermute | solution.py:520
  5.4 1.4 %shard_map.84.keep_ref = bf16[8,192,256]{2,1,0:T(8,128)(2,1)S(1)} custom-call(bf16[256,768]{1,0:T(8,128)(2,1)} %k_ref.3, bf16[256,768]{1,0:T(8,128)(2,1)} %v_ref.3, bf16[256,768]{1,0:T(8,128)(2,1)} %q_ref.3, bf16[256,768]{1,0:T(8,128)(2,1)} %g_ref.3), custom_call_target="tpu_custom_call" | custom-call | tf_op jit(solution)/shard_map/pallas_call | solution.py:76
  6.8 0.5 collective-permute-done.came_ref
  7.3 4.4 %shard_map.86 = (f32[8,64,512]{2,1,0:T(8,128)}, bf16[8,80,256]{2,1,0:T(8,128)(2,1)S(1)}, f32[8,80,128]{2,1,0:T(8,128)}) custom-call(s32[3,16]{1,0:T(4,128)} %off_ref.11, bf16[8,192,256]{2,1,0:T(8,128)(2,1)S(1)} %shard_map.84.keep_ref, bf16[8,192,256]{2,1,0:T(8,128)(2,1)S(1)} %collective-permute-done.came_ref), custom_call_target="tpu_custom_call" | custom-call | tf_op jit(solution)/shard_map/pallas_call | solution.py:47
  11.7 10.8 %all_to_all.15.in_ref = bf16[8,80,256]{2,1,0:T(8,128)(2,1)S(1)} all-to-all(bf16[8,80,256]{2,1,0:T(8,128)(2,1)S(1)} %get-tuple-element.20.taken_ref), channel_id=1, replica_groups=mesh['y_high'=2,'y_low'=2,'z_high'=4,'z_low'=2,'x'=4,'core'=2] {'z_low',..., dimensions={0} | all-to-all | bytes 655360 | tf_op jit(solution)/shard_map/all_to_all | solution.py:535
  22.5 1.8 %shard_map.87 = (f32[512,128]{1,0:T(8,128)S(1)}, bf16[8,128,128]{2,1,0:T(8,128)(2,1)S(1)}) custom-call(s32[3,16]{1,0:T(4,128)} %off_ref.11, bf16[8,80,256]{2,1,0:T(8,128)(2,1)S(1)} %all_to_all.15.in_ref), custom_call_target="tpu_custom_call" | custom-call | tf_op jit(solution)/shard_map/pallas_call | solution.py:47
  24.3 16.8 %all_to_all.16.all_ref = bf16[8,128,128]{2,1,0:T(8,128)(2,1)S(1)} all-to-all(bf16[8,128,128]{2,1,0:T(8,128)(2,1)S(1)} %get-tuple-element.23), channel_id=1, replica_groups=mesh['y_high'=2,'y_low'=2,'z_high'=4,'z_low'=2,'x'=4,'core'=2] {'y_low',..., dimensions={0} | all-to-all | bytes 524288 | tf_op jit(solution)/shard_map/all_to_all | solution.py:542
  41.1 1.8 %shard_map.88 = (f32[512,128]{1,0:T(8,128)S(1)}, bf16[512,256]{1,0:T(8,128)(2,1)S(1)}, bf16[128,256]{1,0:T(8,128)(2,1)S(1)}) custom-call(s32[3,16]{1,0:T(4,128)} %off_ref.11, bf16[8,128,128]{2,1,0:T(8,128)(2,1)S(1)} %all_to_all.16.all_ref), custom_call_target="tpu_custom_call" | custom-call | tf_op jit(solution)/shard_map/pallas_call | solution.py:47
  42.9 2.7 %collective-permute-start.1 = (bf16[128,256]{1,0:T(8,128)(2,1)S(1)}, bf16[128,256]{1,0:T(8,128)(2,1)S(1)}, u32[]{:S(2)}, u32[]{:S(2)}) collective-permute-start(bf16[128,256]{1,0:T(8,128)(2,1)S(1)} %get-tuple-element.26.here_ref), channel_id=1, source_target_pairs={{0,128},{128,0},{1,129},{129,1},{2,130},{130,2},{3,131},{131,3},{4... | collective-permute-start | bytes 196616 | tf_op jit(solution)/shard_map/ppermute | solution.py:549
  45.6 2.0 %collective-permute-done.1.there_ref = bf16[128,256]{1,0:T(8,128)(2,1)S(1)} collective-permute-done((bf16[128,256]{1,0:T(8,128)(2,1)S(1)}, bf16[128,256]{1,0:T(8,128)(2,1)S(1)}, u32[]{:S(2)}, u32[]{:S(2)}) %collective-permute-start.1) | collective-permute-done | bytes 65568 | tf_op jit(solution)/shard_map/ppermute | solution.py:549
  47.6 3.1 %shard_map.89 = f32[8,80,256]{2,1,0:T(8,128)} custom-call(s32[3,16]{1,0:T(4,128)} %off_ref.11, bf16[8,80,256]{2,1,0:T(8,128)(2,1)S(1)} %all_to_all.15.in_ref, f32[512,128]{1,0:T(8,128)S(1)} %get-tuple-element.22.block2_ref, bf16[512,256]{1,0:T(8,128)(2,1)S(1)} %get-tuple-element.24.far3_ref, f32[512,128]{1,0:T(8,128)S(1)} %get-tuple-element.25.block3_ref, ...), custom_call_target="tpu_custom_call" | custom-call | tf_op jit(solution)/shard_map/pallas_call | solution.py:47
  50.7 4.4 %all-to-all-start.2 = ((f32[8,80,256]{2,1,0:T(8,128)}), f32[8,80,256]{2,1,0:T(8,128)S(1)}, u32[]{:S(2)}, u32[]{:S(2)}) async-start(f32[8,80,256]{2,1,0:T(8,128)} %shard_map.89), calls=%async_computation.2 | async-start | bytes 1310720 | tf_op jit(solution)/shard_map/all_to_all | solution.py:557
  55.1 8.2 %shard_map.90 = (bf16[8,96,512]{2,1,0:T(8,128)(2,1)S(1)}, f32[4096,128]{1,0:T(8,128)}) custom-call(s32[3,16]{1,0:T(4,128)} %off_ref.11, bf16[8,192,256]{2,1,0:T(8,128)(2,1)S(1)} %shard_map.84.keep_ref, bf16[8,192,256]{2,1,0:T(8,128)(2,1)S(1)} %collective-permute-done.came_ref, f32[8,64,512]{2,1,0:T(8,128)} %get-tuple-element.27.acc_ref), custom_call_target="tpu_custom_call" | custom-call | tf_op jit(solution)/shard_map/pallas_call | solution.py:47
  63.3 0.0 all-to-all-done.2.back_ref
  63.3 4.2 %shard_map.91 = (bf16[8,192,256]{2,1,0:T(8,128)(2,1)S(1)}, bf16[8,192,256]{2,1,0:T(8,128)(2,1)S(1)}) custom-call(s32[3,16]{1,0:T(4,128)} %off_ref.11, bf16[8,192,256]{2,1,0:T(8,128)(2,1)S(1)} %shard_map.84.keep_ref, bf16[8,192,256]{2,1,0:T(8,128)(2,1)S(1)} %collective-permute-done.came_ref, bf16[8,80,256]{2,1,0:T(8,128)(2,1)S(1)} %get-tuple-element.20.taken_ref, ...), custom_call_target="tpu_custom_call" | custom-call | tf_op jit(solution)/shard_map/pallas_call | solution.py:47
  67.5 5.0 %collective-permute-start.2 = (bf16[8,192,256]{2,1,0:T(8,128)(2,1)S(1)}, bf16[8,192,256]{2,1,0:T(8,128)(2,1)S(1)}, u32[]{:S(2)}, u32[]{:S(2)}) collective-permute-start(bf16[8,192,256]{2,1,0:T(8,128)(2,1)S(1)} %get-tuple-element.30), channel_id=1, source_target_pairs={{0,1},{1,0},{2,3},{3,2},{4,5},{5,4},{6,7},{7,6},{8,9},{9,8},{10,11... | collective-permute-start | bytes 2359304 | tf_op jit(solution)/shard_map/ppermute | solution.py:520
  72.5 1.0 %shard_map.92 = (bf16[256,768]{1,0:T(8,128)(2,1)}, bf16[256,768]{1,0:T(8,128)(2,1)}, bf16[256,768]{1,0:T(8,128)(2,1)}, bf16[256,768]{1,0:T(8,128)(2,1)}) custom-call(bf16[8,192,256]{2,1,0:T(8,128)(2,1)S(1)} %get-tuple-element.31.in_ref), custom_call_target="tpu_custom_call" | custom-call | tf_op jit(solution)/shard_map/pallas_call | solution.py:104
  73.6 0.9 %collective-permute-done.2.in_ref = bf16[8,192,256]{2,1,0:T(8,128)(2,1)S(1)} collective-permute-done((bf16[8,192,256]{2,1,0:T(8,128)(2,1)S(1)}, bf16[8,192,256]{2,1,0:T(8,128)(2,1)S(1)}, u32[]{:S(2)}, u32[]{:S(2)}) %collective-permute-start.2) | collective-permute-done | bytes 786464 | tf_op jit(solution)/shard_map/ppermute | solution.py:520
  74.5 1.0 %shard_map.93 = (bf16[256,768]{1,0:T(8,128)(2,1)}, bf16[256,768]{1,0:T(8,128)(2,1)}, bf16[256,768]{1,0:T(8,128)(2,1)}, bf16[256,768]{1,0:T(8,128)(2,1)}) custom-call(bf16[8,192,256]{2,1,0:T(8,128)(2,1)S(1)} %collective-permute-done.2.in_ref, ...), custom_call_target="tpu_custom_call", output_to_operand_aliasing={{0}: (1, {}), {1}: (2, {}), {2}: (3, {}), {3}: (4, {})} | custom-call | tf_op jit(solution)/shard_map/pallas_call | solution.py:104
Async XLA Ops:
  2.0 5.2 %collective-permute-start = (bf16[8,192,256]{2,1,0:T(8,128)(2,1)S(1)}, bf16[8,192,256]{2,1,0:T(8,128)(2,1)S(1)}, u32[]{:S(2)}, u32[]{:S(2)}) collective-permute-start(bf16[8,192,256]{2,1,0:T(8,128)(2,1)S(1)} %shard_map.85), channel_id=1, source_target_pairs={{0,1},{1,0},{2,3},{3,2},{4,5},{5,4},{6,7},{7,6},{8,9},{9,8},{10,11... | collective-permute-start | bytes 2359304 | tf_op jit(solution)/shard_map/ppermute | solution.py:520
  42.9 4.7 %collective-permute-start.1 = (bf16[128,256]{1,0:T(8,128)(2,1)S(1)}, bf16[128,256]{1,0:T(8,128)(2,1)S(1)}, u32[]{:S(2)}, u32[]{:S(2)}) collective-permute-start(bf16[128,256]{1,0:T(8,128)(2,1)S(1)} %get-tuple-element.26.here_ref), channel_id=1, source_target_pairs={{0,128},{128,0},{1,129},{129,1},{2,130},{130,2},{3,131},{131,3},{4... | collective-permute-start | bytes 196616 | tf_op jit(solution)/shard_map/ppermute | solution.py:549
  50.7 12.6 %all-to-all-start.2 = ((f32[8,80,256]{2,1,0:T(8,128)}), f32[8,80,256]{2,1,0:T(8,128)S(1)}, u32[]{:S(2)}, u32[]{:S(2)}) async-start(f32[8,80,256]{2,1,0:T(8,128)} %shard_map.89), calls=%async_computation.2 | async-start | bytes 1310720 | tf_op jit(solution)/shard_map/all_to_all | solution.py:557
  67.5 6.9 %collective-permute-start.2 = (bf16[8,192,256]{2,1,0:T(8,128)(2,1)S(1)}, bf16[8,192,256]{2,1,0:T(8,128)(2,1)S(1)}, u32[]{:S(2)}, u32[]{:S(2)}) collective-permute-start(bf16[8,192,256]{2,1,0:T(8,128)(2,1)S(1)} %get-tuple-element.30), channel_id=1, source_target_pairs={{0,1},{1,0},{2,3},{3,2},{4,5},{5,4},{6,7},{7,6},{8,9},{9,8},{10,11... | collective-permute-start | bytes 2359304 | tf_op jit(solution)/shard_map/ppermute | solution.py:520

commit v5 on v4

--- a/solution.py
+++ b/solution.py
@@ -1,3 +1,4 @@
+import functools
 import math
 
 import jax
@@ -241,34 +242,29 @@
     return jnp.concatenate([keep_ref[j, low:high, :], came_ref[j, low:high, :]], axis=1)
 
 
-def near_forward_kernel(off_ref, keep_ref, came_ref, near_ref, taken_ref, base_ref, acc_ref):
-    first = OWN * lax.axis_index("core") + 4 * pl.program_id(0)
-
-    blocks = []
-    for j in range(4):
-        kv_t = both(keep_ref, came_ref, j, 0, 2 * WIDTH)
-        blocks.append((turn(kv_t), kv_t[WIDTH:], both(keep_ref, came_ref, j, 2 * WIDTH, 3 * WIDTH)))
-    for j, (numerator, sums) in enumerate(forward_units(blocks)):
-        block = sum_columns(numerator, sums, both(keep_ref, came_ref, j, 3 * WIDTH, TD))
-        near_ref[j, :WIDTH, :] = numerator
-        near_ref[j, WIDTH:, :] = block[DEN : DEN + 16]
-        acc_ref[j * 512 : j * 512 + 512, :] = block.T
-
+def taken_kernel(off_ref, keep_ref, came_ref, taken_ref, base_ref):
+    first = OWN * lax.axis_index("core")
     row = lax.broadcasted_iota(jnp.int32, (TAKEN, 512), 0)
     col = lax.broadcasted_iota(jnp.int32, (TAKEN, 512), 1)
     is_two, is_three = row < 64, row < 72
     start = jnp.where(is_two, 8 * row, jnp.where(is_three, 64 * (row - 64), 256 * (row - 72)))
-    for j in range(4):
+    blocks = []
+    rows = []
+    for j in range(8):
         o2, o3, o4 = off_ref[0, first + j], off_ref[1, first + j], off_ref[2, first + j]
-        base_ref[j, 64:, :] = jnp.ones((16, 128), F32)
-        base_ref[j, :64, :] = acc_ref[pl.ds(j * 512 + o2, 64, stride=8), :]
-        base_ref[j, 64:72, :] = acc_ref[pl.ds(j * 512 + o3, 8, stride=64), :]
-        base_ref[j, 72:74, :] = acc_ref[pl.ds(j * 512 + o4, 2, stride=256), :]
         target = start + jnp.where(is_two, o2, jnp.where(is_three, o3, o4))
         hit = jnp.where(col == target, 1.0, 0.0).astype(BF16)
-        picked = dot_t(hit, both(keep_ref, came_ref, j, 0, TD))
+        columns = both(keep_ref, came_ref, j, 0, TD)
+        picked = dot_t(hit, columns)
+        picked_t = turn(jnp.concatenate([picked.astype(BF16), jnp.zeros((128 - TAKEN, TD), BF16)], axis=0))
+        kv_t = columns[: 2 * WIDTH]
+        blocks.append((turn(kv_t), kv_t[WIDTH:], picked_t[2 * WIDTH : 3 * WIDTH]))
+        rows.append((picked, picked_t[3 * WIDTH :]))
+    for j, (numerator, sums) in enumerate(forward_units(blocks)):
+        picked, g_t = rows[j]
+        base = sum_rows(numerator, sums, g_t)[:TAKEN]
+        base_ref[j] = base
         picked = jnp.concatenate([picked, jnp.zeros((TAKEN, FAR_LANES - TD), F32)], axis=1)
-        base = base_ref[j]
         total = base[:, DEN : DEN + 1]
         taken_ref[j] = with_sums(picked, total, base[:, LINED : LINED + 1] / total)
 
@@ -407,26 +403,51 @@
             out_ref[c, 74:, lanes] = jnp.zeros((TAKEN - 74, 128), F32)
 
 
-def lone_backward_kernel(off_ref, keep_ref, came_ref, acc_ref, near_ref, keys_ref):
-    first = OWN * lax.axis_index("core") + 2 * pl.program_id(0)
+def lone_kernel(first_step, off_ref, keep_ref, came_ref, *refs):
+    near_ref, keys_ref = refs[-2:]
+    first = OWN * lax.axis_index("core") + 2 * (first_step + pl.program_id(0))
     blocks = []
-    turned = []
     for j in range(2):
         kv_t = both(keep_ref, came_ref, j, 0, 2 * WIDTH)
         qg_t = both(keep_ref, came_ref, j, 2 * WIDTH, TD)
-        sums = acc_ref[j]
-        total = sums[WIDTH : WIDTH + 1]
-        near_ref[j, :WIDTH, :] = (sums[:WIDTH] / total).astype(BF16)
-        inverse = jnp.where(chosen_columns(off_ref, first + j), 0.0, 1.0 / (total * 0.25))
-        blocks.append((turn(kv_t), qg_t[:WIDTH], qg_t[WIDTH:], inverse, sums[WIDTH + 8 : WIDTH + 9] / total))
-        turned.append((kv_t[:WIDTH], turn(qg_t)))
-    results = backward_units(blocks)
-    query_parts = [dot(part[0], grad) * SCALE for part, (_, grad) in zip(turned, results)]
-    grad_parts = [dot(grad, part[1]) for part, (_, grad) in zip(turned, results)]
-    value_parts = [dot(share, part[1]) for part, (share, _) in zip(turned, results)]
+        blocks.append((turn(kv_t), kv_t, qg_t, turn(qg_t)))
+    scores = [dot(kv, upper(qg_t[:WIDTH])) for kv, _, qg_t, _ in blocks]
+    probs = [dot(kv, lower(qg_t[WIDTH:])) for kv, _, qg_t, _ in blocks]
+    weights = [jnp.exp2(score * EXPONENT) for score in scores]
+    shares = []
+    for j, weight in enumerate(weights):
+        inverse = 1.0 / (jnp.sum(weight, axis=0, keepdims=True) * 0.25)
+        shares.append(weight * jnp.where(chosen_columns(off_ref, first + j), 0.0, inverse))
+    low = [share.astype(BF16) for share in shares]
+    merged = [dot(block[1][WIDTH:], share) * 0.25 for block, share in zip(blocks, low)]
+    dots = [
+        jnp.sum(block[2][WIDTH:].astype(F32) * part, axis=0, keepdims=True) for block, part in zip(blocks, merged)
+    ]
+    grads = [(share * (prob - line)).astype(BF16) for share, prob, line in zip(shares, probs, dots)]
+    query_parts = [dot(block[1][:WIDTH], grad) * SCALE for block, grad in zip(blocks, grads)]
+    grad_parts = [dot(grad, block[3]) for block, grad in zip(blocks, grads)]
+    value_parts = [dot(share, block[3]) for block, share in zip(blocks, low)]
     for j in range(2):
+        near_ref[j, :WIDTH, :] = merged[j].astype(BF16)
         near_ref[j, WIDTH:, :] = query_parts[j].astype(BF16)
         keys_ref[j * 512 : j * 512 + 512, :] = widen(pick(grad_parts[j], value_parts[j]))
+
+
+def lone_half(first_step, offsets, keep, came, filled):
+    def spec(*shape):
+        return pl.BlockSpec(shape, lambda i: (first_step + i,) + (0,) * (len(shape) - 1))
+
+    heads = spec(2, 4 * WIDTH, ROWS)
+    return pl.pallas_call(
+        functools.partial(lone_kernel, first_step),
+        out_shape=(pltpu.HBM((OWN, 2 * WIDTH, 512), BF16), pltpu.HBM((GROUP_ROWS, 128), F32)),
+        grid=(2,),
+        in_specs=[pl.BlockSpec(memory_space=pltpu.SMEM), heads, heads]
+        + [pl.BlockSpec(memory_space=pl.ANY)] * len(filled),
+        out_specs=(spec(2, 2 * WIDTH, 512), spec(1024, 128)),
+        input_output_aliases={3 + place: place for place in range(len(filled))},
+        compiler_params=pltpu.CompilerParams(vmem_limit_bytes=LIMIT),
+    )(offsets, keep, came, *filled)
 
 
 def chosen_columns(off_ref, head):
@@ -513,6 +534,9 @@
     def in_hbm(x):
         return pltpu.with_memory_space_constraint(x, pltpu.HBM)
 
+    def in_vmem(x):
+        return pltpu.with_memory_space_constraint(x, pltpu.VMEM)
+
     queries, key_states, value_states, cotangent, offsets = map(
         in_hbm, (queries, key_states, value_states, cotangent, offsets)
     )
@@ -524,15 +548,16 @@
     came = swap(pack_half(arrays, False, half))
     keep = pack_half(arrays, True, half)
     rows_f32 = pltpu.HBM((GROUP_ROWS, 128), F32)
-    acc, picked, base = call(
-        near_forward_kernel,
-        (pltpu.HBM((OWN, 64, 512), F32), struct((OWN, TAKEN, FAR_LANES), BF16), pltpu.HBM((OWN, TAKEN, 128), F32)),
-        scratch=(pltpu.VMEM((4 * 512, 128), F32),),
-        steps=2,
+    picked, base = call(
+        taken_kernel,
+        (struct((OWN, TAKEN, FAR_LANES), BF16), pltpu.HBM((OWN, TAKEN, 128), F32)),
+        steps=0,
         smem=1,
         args=(offsets, keep, came),
     )
-    taken = lax.all_to_all(picked, CHIPS, 0, 0, tiled=True)
+    taken = in_vmem(lax.all_to_all(picked, CHIPS, 0, 0, tiled=True))
+    near, lone = lone_half(0, offsets, keep, came, ())
+    taken, near, lone = lax.optimization_barrier((taken, near, lone))
     block2, far = call(
         middle_kernel,
         (struct((PICK_TWO, 128), F32), struct((8, 128, 128), BF16)),
@@ -554,21 +579,15 @@
         smem=1,
         args=(offsets, taken, block2, far3, block3, here, there),
     )
-    back = lax.all_to_all(back, CHIPS, 0, 0, tiled=True)
-    near, lone = call(
-        lone_backward_kernel,
-        (struct((OWN, 2 * WIDTH, 512), BF16), rows_f32),
-        steps=4,
-        smem=1,
-        args=(offsets, keep, came, in_hbm(acc)),
-    )
+    back = in_vmem(lax.all_to_all(back, CHIPS, 0, 0, tiled=True))
+    near, lone = lone_half(2, offsets, keep, came, (in_hbm(near), in_hbm(lone)))
     stay, leave = call(
         last_backward_kernel,
         (half, half),
         scratch=(pltpu.VMEM((4, 128, 128), F32), pltpu.VMEM((2048, 128), F32)),
         steps=2,
         smem=1,
-        args=(offsets, keep, came, picked, in_hbm(base), back, near, in_hbm(lone)),
+        args=(offsets, keep, came, picked, in_hbm(base), back, in_hbm(near), in_hbm(lone)),
     )
     came = swap(leave)
     outs = unpack_half(stay, True, ())

time: 75.9 us -> 75.7 us (level)
  blocking collectives: 27.6 us -> 16.6 us
  starting transfers between devices: 15.5 us -> 21 us
  waiting for transfers between devices: 3.43 us -> 6.4 us
  Pallas kernels: 28.3 us -> 30.4 us
    pallas_call x0 -> x2, Pallas kernels: none -> 11.2 us  [lone_half(): pl.pallas_call(functools.partial(lone_kernel, first_step), out_shape=(plt...]
    all_to_all x1 -> x0, blocking collectives: 10.8 us -> none  [per_device(): taken = lax.all_to_all(picked, CHIPS, 0, 0, tiled=True)]
    pallas_call x6 -> x5, Pallas kernels: 23.5 us -> 14.4 us  [call(): pl.pallas_call(kernel, out_shape=out_shape, grid=(steps,) if steps else (...]
    all_to_all x1 -> x2, starting transfers between devices: 4.44 us -> 10.4 us  [the longest x1 6.72 us: per_device(): back = in_vmem(lax.all_to_all(back, CHIPS, 0, 0, tiled=True))]
    all_to_all x1 -> x2, waiting for transfers between devices: 0.01 us -> 2.98 us  [the longest x1 2.05 us: per_device(): back = in_vmem(lax.all_to_all(back, CHIPS, 0, 0, tiled=True))]
  transfers between devices with their start and end apart: 4 -> 5, of which waited for: 3 -> 5; matrix products, arithmetic and copies ran while one was open for 0% -> 0% of each run, Pallas kernels for 14% -> 18%
where the time goes in v5:
time: 75.7 us; the launch traced here: 75.2 us
  Pallas kernels  30.4 us (40%)
  starting transfers between devices  21 us (28%)
  blocking collectives  16.6 us (22%)
  waiting for transfers between devices  6.4 us (8%)
    all_to_all x1, blocking collectives, per_device(): far = lax.all_to_all(far, HALF, 0, 0, tiled=True)  16.6 us
    pallas_call x5, Pallas kernels, call(): pl.pallas_call(kernel, out_shape=out_shape, grid=(steps,) if steps else (...  14.4 us
    pallas_call x2, Pallas kernels, lone_half(): pl.pallas_call(functools.partial(lone_kernel, first_step), out_shape=(plt...  11.2 us
    ppermute x2, starting transfers between devices, swap(): return lax.ppermute(x, 'core', [(0, 1), (1, 0)])  7.98 us
    all_to_all x1, starting transfers between devices, per_device(): back = in_vmem(lax.all_to_all(back, CHIPS, 0, 0, tiled=True))  6.72 us
    all_to_all x1, starting transfers between devices, per_device(): taken = in_vmem(lax.all_to_all(picked, CHIPS, 0, 0, tiled=True))  3.64 us
    pallas_call x2, Pallas kernels, pack_half(): pl.pallas_call(kernel, out_shape=half, in_specs=[pl.BlockSpec(memory_spac...  2.78 us
    ppermute x1, starting transfers between devices, per_device(): there = lax.ppermute(here, 'y_high', [(0, 1), (1, 0)])  2.71 us
  transfers between devices with their start and end apart: 5, of which 5 were waited for; matrix products, arithmetic and copies ran while one was open for 0% of the time, Pallas kernels for 18%

profile of v5, /device:TPU:1, one launch (start us, length us, event | category | flops | bytes accessed | tf_op | source)
XLA Modules:
  0.0 75.2 jit_solution(4005547779156994872)
XLA Ops:
  0.6 1.4 %shard_map.85 = bf16[8,192,256]{2,1,0:T(8,128)(2,1)S(1)} custom-call(bf16[256,768]{1,0:T(8,128)(2,1)} %k_ref.3, bf16[256,768]{1,0:T(8,128)(2,1)} %v_ref.3, bf16[256,768]{1,0:T(8,128)(2,1)} %q_ref.3, bf16[256,768]{1,0:T(8,128)(2,1)} %g_ref.3), custom_call_target="tpu_custom_call" | custom-call | tf_op jit(solution)/shard_map/pallas_call | solution.py:77
  2.0 3.3 %collective-permute-start = (bf16[8,192,256]{2,1,0:T(8,128)(2,1)S(1)}, bf16[8,192,256]{2,1,0:T(8,128)(2,1)S(1)}, u32[]{:S(2)}, u32[]{:S(2)}) collective-permute-start(bf16[8,192,256]{2,1,0:T(8,128)(2,1)S(1)} %shard_map.85), channel_id=1, source_target_pairs={{0,1},{1,0},{2,3},{3,2},{4,5},{5,4},{6,7},{7,6},{8,9},{9,8},{10,11... | collective-permute-start | bytes 2359304 | tf_op jit(solution)/shard_map/ppermute | solution.py:544
  5.4 1.4 %shard_map.84.keep_ref = bf16[8,192,256]{2,1,0:T(8,128)(2,1)S(1)} custom-call(bf16[256,768]{1,0:T(8,128)(2,1)} %k_ref.3, bf16[256,768]{1,0:T(8,128)(2,1)} %v_ref.3, bf16[256,768]{1,0:T(8,128)(2,1)} %q_ref.3, bf16[256,768]{1,0:T(8,128)(2,1)} %g_ref.3), custom_call_target="tpu_custom_call" | custom-call | tf_op jit(solution)/shard_map/pallas_call | solution.py:77
  6.8 0.5 collective-permute-done.came_ref
  7.3 3.4 %shard_map.86 = (bf16[8,80,256]{2,1,0:T(8,128)(2,1)}, f32[8,80,128]{2,1,0:T(8,128)}) custom-call(s32[3,16]{1,0:T(4,128)} %off_ref.13, bf16[8,192,256]{2,1,0:T(8,128)(2,1)S(1)} %shard_map.84.keep_ref, bf16[8,192,256]{2,1,0:T(8,128)(2,1)S(1)} %collective-permute-done.came_ref), custom_call_target="tpu_custom_call" | custom-call | tf_op jit(solution)/shard_map/pallas_call | solution.py:48
  10.7 3.6 %all-to-all-start = ((bf16[8,80,256]{2,1,0:T(8,128)(2,1)}), bf16[8,80,256]{2,1,0:T(8,128)(2,1)S(1)}, u32[]{:S(2)}, u32[]{:S(2)}) async-start(bf16[8,80,256]{2,1,0:T(8,128)(2,1)} %get-tuple-element.24.taken_ref), calls=%async_computation | async-start | bytes 655360 | tf_op jit(solution)/shard_map/all_to_all | solution.py:558
  14.3 5.6 %shard_map.87 = (bf16[8,96,512]{2,1,0:T(8,128)(2,1)}, f32[4096,128]{1,0:T(8,128)}) custom-call(s32[3,16]{1,0:T(4,128)} %off_ref.13, bf16[8,192,256]{2,1,0:T(8,128)(2,1)S(1)} %shard_map.84.keep_ref, bf16[8,192,256]{2,1,0:T(8,128)(2,1)S(1)} %collective-permute-done.came_ref), custom_call_target="tpu_custom_call" | custom-call | tf_op jit(solution)/shard_map/pallas_call | solution.py:441
  19.9 0.9 %all-to-all-done.in_ref = bf16[8,80,256]{2,1,0:T(8,128)(2,1)S(1)} async-done(((bf16[8,80,256]{2,1,0:T(8,128)(2,1)}), bf16[8,80,256]{2,1,0:T(8,128)(2,1)S(1)}, u32[]{:S(2)}, u32[]{:S(2)}) %all-to-all-start) | async-done | bytes 327712 | tf_op jit(solution)/shard_map/all_to_all | solution.py:558
  20.8 1.8 %shard_map.88 = (f32[512,128]{1,0:T(8,128)S(1)}, bf16[8,128,128]{2,1,0:T(8,128)(2,1)S(1)}) custom-call(s32[3,16]{1,0:T(4,128)} %off_ref.13, bf16[8,80,256]{2,1,0:T(8,128)(2,1)S(1)} %all-to-all-done.in_ref), custom_call_target="tpu_custom_call" | custom-call | tf_op jit(solution)/shard_map/pallas_call | solution.py:48
  22.6 16.6 %all_to_all.15.all_ref = bf16[8,128,128]{2,1,0:T(8,128)(2,1)S(1)} all-to-all(bf16[8,128,128]{2,1,0:T(8,128)(2,1)S(1)} %get-tuple-element.30), channel_id=1, replica_groups=mesh['y_high'=2,'y_low'=2,'z_high'=4,'z_low'=2,'x'=4,'core'=2] {'y_low',..., dimensions={0} | all-to-all | bytes 524288 | tf_op jit(solution)/shard_map/all_to_all | solution.py:567
  39.3 1.8 %shard_map.89 = (f32[512,128]{1,0:T(8,128)S(1)}, bf16[512,256]{1,0:T(8,128)(2,1)S(1)}, bf16[128,256]{1,0:T(8,128)(2,1)S(1)}) custom-call(s32[3,16]{1,0:T(4,128)} %off_ref.13, bf16[8,128,128]{2,1,0:T(8,128)(2,1)S(1)} %all_to_all.15.all_ref), custom_call_target="tpu_custom_call" | custom-call | tf_op jit(solution)/shard_map/pallas_call | solution.py:48
  41.1 2.7 %collective-permute-start.1 = (bf16[128,256]{1,0:T(8,128)(2,1)S(1)}, bf16[128,256]{1,0:T(8,128)(2,1)S(1)}, u32[]{:S(2)}, u32[]{:S(2)}) collective-permute-start(bf16[128,256]{1,0:T(8,128)(2,1)S(1)} %get-tuple-element.33.here_ref), channel_id=1, source_target_pairs={{0,128},{128,0},{1,129},{129,1},{2,130},{130,2},{3,131},{131,3},{4... | collective-permute-start | bytes 196616 | tf_op jit(solution)/shard_map/ppermute | solution.py:574
  43.8 2.0 %collective-permute-done.1.there_ref = bf16[128,256]{1,0:T(8,128)(2,1)S(1)} collective-permute-done((bf16[128,256]{1,0:T(8,128)(2,1)S(1)}, bf16[128,256]{1,0:T(8,128)(2,1)S(1)}, u32[]{:S(2)}, u32[]{:S(2)}) %collective-permute-start.1) | collective-permute-done | bytes 65568 | tf_op jit(solution)/shard_map/ppermute | solution.py:574
  45.8 3.1 %shard_map.90 = f32[8,80,256]{2,1,0:T(8,128)} custom-call(s32[3,16]{1,0:T(4,128)} %off_ref.13, bf16[8,80,256]{2,1,0:T(8,128)(2,1)S(1)} %all-to-all-done.in_ref, f32[512,128]{1,0:T(8,128)S(1)} %get-tuple-element.29.block2_ref, bf16[512,256]{1,0:T(8,128)(2,1)S(1)} %get-tuple-element.31.far3_ref, f32[512,128]{1,0:T(8,128)S(1)} %get-tuple-element.32.block3_ref, ...), custom_call_target="tpu_custom_call" | custom-call | tf_op jit(solution)/shard_map/pallas_call | solution.py:48
  48.8 6.7 %all-to-all-start.2 = ((f32[8,80,256]{2,1,0:T(8,128)}), f32[8,80,256]{2,1,0:T(8,128)S(1)}, u32[]{:S(2)}, u32[]{:S(2)}) async-start(f32[8,80,256]{2,1,0:T(8,128)} %shard_map.90), calls=%async_computation.2 | async-start | bytes 1310720 | tf_op jit(solution)/shard_map/all_to_all | solution.py:582
  55.6 5.6 %shard_map.91 = (bf16[8,96,512]{2,1,0:T(8,128)(2,1)}, f32[4096,128]{1,0:T(8,128)}) custom-call(s32[3,16]{1,0:T(4,128)} %off_ref.13, bf16[8,192,256]{2,1,0:T(8,128)(2,1)S(1)} %shard_map.84.keep_ref, bf16[8,192,256]{2,1,0:T(8,128)(2,1)S(1)} %collective-permute-done.came_ref, ...), custom_call_target="tpu_custom_call", output_to_operand_aliasing={{0}: (3, {}), {1}: (4, {})} | custom-call | tf_op jit(solution)/shard_map/pallas_call | solution.py:441
  61.2 2.0 %all-to-all-done.2.back_ref = f32[8,80,256]{2,1,0:T(8,128)S(1)} async-done(((f32[8,80,256]{2,1,0:T(8,128)}), f32[8,80,256]{2,1,0:T(8,128)S(1)}, u32[]{:S(2)}, u32[]{:S(2)}) %all-to-all-start.2) | async-done | bytes 655392 | tf_op jit(solution)/shard_map/all_to_all | solution.py:582
  63.2 4.4 %shard_map.92 = (bf16[8,192,256]{2,1,0:T(8,128)(2,1)S(1)}, bf16[8,192,256]{2,1,0:T(8,128)(2,1)S(1)}) custom-call(s32[3,16]{1,0:T(4,128)} %off_ref.13, bf16[8,192,256]{2,1,0:T(8,128)(2,1)S(1)} %shard_map.84.keep_ref, bf16[8,192,256]{2,1,0:T(8,128)(2,1)S(1)} %collective-permute-done.came_ref, bf16[8,80,256]{2,1,0:T(8,128)(2,1)} %get-tuple-element.24.taken_ref, ...), custom_call_target="tpu_custom_call" | custom-call | tf_op jit(solution)/shard_map/pallas_call | solution.py:48
  67.6 4.7 %collective-permute-start.2 = (bf16[8,192,256]{2,1,0:T(8,128)(2,1)S(1)}, bf16[8,192,256]{2,1,0:T(8,128)(2,1)S(1)}, u32[]{:S(2)}, u32[]{:S(2)}) collective-permute-start(bf16[8,192,256]{2,1,0:T(8,128)(2,1)S(1)} %get-tuple-element.38), channel_id=1, source_target_pairs={{0,1},{1,0},{2,3},{3,2},{4,5},{5,4},{6,7},{7,6},{8,9},{9,8},{10,11... | collective-permute-start | bytes 2359304 | tf_op jit(solution)/shard_map/ppermute | solution.py:544
  72.3 1.0 %shard_map.93 = (bf16[256,768]{1,0:T(8,128)(2,1)}, bf16[256,768]{1,0:T(8,128)(2,1)}, bf16[256,768]{1,0:T(8,128)(2,1)}, bf16[256,768]{1,0:T(8,128)(2,1)}) custom-call(bf16[8,192,256]{2,1,0:T(8,128)(2,1)S(1)} %get-tuple-element.39.in_ref), custom_call_target="tpu_custom_call" | custom-call | tf_op jit(solution)/shard_map/pallas_call | solution.py:105
  73.3 0.9 %collective-permute-done.2.in_ref = bf16[8,192,256]{2,1,0:T(8,128)(2,1)S(1)} collective-permute-done((bf16[8,192,256]{2,1,0:T(8,128)(2,1)S(1)}, bf16[8,192,256]{2,1,0:T(8,128)(2,1)S(1)}, u32[]{:S(2)}, u32[]{:S(2)}) %collective-permute-start.2) | collective-permute-done | bytes 786464 | tf_op jit(solution)/shard_map/ppermute | solution.py:544
  74.2 1.0 %shard_map.94 = (bf16[256,768]{1,0:T(8,128)(2,1)}, bf16[256,768]{1,0:T(8,128)(2,1)}, bf16[256,768]{1,0:T(8,128)(2,1)}, bf16[256,768]{1,0:T(8,128)(2,1)}) custom-call(bf16[8,192,256]{2,1,0:T(8,128)(2,1)S(1)} %collective-permute-done.2.in_ref, ...), custom_call_target="tpu_custom_call", output_to_operand_aliasing={{0}: (1, {}), {1}: (2, {}), {2}: (3, {}), {3}: (4, {})} | custom-call | tf_op jit(solution)/shard_map/pallas_call | solution.py:105
Async XLA Ops:
  2.0 5.2 %collective-permute-start = (bf16[8,192,256]{2,1,0:T(8,128)(2,1)S(1)}, bf16[8,192,256]{2,1,0:T(8,128)(2,1)S(1)}, u32[]{:S(2)}, u32[]{:S(2)}) collective-permute-start(bf16[8,192,256]{2,1,0:T(8,128)(2,1)S(1)} %shard_map.85), channel_id=1, source_target_pairs={{0,1},{1,0},{2,3},{3,2},{4,5},{5,4},{6,7},{7,6},{8,9},{9,8},{10,11... | collective-permute-start | bytes 2359304 | tf_op jit(solution)/shard_map/ppermute | solution.py:544
  10.7 10.2 %all-to-all-start = ((bf16[8,80,256]{2,1,0:T(8,128)(2,1)}), bf16[8,80,256]{2,1,0:T(8,128)(2,1)S(1)}, u32[]{:S(2)}, u32[]{:S(2)}) async-start(bf16[8,80,256]{2,1,0:T(8,128)(2,1)} %get-tuple-element.24.taken_ref), calls=%async_computation | async-start | bytes 655360 | tf_op jit(solution)/shard_map/all_to_all | solution.py:558
  41.1 4.7 %collective-permute-start.1 = (bf16[128,256]{1,0:T(8,128)(2,1)S(1)}, bf16[128,256]{1,0:T(8,128)(2,1)S(1)}, u32[]{:S(2)}, u32[]{:S(2)}) collective-permute-start(bf16[128,256]{1,0:T(8,128)(2,1)S(1)} %get-tuple-element.33.here_ref), channel_id=1, source_target_pairs={{0,128},{128,0},{1,129},{129,1},{2,130},{130,2},{3,131},{131,3},{4... | collective-permute-start | bytes 196616 | tf_op jit(solution)/shard_map/ppermute | solution.py:574
  48.8 14.4 %all-to-all-start.2 = ((f32[8,80,256]{2,1,0:T(8,128)}), f32[8,80,256]{2,1,0:T(8,128)S(1)}, u32[]{:S(2)}, u32[]{:S(2)}) async-start(f32[8,80,256]{2,1,0:T(8,128)} %shard_map.90), calls=%async_computation.2 | async-start | bytes 1310720 | tf_op jit(solution)/shard_map/all_to_all | solution.py:582
  67.6 6.6 %collective-permute-start.2 = (bf16[8,192,256]{2,1,0:T(8,128)(2,1)S(1)}, bf16[8,192,256]{2,1,0:T(8,128)(2,1)S(1)}, u32[]{:S(2)}, u32[]{:S(2)}) collective-permute-start(bf16[8,192,256]{2,1,0:T(8,128)(2,1)S(1)} %get-tuple-element.38), channel_id=1, source_target_pairs={{0,1},{1,0},{2,3},{3,2},{4,5},{5,4},{6,7},{7,6},{8,9},{9,8},{10,11... | collective-permute-start | bytes 2359304 | tf_op jit(solution)/shard_map/ppermute | solution.py:544

commit v6 on v5

--- a/solution.py
+++ b/solution.py
@@ -328,8 +328,20 @@
     return 1.0 / (total * 0.25), (near_dots * near_total + far[LINED : LINED + 1]) / total
 
 
+def ahead_kernel(in_ref, far3_ref, two_ref, two_t_ref, far3_t_ref, weights_ref, probs_ref):
+    two = jnp.concatenate([in_ref[s, :64, :] for s in range(OWN)], axis=0)
+    two_t = turn(two)
+    two_ref[...] = two
+    two_t_ref[...] = two_t
+    far3_t_ref[...] = turn(far3_ref[...])
+    kv = two[:, : 2 * WIDTH]
+    weights_ref[...] = jnp.exp2(dot(kv, upper(two_t[2 * WIDTH : 3 * WIDTH])) * EXPONENT)
+    probs_ref[...] = dot(kv, lower(two_t[3 * WIDTH : TD]))
+
+
 def far_kernel(
-    off_ref, in_ref, block2_ref, far3_ref, block3_ref, here_ref, there_ref,
+    off_ref, two_in_ref, two_t_ref, far3_t_ref, weights_ref, probs_ref,
+    block2_ref, far3_ref, block3_ref, here_ref, there_ref,
     out_ref, two_ref, three_ref, four_ref,
 ):
     head = OWN * lax.axis_index("core") + lax.axis_index(CHIPS)
@@ -340,7 +352,7 @@
     own_rows4 = pl.ds(pl.multiple_of(group * PICK_FOUR, PICK_FOUR), PICK_FOUR)
 
     far3 = far3_ref[...]
-    far3_t = turn(far3)
+    far3_t = far3_t_ref[...]
     far4 = jnp.concatenate([here_ref[...], there_ref[...]], axis=0)
     far4_t, block4 = far_forward(far4)
     four_ref[...] = block4
@@ -357,8 +369,8 @@
     in_two = pl.ds(o4 >> 3, PICK_FOUR, stride=32)
     two_ref[in_two, :] = two_ref[in_two, :] + jnp.where((o4 & 7) == o2, only4, 0.0)
 
-    two = jnp.concatenate([in_ref[s, :64, :] for s in range(OWN)], axis=0)
-    two_t = turn(two)
+    two = two_in_ref[...]
+    two_t = two_t_ref[...]
     pad = 128 - PICK_FAR
     own = jnp.concatenate(
         [far3_ref[own_rows3, :], here_ref[own_rows4, :], jnp.zeros((pad, FAR_LANES), BF16)], axis=0
@@ -374,8 +386,9 @@
         return turned[2 * WIDTH : 3 * WIDTH], turned[3 * WIDTH : TD]
 
     kv_own = own[:, : 2 * WIDTH]
-    results = backward_units((
-        (two[:, : 2 * WIDTH], *queries(two_t), inverse2, dots2),
+    shares2 = weights_ref[...] * inverse2
+    result2 = (shares2.astype(BF16), (shares2 * (probs_ref[...] - dots2)).astype(BF16))
+    results = [result2] + backward_units((
         (far3[:, : 2 * WIDTH], *queries(own_t), own_inverse, own_dots),
         (far4[:, : 2 * WIDTH], *queries(own_t), own_inverse, own_dots),
         (kv_own, *queries(far3_t), inverse3, dots3),
@@ -572,12 +585,19 @@
         args=(offsets, far),
     )
     there = lax.ppermute(here, "y_high", [(0, 1), (1, 0)])
+    square = struct((512, 512), F32)
+    turned = struct((FAR_LANES, 512), BF16)
+    ahead = call(
+        ahead_kernel,
+        (struct((512, FAR_LANES), BF16), turned, turned, square, square),
+        args=(taken, far3),
+    )
     back = call(
         far_kernel,
         struct((OWN, TAKEN, 256), F32),
         scratch=(pltpu.VMEM((512, 128), F32), pltpu.VMEM((512, 128), F32), pltpu.VMEM((256, 128), F32)),
         smem=1,
-        args=(offsets, taken, block2, far3, block3, here, there),
+        args=(offsets, *ahead, block2, far3, block3, here, there),
     )
     back = in_vmem(lax.all_to_all(back, CHIPS, 0, 0, tiled=True))
     near, lone = lone_half(2, offsets, keep, came, (in_hbm(near), in_hbm(lone)))

time: 75.7 us -> 75.6 us (level)
    pallas_call x5 -> x6, Pallas kernels: 14.4 us -> 14.9 us  [call(): pl.pallas_call(kernel, out_shape=out_shape, grid=(steps,) if steps else (...]
  transfers between devices with their start and end apart: 5 -> 5, of which waited for: 5 -> 5; matrix products, arithmetic and copies ran while one was open for 0% -> 0% of each run, Pallas kernels for 18% -> 19%
where the time goes in v6:
time: 75.6 us; the launch traced here: 75.1 us
  Pallas kernels  30.8 us (41%)
  starting transfers between devices  21 us (28%)
  blocking collectives  16.6 us (22%)
  waiting for transfers between devices  5.87 us (8%)
    all_to_all x1, blocking collectives, per_device(): far = lax.all_to_all(far, HALF, 0, 0, tiled=True)  16.6 us
    pallas_call x6, Pallas kernels, call(): pl.pallas_call(kernel, out_shape=out_shape, grid=(steps,) if steps else (...  14.9 us
    pallas_call x2, Pallas kernels, lone_half(): pl.pallas_call(functools.partial(lone_kernel, first_step), out_shape=(plt...  11.2 us
    ppermute x2, starting transfers between devices, swap(): return lax.ppermute(x, 'core', [(0, 1), (1, 0)])  7.97 us
    all_to_all x1, starting transfers between devices, per_device(): back = in_vmem(lax.all_to_all(back, CHIPS, 0, 0, tiled=True))  6.74 us
    all_to_all x1, starting transfers between devices, per_device(): taken = in_vmem(lax.all_to_all(picked, CHIPS, 0, 0, tiled=True))  3.64 us
    pallas_call x2, Pallas kernels, pack_half(): pl.pallas_call(kernel, out_shape=half, in_specs=[pl.BlockSpec(memory_spac...  2.78 us
    ppermute x1, starting transfers between devices, per_device(): there = lax.ppermute(here, 'y_high', [(0, 1), (1, 0)])  2.71 us
  transfers between devices with their start and end apart: 5, of which 5 were waited for; matrix products, arithmetic and copies ran while one was open for 0% of the time, Pallas kernels for 19%

profile of v6, /device:TPU:1, one launch (start us, length us, event | category | flops | bytes accessed | tf_op | source)
XLA Modules:
  0.0 75.1 jit_solution(1685868583271976165)
XLA Ops:
  0.6 1.4 %shard_map.85 = bf16[8,192,256]{2,1,0:T(8,128)(2,1)S(1)} custom-call(bf16[256,768]{1,0:T(8,128)(2,1)} %k_ref.3, bf16[256,768]{1,0:T(8,128)(2,1)} %v_ref.3, bf16[256,768]{1,0:T(8,128)(2,1)} %q_ref.3, bf16[256,768]{1,0:T(8,128)(2,1)} %g_ref.3), custom_call_target="tpu_custom_call" | custom-call | tf_op jit(solution)/shard_map/pallas_call | solution.py:77
  2.0 3.3 %collective-permute-start = (bf16[8,192,256]{2,1,0:T(8,128)(2,1)S(1)}, bf16[8,192,256]{2,1,0:T(8,128)(2,1)S(1)}, u32[]{:S(2)}, u32[]{:S(2)}) collective-permute-start(bf16[8,192,256]{2,1,0:T(8,128)(2,1)S(1)} %shard_map.85), channel_id=1, source_target_pairs={{0,1},{1,0},{2,3},{3,2},{4,5},{5,4},{6,7},{7,6},{8,9},{9,8},{10,11... | collective-permute-start | bytes 2359304 | tf_op jit(solution)/shard_map/ppermute | solution.py:557
  5.4 1.4 %shard_map.84.keep_ref = bf16[8,192,256]{2,1,0:T(8,128)(2,1)S(1)} custom-call(bf16[256,768]{1,0:T(8,128)(2,1)} %k_ref.3, bf16[256,768]{1,0:T(8,128)(2,1)} %v_ref.3, bf16[256,768]{1,0:T(8,128)(2,1)} %q_ref.3, bf16[256,768]{1,0:T(8,128)(2,1)} %g_ref.3), custom_call_target="tpu_custom_call" | custom-call | tf_op jit(solution)/shard_map/pallas_call | solution.py:77
  6.8 0.5 collective-permute-done.came_ref
  7.3 3.4 %shard_map.86 = (bf16[8,80,256]{2,1,0:T(8,128)(2,1)}, f32[8,80,128]{2,1,0:T(8,128)}) custom-call(s32[3,16]{1,0:T(4,128)} %off_ref.13, bf16[8,192,256]{2,1,0:T(8,128)(2,1)S(1)} %shard_map.84.keep_ref, bf16[8,192,256]{2,1,0:T(8,128)(2,1)S(1)} %collective-permute-done.came_ref), custom_call_target="tpu_custom_call" | custom-call | tf_op jit(solution)/shard_map/pallas_call | solution.py:48
  10.7 3.6 %all-to-all-start = ((bf16[8,80,256]{2,1,0:T(8,128)(2,1)}), bf16[8,80,256]{2,1,0:T(8,128)(2,1)S(1)}, u32[]{:S(2)}, u32[]{:S(2)}) async-start(bf16[8,80,256]{2,1,0:T(8,128)(2,1)} %get-tuple-element.29.taken_ref), calls=%async_computation | async-start | bytes 655360 | tf_op jit(solution)/shard_map/all_to_all | solution.py:571
  14.3 5.6 %shard_map.87 = (bf16[8,96,512]{2,1,0:T(8,128)(2,1)}, f32[4096,128]{1,0:T(8,128)}) custom-call(s32[3,16]{1,0:T(4,128)} %off_ref.13, bf16[8,192,256]{2,1,0:T(8,128)(2,1)S(1)} %shard_map.84.keep_ref, bf16[8,192,256]{2,1,0:T(8,128)(2,1)S(1)} %collective-permute-done.came_ref), custom_call_target="tpu_custom_call" | custom-call | tf_op jit(solution)/shard_map/pallas_call | solution.py:454
  19.9 0.9 %all-to-all-done.in_ref = bf16[8,80,256]{2,1,0:T(8,128)(2,1)S(1)} async-done(((bf16[8,80,256]{2,1,0:T(8,128)(2,1)}), bf16[8,80,256]{2,1,0:T(8,128)(2,1)S(1)}, u32[]{:S(2)}, u32[]{:S(2)}) %all-to-all-start) | async-done | bytes 327712 | tf_op jit(solution)/shard_map/all_to_all | solution.py:571
  20.8 1.8 %shard_map.88 = (f32[512,128]{1,0:T(8,128)S(1)}, bf16[8,128,128]{2,1,0:T(8,128)(2,1)S(1)}) custom-call(s32[3,16]{1,0:T(4,128)} %off_ref.13, bf16[8,80,256]{2,1,0:T(8,128)(2,1)S(1)} %all-to-all-done.in_ref), custom_call_target="tpu_custom_call" | custom-call | tf_op jit(solution)/shard_map/pallas_call | solution.py:48
  22.6 16.6 %all_to_all.15.all_ref = bf16[8,128,128]{2,1,0:T(8,128)(2,1)S(1)} all-to-all(bf16[8,128,128]{2,1,0:T(8,128)(2,1)S(1)} %get-tuple-element.34), channel_id=1, replica_groups=mesh['y_high'=2,'y_low'=2,'z_high'=4,'z_low'=2,'x'=4,'core'=2] {'y_low',..., dimensions={0} | all-to-all | bytes 524288 | tf_op jit(solution)/shard_map/all_to_all | solution.py:580
  39.3 1.8 %shard_map.89 = (f32[512,128]{1,0:T(8,128)S(1)}, bf16[512,256]{1,0:T(8,128)(2,1)S(1)}, bf16[128,256]{1,0:T(8,128)(2,1)S(1)}) custom-call(s32[3,16]{1,0:T(4,128)} %off_ref.13, bf16[8,128,128]{2,1,0:T(8,128)(2,1)S(1)} %all_to_all.15.all_ref), custom_call_target="tpu_custom_call" | custom-call | tf_op jit(solution)/shard_map/pallas_call | solution.py:48
  41.1 2.7 %collective-permute-start.1 = (bf16[128,256]{1,0:T(8,128)(2,1)S(1)}, bf16[128,256]{1,0:T(8,128)(2,1)S(1)}, u32[]{:S(2)}, u32[]{:S(2)}) collective-permute-start(bf16[128,256]{1,0:T(8,128)(2,1)S(1)} %get-tuple-element.43.here_ref), channel_id=1, source_target_pairs={{0,128},{128,0},{1,129},{129,1},{2,130},{130,2},{3,131},{131,3},{4... | collective-permute-start | bytes 196616 | tf_op jit(solution)/shard_map/ppermute | solution.py:587
  43.8 0.5 shard_map.90
  44.3 1.5 %collective-permute-done.1.there_ref = bf16[128,256]{1,0:T(8,128)(2,1)S(1)} collective-permute-done((bf16[128,256]{1,0:T(8,128)(2,1)S(1)}, bf16[128,256]{1,0:T(8,128)(2,1)S(1)}, u32[]{:S(2)}, u32[]{:S(2)}) %collective-permute-start.1) | collective-permute-done | bytes 65568 | tf_op jit(solution)/shard_map/ppermute | solution.py:587
  45.8 3.0 %shard_map.91 = f32[8,80,256]{2,1,0:T(8,128)} custom-call(s32[3,16]{1,0:T(4,128)} %off_ref.13, bf16[512,256]{1,0:T(8,128)(2,1)S(1)} %get-tuple-element.36.two_in_ref, bf16[256,512]{1,0:T(8,128)(2,1)S(1)} %get-tuple-element.37.two_t_ref, bf16[256,512]{1,0:T(8,128)(2,1)S(1)} %get-tuple-element.38.far3_t_ref, f32[512,512]{1,0:T(8,128)S(1)} %get-tuple-element.39.weights_ref, ...), custom_call_target="tpu_custom_call" | custom-call | tf_op jit(solution)/shard_map/pallas_call | solution.py:48
  48.8 6.7 %all-to-all-start.2 = ((f32[8,80,256]{2,1,0:T(8,128)}), f32[8,80,256]{2,1,0:T(8,128)S(1)}, u32[]{:S(2)}, u32[]{:S(2)}) async-start(f32[8,80,256]{2,1,0:T(8,128)} %shard_map.91), calls=%async_computation.2 | async-start | bytes 1310720 | tf_op jit(solution)/shard_map/all_to_all | solution.py:602
  55.5 5.6 %shard_map.92 = (bf16[8,96,512]{2,1,0:T(8,128)(2,1)}, f32[4096,128]{1,0:T(8,128)}) custom-call(s32[3,16]{1,0:T(4,128)} %off_ref.13, bf16[8,192,256]{2,1,0:T(8,128)(2,1)S(1)} %shard_map.84.keep_ref, bf16[8,192,256]{2,1,0:T(8,128)(2,1)S(1)} %collective-permute-done.came_ref, ...), custom_call_target="tpu_custom_call", output_to_operand_aliasing={{0}: (3, {}), {1}: (4, {})} | custom-call | tf_op jit(solution)/shard_map/pallas_call | solution.py:454
  61.1 2.1 %all-to-all-done.2.back_ref = f32[8,80,256]{2,1,0:T(8,128)S(1)} async-done(((f32[8,80,256]{2,1,0:T(8,128)}), f32[8,80,256]{2,1,0:T(8,128)S(1)}, u32[]{:S(2)}, u32[]{:S(2)}) %all-to-all-start.2) | async-done | bytes 655392 | tf_op jit(solution)/shard_map/all_to_all | solution.py:602
  63.2 4.4 %shard_map.93 = (bf16[8,192,256]{2,1,0:T(8,128)(2,1)S(1)}, bf16[8,192,256]{2,1,0:T(8,128)(2,1)S(1)}) custom-call(s32[3,16]{1,0:T(4,128)} %off_ref.13, bf16[8,192,256]{2,1,0:T(8,128)(2,1)S(1)} %shard_map.84.keep_ref, bf16[8,192,256]{2,1,0:T(8,128)(2,1)S(1)} %collective-permute-done.came_ref, bf16[8,80,256]{2,1,0:T(8,128)(2,1)} %get-tuple-element.29.taken_ref, ...), custom_call_target="tpu_custom_call" | custom-call | tf_op jit(solution)/shard_map/pallas_call | solution.py:48
  67.5 4.6 %collective-permute-start.2 = (bf16[8,192,256]{2,1,0:T(8,128)(2,1)S(1)}, bf16[8,192,256]{2,1,0:T(8,128)(2,1)S(1)}, u32[]{:S(2)}, u32[]{:S(2)}) collective-permute-start(bf16[8,192,256]{2,1,0:T(8,128)(2,1)S(1)} %get-tuple-element.48), channel_id=1, source_target_pairs={{0,1},{1,0},{2,3},{3,2},{4,5},{5,4},{6,7},{7,6},{8,9},{9,8},{10,11... | collective-permute-start | bytes 2359304 | tf_op jit(solution)/shard_map/ppermute | solution.py:557
  72.2 1.0 %shard_map.94 = (bf16[256,768]{1,0:T(8,128)(2,1)}, bf16[256,768]{1,0:T(8,128)(2,1)}, bf16[256,768]{1,0:T(8,128)(2,1)}, bf16[256,768]{1,0:T(8,128)(2,1)}) custom-call(bf16[8,192,256]{2,1,0:T(8,128)(2,1)S(1)} %get-tuple-element.49.in_ref), custom_call_target="tpu_custom_call" | custom-call | tf_op jit(solution)/shard_map/pallas_call | solution.py:105
  73.2 0.9 %collective-permute-done.2.in_ref = bf16[8,192,256]{2,1,0:T(8,128)(2,1)S(1)} collective-permute-done((bf16[8,192,256]{2,1,0:T(8,128)(2,1)S(1)}, bf16[8,192,256]{2,1,0:T(8,128)(2,1)S(1)}, u32[]{:S(2)}, u32[]{:S(2)}) %collective-permute-start.2) | collective-permute-done | bytes 786464 | tf_op jit(solution)/shard_map/ppermute | solution.py:557
  74.1 1.0 %shard_map.95 = (bf16[256,768]{1,0:T(8,128)(2,1)}, bf16[256,768]{1,0:T(8,128)(2,1)}, bf16[256,768]{1,0:T(8,128)(2,1)}, bf16[256,768]{1,0:T(8,128)(2,1)}) custom-call(bf16[8,192,256]{2,1,0:T(8,128)(2,1)S(1)} %collective-permute-done.2.in_ref, ...), custom_call_target="tpu_custom_call", output_to_operand_aliasing={{0}: (1, {}), {1}: (2, {}), {2}: (3, {}), {3}: (4, {})} | custom-call | tf_op jit(solution)/shard_map/pallas_call | solution.py:105
Async XLA Ops:
  2.0 5.2 %collective-permute-start = (bf16[8,192,256]{2,1,0:T(8,128)(2,1)S(1)}, bf16[8,192,256]{2,1,0:T(8,128)(2,1)S(1)}, u32[]{:S(2)}, u32[]{:S(2)}) collective-permute-start(bf16[8,192,256]{2,1,0:T(8,128)(2,1)S(1)} %shard_map.85), channel_id=1, source_target_pairs={{0,1},{1,0},{2,3},{3,2},{4,5},{5,4},{6,7},{7,6},{8,9},{9,8},{10,11... | collective-permute-start | bytes 2359304 | tf_op jit(solution)/shard_map/ppermute | solution.py:557
  10.7 10.2 %all-to-all-start = ((bf16[8,80,256]{2,1,0:T(8,128)(2,1)}), bf16[8,80,256]{2,1,0:T(8,128)(2,1)S(1)}, u32[]{:S(2)}, u32[]{:S(2)}) async-start(bf16[8,80,256]{2,1,0:T(8,128)(2,1)} %get-tuple-element.29.taken_ref), calls=%async_computation | async-start | bytes 655360 | tf_op jit(solution)/shard_map/all_to_all | solution.py:571
  41.1 4.7 %collective-permute-start.1 = (bf16[128,256]{1,0:T(8,128)(2,1)S(1)}, bf16[128,256]{1,0:T(8,128)(2,1)S(1)}, u32[]{:S(2)}, u32[]{:S(2)}) collective-permute-start(bf16[128,256]{1,0:T(8,128)(2,1)S(1)} %get-tuple-element.43.here_ref), channel_id=1, source_target_pairs={{0,128},{128,0},{1,129},{129,1},{2,130},{130,2},{3,131},{131,3},{4... | collective-permute-start | bytes 196616 | tf_op jit(solution)/shard_map/ppermute | solution.py:587
  48.8 14.4 %all-to-all-start.2 = ((f32[8,80,256]{2,1,0:T(8,128)}), f32[8,80,256]{2,1,0:T(8,128)S(1)}, u32[]{:S(2)}, u32[]{:S(2)}) async-start(f32[8,80,256]{2,1,0:T(8,128)} %shard_map.91), calls=%async_computation.2 | async-start | bytes 1310720 | tf_op jit(solution)/shard_map/all_to_all | solution.py:602
  67.5 6.6 %collective-permute-start.2 = (bf16[8,192,256]{2,1,0:T(8,128)(2,1)S(1)}, bf16[8,192,256]{2,1,0:T(8,128)(2,1)S(1)}, u32[]{:S(2)}, u32[]{:S(2)}) collective-permute-start(bf16[8,192,256]{2,1,0:T(8,128)(2,1)S(1)} %get-tuple-element.48), channel_id=1, source_target_pairs={{0,1},{1,0},{2,3},{3,2},{4,5},{5,4},{6,7},{7,6},{8,9},{9,8},{10,11... | collective-permute-start | bytes 2359304 | tf_op jit(solution)/shard_map/ppermute | solution.py:557

commit v7 on v6

--- a/solution.py
+++ b/solution.py
@@ -22,7 +22,7 @@
 EXPONENT = FACTOR * math.log2(math.e)
 BF16 = jnp.bfloat16
 F32 = jnp.float32
-LIMIT = 32 * 1024 * 1024
+LIMIT = 24 * 1024 * 1024
 
 CHIPS = ("z_low", "x")
 HALF = ("y_low", "z_high")

time: 75.6 us -> 75.6 us (level)
  no operation moved by 1% of the time
where the time goes in v7:
time: 75.6 us; the launch traced here: 75.1 us
  Pallas kernels  30.9 us (41%)
  starting transfers between devices  21 us (28%)
  blocking collectives  16.6 us (22%)
  waiting for transfers between devices  5.87 us (8%)
    all_to_all x1, blocking collectives, per_device(): far = lax.all_to_all(far, HALF, 0, 0, tiled=True)  16.6 us
    pallas_call x6, Pallas kernels, call(): pl.pallas_call(kernel, out_shape=out_shape, grid=(steps,) if steps else (...  14.9 us
    pallas_call x2, Pallas kernels, lone_half(): pl.pallas_call(functools.partial(lone_kernel, first_step), out_shape=(plt...  11.2 us
    ppermute x2, starting transfers between devices, swap(): return lax.ppermute(x, 'core', [(0, 1), (1, 0)])  7.97 us
    all_to_all x1, starting transfers between devices, per_device(): back = in_vmem(lax.all_to_all(back, CHIPS, 0, 0, tiled=True))  6.73 us
    all_to_all x1, starting transfers between devices, per_device(): taken = in_vmem(lax.all_to_all(picked, CHIPS, 0, 0, tiled=True))  3.64 us
    pallas_call x2, Pallas kernels, pack_half(): pl.pallas_call(kernel, out_shape=half, in_specs=[pl.BlockSpec(memory_spac...  2.78 us
    ppermute x1, starting transfers between devices, per_device(): there = lax.ppermute(here, 'y_high', [(0, 1), (1, 0)])  2.71 us
  transfers between devices with their start and end apart: 5, of which 5 were waited for; matrix products, arithmetic and copies ran while one was open for 0% of the time, Pallas kernels for 19%

profile of v7, /device:TPU:1, one launch (start us, length us, event | category | flops | bytes accessed | tf_op | source)
XLA Modules:
  0.0 75.1 jit_solution(14997557740709844528)
XLA Ops:
  0.6 1.4 %shard_map.85 = bf16[8,192,256]{2,1,0:T(8,128)(2,1)S(1)} custom-call(bf16[256,768]{1,0:T(8,128)(2,1)} %k_ref.3, bf16[256,768]{1,0:T(8,128)(2,1)} %v_ref.3, bf16[256,768]{1,0:T(8,128)(2,1)} %q_ref.3, bf16[256,768]{1,0:T(8,128)(2,1)} %g_ref.3), custom_call_target="tpu_custom_call" | custom-call | tf_op jit(solution)/shard_map/pallas_call | solution.py:77
  2.0 3.3 %collective-permute-start = (bf16[8,192,256]{2,1,0:T(8,128)(2,1)S(1)}, bf16[8,192,256]{2,1,0:T(8,128)(2,1)S(1)}, u32[]{:S(2)}, u32[]{:S(2)}) collective-permute-start(bf16[8,192,256]{2,1,0:T(8,128)(2,1)S(1)} %shard_map.85), channel_id=1, source_target_pairs={{0,1},{1,0},{2,3},{3,2},{4,5},{5,4},{6,7},{7,6},{8,9},{9,8},{10,11... | collective-permute-start | bytes 2359304 | tf_op jit(solution)/shard_map/ppermute | solution.py:557
  5.4 1.4 %shard_map.84.keep_ref = bf16[8,192,256]{2,1,0:T(8,128)(2,1)S(1)} custom-call(bf16[256,768]{1,0:T(8,128)(2,1)} %k_ref.3, bf16[256,768]{1,0:T(8,128)(2,1)} %v_ref.3, bf16[256,768]{1,0:T(8,128)(2,1)} %q_ref.3, bf16[256,768]{1,0:T(8,128)(2,1)} %g_ref.3), custom_call_target="tpu_custom_call" | custom-call | tf_op jit(solution)/shard_map/pallas_call | solution.py:77
  6.8 0.5 collective-permute-done.came_ref
  7.3 3.4 %shard_map.86 = (bf16[8,80,256]{2,1,0:T(8,128)(2,1)}, f32[8,80,128]{2,1,0:T(8,128)}) custom-call(s32[3,16]{1,0:T(4,128)} %off_ref.13, bf16[8,192,256]{2,1,0:T(8,128)(2,1)S(1)} %shard_map.84.keep_ref, bf16[8,192,256]{2,1,0:T(8,128)(2,1)S(1)} %collective-permute-done.came_ref), custom_call_target="tpu_custom_call" | custom-call | tf_op jit(solution)/shard_map/pallas_call | solution.py:48
  10.7 3.6 %all-to-all-start = ((bf16[8,80,256]{2,1,0:T(8,128)(2,1)}), bf16[8,80,256]{2,1,0:T(8,128)(2,1)S(1)}, u32[]{:S(2)}, u32[]{:S(2)}) async-start(bf16[8,80,256]{2,1,0:T(8,128)(2,1)} %get-tuple-element.29.taken_ref), calls=%async_computation | async-start | bytes 655360 | tf_op jit(solution)/shard_map/all_to_all | solution.py:571
  14.3 5.6 %shard_map.87 = (bf16[8,96,512]{2,1,0:T(8,128)(2,1)}, f32[4096,128]{1,0:T(8,128)}) custom-call(s32[3,16]{1,0:T(4,128)} %off_ref.13, bf16[8,192,256]{2,1,0:T(8,128)(2,1)S(1)} %shard_map.84.keep_ref, bf16[8,192,256]{2,1,0:T(8,128)(2,1)S(1)} %collective-permute-done.came_ref), custom_call_target="tpu_custom_call" | custom-call | tf_op jit(solution)/shard_map/pallas_call | solution.py:454
  19.9 0.9 %all-to-all-done.in_ref = bf16[8,80,256]{2,1,0:T(8,128)(2,1)S(1)} async-done(((bf16[8,80,256]{2,1,0:T(8,128)(2,1)}), bf16[8,80,256]{2,1,0:T(8,128)(2,1)S(1)}, u32[]{:S(2)}, u32[]{:S(2)}) %all-to-all-start) | async-done | bytes 327712 | tf_op jit(solution)/shard_map/all_to_all | solution.py:571
  20.8 1.8 %shard_map.88 = (f32[512,128]{1,0:T(8,128)S(1)}, bf16[8,128,128]{2,1,0:T(8,128)(2,1)S(1)}) custom-call(s32[3,16]{1,0:T(4,128)} %off_ref.13, bf16[8,80,256]{2,1,0:T(8,128)(2,1)S(1)} %all-to-all-done.in_ref), custom_call_target="tpu_custom_call" | custom-call | tf_op jit(solution)/shard_map/pallas_call | solution.py:48
  22.6 16.6 %all_to_all.15.all_ref = bf16[8,128,128]{2,1,0:T(8,128)(2,1)S(1)} all-to-all(bf16[8,128,128]{2,1,0:T(8,128)(2,1)S(1)} %get-tuple-element.34), channel_id=1, replica_groups=mesh['y_high'=2,'y_low'=2,'z_high'=4,'z_low'=2,'x'=4,'core'=2] {'y_low',..., dimensions={0} | all-to-all | bytes 524288 | tf_op jit(solution)/shard_map/all_to_all | solution.py:580
  39.3 1.8 %shard_map.89 = (f32[512,128]{1,0:T(8,128)S(1)}, bf16[512,256]{1,0:T(8,128)(2,1)S(1)}, bf16[128,256]{1,0:T(8,128)(2,1)S(1)}) custom-call(s32[3,16]{1,0:T(4,128)} %off_ref.13, bf16[8,128,128]{2,1,0:T(8,128)(2,1)S(1)} %all_to_all.15.all_ref), custom_call_target="tpu_custom_call" | custom-call | tf_op jit(solution)/shard_map/pallas_call | solution.py:48
  41.1 2.7 %collective-permute-start.1 = (bf16[128,256]{1,0:T(8,128)(2,1)S(1)}, bf16[128,256]{1,0:T(8,128)(2,1)S(1)}, u32[]{:S(2)}, u32[]{:S(2)}) collective-permute-start(bf16[128,256]{1,0:T(8,128)(2,1)S(1)} %get-tuple-element.43.here_ref), channel_id=1, source_target_pairs={{0,128},{128,0},{1,129},{129,1},{2,130},{130,2},{3,131},{131,3},{4... | collective-permute-start | bytes 196616 | tf_op jit(solution)/shard_map/ppermute | solution.py:587
  43.8 0.5 shard_map.90
  44.3 1.5 %collective-permute-done.1.there_ref = bf16[128,256]{1,0:T(8,128)(2,1)S(1)} collective-permute-done((bf16[128,256]{1,0:T(8,128)(2,1)S(1)}, bf16[128,256]{1,0:T(8,128)(2,1)S(1)}, u32[]{:S(2)}, u32[]{:S(2)}) %collective-permute-start.1) | collective-permute-done | bytes 65568 | tf_op jit(solution)/shard_map/ppermute | solution.py:587
  45.8 3.0 %shard_map.91 = f32[8,80,256]{2,1,0:T(8,128)} custom-call(s32[3,16]{1,0:T(4,128)} %off_ref.13, bf16[512,256]{1,0:T(8,128)(2,1)S(1)} %get-tuple-element.36.two_in_ref, bf16[256,512]{1,0:T(8,128)(2,1)S(1)} %get-tuple-element.37.two_t_ref, bf16[256,512]{1,0:T(8,128)(2,1)S(1)} %get-tuple-element.38.far3_t_ref, f32[512,512]{1,0:T(8,128)S(1)} %get-tuple-element.39.weights_ref, ...), custom_call_target="tpu_custom_call" | custom-call | tf_op jit(solution)/shard_map/pallas_call | solution.py:48
  48.8 6.7 %all-to-all-start.2 = ((f32[8,80,256]{2,1,0:T(8,128)}), f32[8,80,256]{2,1,0:T(8,128)S(1)}, u32[]{:S(2)}, u32[]{:S(2)}) async-start(f32[8,80,256]{2,1,0:T(8,128)} %shard_map.91), calls=%async_computation.2 | async-start | bytes 1310720 | tf_op jit(solution)/shard_map/all_to_all | solution.py:602
  55.5 5.6 %shard_map.92 = (bf16[8,96,512]{2,1,0:T(8,128)(2,1)}, f32[4096,128]{1,0:T(8,128)}) custom-call(s32[3,16]{1,0:T(4,128)} %off_ref.13, bf16[8,192,256]{2,1,0:T(8,128)(2,1)S(1)} %shard_map.84.keep_ref, bf16[8,192,256]{2,1,0:T(8,128)(2,1)S(1)} %collective-permute-done.came_ref, ...), custom_call_target="tpu_custom_call", output_to_operand_aliasing={{0}: (3, {}), {1}: (4, {})} | custom-call | tf_op jit(solution)/shard_map/pallas_call | solution.py:454
  61.1 2.1 %all-to-all-done.2.back_ref = f32[8,80,256]{2,1,0:T(8,128)S(1)} async-done(((f32[8,80,256]{2,1,0:T(8,128)}), f32[8,80,256]{2,1,0:T(8,128)S(1)}, u32[]{:S(2)}, u32[]{:S(2)}) %all-to-all-start.2) | async-done | bytes 655392 | tf_op jit(solution)/shard_map/all_to_all | solution.py:602
  63.2 4.4 %shard_map.93 = (bf16[8,192,256]{2,1,0:T(8,128)(2,1)S(1)}, bf16[8,192,256]{2,1,0:T(8,128)(2,1)S(1)}) custom-call(s32[3,16]{1,0:T(4,128)} %off_ref.13, bf16[8,192,256]{2,1,0:T(8,128)(2,1)S(1)} %shard_map.84.keep_ref, bf16[8,192,256]{2,1,0:T(8,128)(2,1)S(1)} %collective-permute-done.came_ref, bf16[8,80,256]{2,1,0:T(8,128)(2,1)} %get-tuple-element.29.taken_ref, ...), custom_call_target="tpu_custom_call" | custom-call | tf_op jit(solution)/shard_map/pallas_call | solution.py:48
  67.5 4.6 %collective-permute-start.2 = (bf16[8,192,256]{2,1,0:T(8,128)(2,1)S(1)}, bf16[8,192,256]{2,1,0:T(8,128)(2,1)S(1)}, u32[]{:S(2)}, u32[]{:S(2)}) collective-permute-start(bf16[8,192,256]{2,1,0:T(8,128)(2,1)S(1)} %get-tuple-element.48), channel_id=1, source_target_pairs={{0,1},{1,0},{2,3},{3,2},{4,5},{5,4},{6,7},{7,6},{8,9},{9,8},{10,11... | collective-permute-start | bytes 2359304 | tf_op jit(solution)/shard_map/ppermute | solution.py:557
  72.2 1.0 %shard_map.94 = (bf16[256,768]{1,0:T(8,128)(2,1)}, bf16[256,768]{1,0:T(8,128)(2,1)}, bf16[256,768]{1,0:T(8,128)(2,1)}, bf16[256,768]{1,0:T(8,128)(2,1)}) custom-call(bf16[8,192,256]{2,1,0:T(8,128)(2,1)S(1)} %get-tuple-element.49.in_ref), custom_call_target="tpu_custom_call" | custom-call | tf_op jit(solution)/shard_map/pallas_call | solution.py:105
  73.2 0.9 %collective-permute-done.2.in_ref = bf16[8,192,256]{2,1,0:T(8,128)(2,1)S(1)} collective-permute-done((bf16[8,192,256]{2,1,0:T(8,128)(2,1)S(1)}, bf16[8,192,256]{2,1,0:T(8,128)(2,1)S(1)}, u32[]{:S(2)}, u32[]{:S(2)}) %collective-permute-start.2) | collective-permute-done | bytes 786464 | tf_op jit(solution)/shard_map/ppermute | solution.py:557
  74.1 1.0 %shard_map.95 = (bf16[256,768]{1,0:T(8,128)(2,1)}, bf16[256,768]{1,0:T(8,128)(2,1)}, bf16[256,768]{1,0:T(8,128)(2,1)}, bf16[256,768]{1,0:T(8,128)(2,1)}) custom-call(bf16[8,192,256]{2,1,0:T(8,128)(2,1)S(1)} %collective-permute-done.2.in_ref, ...), custom_call_target="tpu_custom_call", output_to_operand_aliasing={{0}: (1, {}), {1}: (2, {}), {2}: (3, {}), {3}: (4, {})} | custom-call | tf_op jit(solution)/shard_map/pallas_call | solution.py:105
Async XLA Ops:
  2.0 5.2 %collective-permute-start = (bf16[8,192,256]{2,1,0:T(8,128)(2,1)S(1)}, bf16[8,192,256]{2,1,0:T(8,128)(2,1)S(1)}, u32[]{:S(2)}, u32[]{:S(2)}) collective-permute-start(bf16[8,192,256]{2,1,0:T(8,128)(2,1)S(1)} %shard_map.85), channel_id=1, source_target_pairs={{0,1},{1,0},{2,3},{3,2},{4,5},{5,4},{6,7},{7,6},{8,9},{9,8},{10,11... | collective-permute-start | bytes 2359304 | tf_op jit(solution)/shard_map/ppermute | solution.py:557
  10.7 10.2 %all-to-all-start = ((bf16[8,80,256]{2,1,0:T(8,128)(2,1)}), bf16[8,80,256]{2,1,0:T(8,128)(2,1)S(1)}, u32[]{:S(2)}, u32[]{:S(2)}) async-start(bf16[8,80,256]{2,1,0:T(8,128)(2,1)} %get-tuple-element.29.taken_ref), calls=%async_computation | async-start | bytes 655360 | tf_op jit(solution)/shard_map/all_to_all | solution.py:571
  41.1 4.7 %collective-permute-start.1 = (bf16[128,256]{1,0:T(8,128)(2,1)S(1)}, bf16[128,256]{1,0:T(8,128)(2,1)S(1)}, u32[]{:S(2)}, u32[]{:S(2)}) collective-permute-start(bf16[128,256]{1,0:T(8,128)(2,1)S(1)} %get-tuple-element.43.here_ref), channel_id=1, source_target_pairs={{0,128},{128,0},{1,129},{129,1},{2,130},{130,2},{3,131},{131,3},{4... | collective-permute-start | bytes 196616 | tf_op jit(solution)/shard_map/ppermute | solution.py:587
  48.8 14.4 %all-to-all-start.2 = ((f32[8,80,256]{2,1,0:T(8,128)}), f32[8,80,256]{2,1,0:T(8,128)S(1)}, u32[]{:S(2)}, u32[]{:S(2)}) async-start(f32[8,80,256]{2,1,0:T(8,128)} %shard_map.91), calls=%async_computation.2 | async-start | bytes 1310720 | tf_op jit(solution)/shard_map/all_to_all | solution.py:602
  67.5 6.6 %collective-permute-start.2 = (bf16[8,192,256]{2,1,0:T(8,128)(2,1)S(1)}, bf16[8,192,256]{2,1,0:T(8,128)(2,1)S(1)}, u32[]{:S(2)}, u32[]{:S(2)}) collective-permute-start(bf16[8,192,256]{2,1,0:T(8,128)(2,1)S(1)} %get-tuple-element.48), channel_id=1, source_target_pairs={{0,1},{1,0},{2,3},{3,2},{4,5},{5,4},{6,7},{7,6},{8,9},{9,8},{10,11... | collective-permute-start | bytes 2359304 | tf_op jit(solution)/shard_map/ppermute | solution.py:557
